TPU v7x, 32 devices: a whole 2x2x4 slice. The times are simulated.
32 devices in a mesh: dp: 8 (over z, x), mp: 4 (over y, core).
Axes of the slice: x: 2, y: 2, z: 4, core: 2. Of those that a mesh axis runs over, the one named last changes fastest.
Arguments:
- text_embed: bfloat16 [8192, 2048], P(('dp', 'mp')), may hold values from -6 to 6
- clip_feats: bfloat16 [16, 256, 1024], P('dp'), may hold values from -6 to 6
- type_table: bfloat16 [3, 2048], replicated, may hold values from -3 to 3
- gain_attn_in: float32 [2048], replicated, may hold values from 0.5 to 1.5
- qkv_weight: bfloat16 [2048, 3, 2048], P(None, None, 'mp'), may hold values from -0.125 to 0.125
- gain_attn_out: float32 [2048], P('mp'), may hold values from 0.5 to 1.5
- out_weight: bfloat16 [2048, 2048], P('mp'), may hold values from -0.125 to 0.125
- gain_ffn_in: float32 [2048], replicated, may hold values from 0.5 to 1.5
- up_weight: bfloat16 [2048, 8192], P(None, 'mp'), may hold values from -0.125 to 0.125
- gain_ffn_out: float32 [8192], P('mp'), may hold values from 0.5 to 1.5
- down_weight: bfloat16 [8192, 2048], P('mp'), may hold values from -0.0625 to 0.0625
- res_query: bfloat16 [64, 2048], P(None, 'mp'), may hold values from -6 to 6
- res_key: bfloat16 [1024, 2048], P(None, 'mp'), may hold values from -0.1875 to 0.1875
- res_value: bfloat16 [1024, 2048], P(None, 'mp'), may hold values from -0.1875 to 0.1875
- res_out: bfloat16 [2048, 2048], P('mp'), may hold values from -1.5 to 1.5
- cotangent: bfloat16 [8192, 2048], P(('dp', 'mp')), may hold values from -6 to 6
- owner_count: int32 [8], replicated, may hold values from 1 to 2, as said below
- image_seq: int32 [16], replicated, may hold values from 0 to 7, as said below
- slot_block: int32 [8, 4], replicated, may hold values from 0 to 15, as said below
- seq_kind: int32 [8], replicated, may hold values from 0 to 2
Outputs:
- layer_out: float32 [8192, 2048], P(('dp', 'mp'))
- text_grad: float32 [8192, 2048], P(('dp', 'mp'))
- clip_grad: float32 [16, 256, 1024], P('dp', 'mp')
- type_grad: float32 [3, 2048], replicated
- gain_attn_in_grad: float32 [2048], replicated
- qkv_grad: float32 [2048, 3, 2048], P('dp', None, 'mp')
- gain_attn_out_grad: float32 [2048], replicated
- out_grad: float32 [2048, 2048], P('mp', 'dp')
- gain_ffn_in_grad: float32 [2048], replicated
- up_grad: float32 [2048, 8192], P('dp', 'mp')
- gain_ffn_out_grad: float32 [8192], replicated
- down_grad: float32 [8192, 2048], P('mp', 'dp')
- query_grad: float32 [64, 2048], replicated
- key_grad: float32 [1024, 2048], P('dp', 'mp')
- value_grad: float32 [1024, 2048], P('dp', 'mp')
- res_out_grad: float32 [2048, 2048], P('mp', 'dp')
Inputs may be any that keep to these rules, and one draw needn't show every extreme that they name: Places 2 o to 2 o + owner_count[o] - 1 of owner o hold real images, the rest are padding; some owner is full. `image_seq`: the sequence into which a real image goes; a sequence receives at most 4 real images and some sequence exactly 4; sequences of kind 0 receive none and of kind 1 at most one; entries of padding places are ignored. `slot_block`: each row holds 4 distinct blocks of 64 positions in increasing order; entries past a sequence's image count are ignored.
All inputs are finite; a program needn't handle non-finite values.
Results may differ from a plain program's by a relative error of at most 0.022.
Values may be sent and summed in bfloat16 or wider, within the bound.
A program may use at most 256 MiB of HBM per device.

v0:
```python
import jax
import jax.numpy as jnp
from jax import lax
from jax.sharding import PartitionSpec as P

HEAD = 64


EPS = 1e-05
NEG = -1e30
XPOS_BASE = 512.0


def full_rows(values):
    return lax.all_gather(values, "mp", axis=0, tiled=True)


def row_sums(maker, count_rows):
    return lax.psum_scatter(
        maker(jnp.int32(0), count_rows * lax.axis_size("mp")).astype(jnp.bfloat16),
        "mp",
        scatter_dimension=0,
        tiled=True,
    ).astype(jnp.float32)


def width_stats(first, second):
    return lax.psum((first, second), "mp")


def weight_grads(left, right):
    return lax.psum_scatter(
        lax.dot_general(
            left, right, (((0,), (0,)), ((), ())), preferred_element_type=jnp.float32
        ).astype(jnp.bfloat16),
        "dp",
        scatter_dimension=0,
        tiled=True,
    ).astype(jnp.float32)


def local_norm(values, gain):
    width = values.shape[-1]
    mean = jnp.sum(values, axis=-1, keepdims=True) / width
    square = jnp.sum(values * values, axis=-1, keepdims=True) / width
    inv_std = lax.rsqrt(square - mean * mean + EPS)
    normed = (values - mean) * inv_std
    return (normed * gain, normed, inv_std)


def local_back(upstream, normed, inv_std, gain):
    width = upstream.shape[-1]
    scaled = upstream * gain
    first = jnp.sum(scaled, axis=-1, keepdims=True)
    second = jnp.sum(scaled * normed, axis=-1, keepdims=True)
    return inv_std * (scaled - first / width - normed * second / width)


def split_norm(values, gain, width):
    totals = width_stats(jnp.sum(values, axis=-1), jnp.sum(values * values, axis=-1))
    mean = (totals[0] / width)[:, None]
    inv_std = lax.rsqrt((totals[1] / width)[:, None] - mean * mean + EPS)
    normed = (values - mean) * inv_std
    return (normed * gain, normed, inv_std)


def split_back(upstream, normed, inv_std, gain, width):
    scaled = upstream * gain
    totals = width_stats(jnp.sum(scaled, axis=-1), jnp.sum(scaled * normed, axis=-1))
    return inv_std * (scaled - totals[0][:, None] / width - normed * totals[1][:, None] / width)


def rotate_tables(size, positions, center, sign):
    half = size // 2
    ladder = jnp.arange(half, dtype=jnp.float32)
    frequency = jnp.power(10000.0, -2.0 * ladder / size)
    angle = positions[:, None] * frequency[None, :]
    decay = (2.0 * ladder + 0.4 * size) / (1.4 * size)
    scale = jnp.power(decay[None, :], sign * (positions[:, None] - center) / XPOS_BASE)
    return ((jnp.cos(angle) * scale)[:, None, :], (jnp.sin(angle) * scale)[:, None, :])


def rotate_scale(values, sign, positions, center):
    half = values.shape[-1] // 2
    cosine, sine = rotate_tables(values.shape[-1], positions, center, sign)
    first = values[..., :half]
    second = values[..., half:]
    return jnp.concatenate(
        [first * cosine - second * sine, second * cosine + first * sine], axis=-1
    )


def rotate_back(upstream, sign, positions, center):
    half = upstream.shape[-1] // 2
    cosine, sine = rotate_tables(upstream.shape[-1], positions, center, sign)
    first = upstream[..., :half]
    second = upstream[..., half:]
    return jnp.concatenate(
        [first * cosine + second * sine, second * cosine - first * sine], axis=-1
    )


def masked_scores(piece, keys, start):
    length = keys.shape[0]
    block = piece.shape[0]
    scores = jnp.einsum("qhe,khe->hqk", piece, keys, preferred_element_type=jnp.float32) * 0.125
    allowed = (start + jnp.arange(block))[:, None] >= jnp.arange(length)[None, :]
    return jnp.where(allowed[None], scores, NEG)


def attention_forward(query, keys, values, block):
    length, heads, size = query.shape
    count = length // block

    def one_block(item):
        piece, start = item
        scores = masked_scores(piece, keys, start)
        normal = jax.nn.logsumexp(scores, axis=-1, keepdims=True)
        shares = jnp.exp(scores - normal).astype(jnp.bfloat16)
        return (
            jnp.einsum("hqk,khe->qhe", shares, values, preferred_element_type=jnp.float32),
            normal[..., 0],
        )

    outputs, normals = lax.map(
        one_block, (query.reshape(count, block, heads, size), jnp.arange(count) * block)
    )
    return (outputs.reshape(length, heads, size), normals)


def attention_backward(query, keys, values, upstream, normals, block):
    length, heads, size = query.shape
    count = length // block

    def one_block(carry, item):
        piece, grad_piece, normal, start = item
        scores = masked_scores(piece, keys, start)
        shares = jnp.exp(scores - normal[..., None])
        grad_shares = jnp.einsum(
            "qhe,khe->hqk", grad_piece, values, preferred_element_type=jnp.float32
        )
        inner = jnp.sum(shares * grad_shares, axis=-1, keepdims=True)
        grad_scores = (shares * (grad_shares - inner)).astype(jnp.bfloat16)
        grad_query = (
            jnp.einsum("hqk,khe->qhe", grad_scores, keys, preferred_element_type=jnp.float32)
            * 0.125
        )
        grad_keys = (
            carry[0]
            + jnp.einsum("hqk,qhe->khe", grad_scores, piece, preferred_element_type=jnp.float32)
            * 0.125
        )
        grad_values = carry[1] + jnp.einsum(
            "hqk,qhe->khe",
            shares.astype(jnp.bfloat16),
            grad_piece,
            preferred_element_type=jnp.float32,
        )
        return ((grad_keys, grad_values), grad_query)

    empty = jnp.zeros((length, heads, size), jnp.float32)
    carried, grad_query = lax.scan(
        one_block,
        (empty, empty),
        (
            query.reshape(count, block, heads, size),
            upstream.reshape(count, block, heads, size),
            normals,
            jnp.arange(count) * block,
        ),
    )
    return (grad_query.reshape(length, heads, size), carried[0], carried[1])


def gelu_exact(values):
    return jax.nn.gelu(values, approximate=False)


def spread(local, part_index, parts):
    whole = jnp.zeros(local.shape[:-1] + (local.shape[-1] * parts,), jnp.float32)
    return lax.dynamic_update_slice_in_dim(
        whole, local, part_index * local.shape[-1], local.ndim - 1
    )


def shards(
    text_embed,
    clip_feats,
    type_table,
    gain_attn_in,
    qkv_weight,
    gain_attn_out,
    out_weight,
    gain_ffn_in,
    up_weight,
    gain_ffn_out,
    down_weight,
    res_query,
    res_key,
    res_value,
    res_out,
    cotangent,
    owner_count,
    image_seq,
    slot_block,
    seq_kind,
):
    mp_count = lax.axis_size("mp")
    seq_index = lax.axis_index("dp")
    part_index = lax.axis_index("mp")
    local_rows, width = text_embed.shape
    seq_len = local_rows * mp_count
    latent = res_query.shape[0]
    image_total = image_seq.shape[0]
    slot_count = slot_block.shape[1]
    image_local, patches, clip_width = clip_feats.shape
    local_width = qkv_weight.shape[2]
    local_heads = local_width // HEAD
    ff_local = up_weight.shape[1]
    ff_width = ff_local * mp_count
    blocks_here = local_rows // latent
    image_ids = jnp.arange(image_total, dtype=jnp.int32)
    is_real = image_ids % image_local < jnp.take(owner_count, image_ids // image_local)
    earlier = (
        (image_seq[None, :] == image_seq[:, None])
        & is_real[None, :]
        & (image_ids[None, :] < image_ids[:, None])
    )
    ranks = jnp.minimum(jnp.sum(earlier.astype(jnp.int32), axis=1), slot_count - 1)
    blocks = slot_block[image_seq, ranks]
    mine = is_real & (image_seq == seq_index)
    local_block = blocks - part_index * blocks_here
    picker = (mine[None, :] & (local_block[None, :] == jnp.arange(blocks_here)[:, None])).astype(
        jnp.float32
    )
    block_mask = jnp.sum(picker, axis=1) > 0.5
    row_mask = jnp.broadcast_to(block_mask[:, None], (blocks_here, latent)).reshape(local_rows)
    kind_onehot = (jnp.arange(3) == seq_kind[seq_index]).astype(jnp.float32)
    kind_row = jnp.dot(
        kind_onehot[None, :].astype(jnp.bfloat16), type_table, preferred_element_type=jnp.float32
    )
    key_proj = jnp.einsum(
        "ipc,cd->ipd", clip_feats, res_key, preferred_element_type=jnp.float32
    ).astype(jnp.bfloat16)
    value_proj = jnp.einsum(
        "ipc,cd->ipd", clip_feats, res_value, preferred_element_type=jnp.float32
    ).astype(jnp.bfloat16)
    query_heads = res_query.reshape(latent, local_heads, HEAD)
    key_heads = key_proj.reshape(image_local, patches, local_heads, HEAD)
    value_heads = value_proj.reshape(image_local, patches, local_heads, HEAD)
    pool_scores = (
        jnp.einsum("lhe,iphe->ihlp", query_heads, key_heads, preferred_element_type=jnp.float32)
        * 0.125
    )
    pool_shares = jnp.exp(pool_scores - jax.nn.logsumexp(pool_scores, axis=-1, keepdims=True))
    pool_low = pool_shares.astype(jnp.bfloat16)
    pool_out = jnp.einsum(
        "ihlp,iphe->ilhe", pool_low, value_heads, preferred_element_type=jnp.float32
    )
    pool_out = pool_out.reshape(image_local * latent, local_width).astype(jnp.bfloat16)

    def pool_term(start, count):
        return jnp.dot(pool_out, res_out, preferred_element_type=jnp.float32)

    pooled_part = row_sums(pool_term, image_local * latent // mp_count).astype(jnp.bfloat16)
    pooled_all = lax.all_gather(pooled_part, ("dp", "mp"), axis=0, tiled=True).reshape(
        image_total, latent, width
    )
    image_part = jnp.einsum(
        "bi,ild->bld", picker.astype(jnp.bfloat16), pooled_all, preferred_element_type=jnp.float32
    )
    mixed = (
        jnp.where(
            row_mask[:, None], image_part.reshape(local_rows, width), text_embed.astype(jnp.float32)
        )
        + kind_row
    )
    norm_in, normed_in, inv_in = local_norm(mixed, gain_attn_in)
    in_full = full_rows(norm_in.astype(jnp.bfloat16))
    qkv = jnp.einsum("sd,dce->sce", in_full, qkv_weight, preferred_element_type=jnp.float32)
    positions = jnp.arange(seq_len, dtype=jnp.float32)
    center = seq_len // 2
    query = rotate_scale(
        qkv[:, 0].reshape(seq_len, local_heads, HEAD), 1.0, positions, center
    ).astype(jnp.bfloat16)
    keys = rotate_scale(
        qkv[:, 1].reshape(seq_len, local_heads, HEAD), -1.0, positions, center
    ).astype(jnp.bfloat16)
    values = qkv[:, 2].reshape(seq_len, local_heads, HEAD).astype(jnp.bfloat16)
    block = min(512, seq_len)
    attended, normals = attention_forward(query, keys, values, block)
    mid_norm, mid_normed, mid_inv = split_norm(
        attended.reshape(seq_len, local_width), gain_attn_out, width
    )
    mid_low = mid_norm.astype(jnp.bfloat16)

    def out_term(start, count):
        return jnp.dot(mid_low, out_weight, preferred_element_type=jnp.float32)

    after_attn = mixed + row_sums(out_term, local_rows)
    norm_ffn, normed_ffn, inv_ffn = local_norm(after_attn, gain_ffn_in)
    ffn_full = full_rows(norm_ffn.astype(jnp.bfloat16))
    pre_act = jnp.dot(ffn_full, up_weight, preferred_element_type=jnp.float32)
    activ, gelu_pull = jax.vjp(gelu_exact, pre_act)
    up_norm, up_normed, up_inv = split_norm(activ, gain_ffn_out, ff_width)
    up_low = up_norm.astype(jnp.bfloat16)

    def down_term(start, count):
        return jnp.dot(up_low, down_weight, preferred_element_type=jnp.float32)

    layer_out = after_attn + row_sums(down_term, local_rows)
    grad_out = cotangent.astype(jnp.float32)
    grad_full = full_rows(cotangent)
    down_grad = weight_grads(grad_full, up_low).T
    d_up = lax.dot_general(
        grad_full, down_weight, (((1,), (1,)), ((), ())), preferred_element_type=jnp.float32
    )
    gain_ffn_out_local = jnp.sum(d_up * up_normed, axis=0)
    d_activ = split_back(d_up, up_normed, up_inv, gain_ffn_out, ff_width)
    d_pre = gelu_pull(d_activ)[0].astype(jnp.bfloat16)
    up_grad = weight_grads(ffn_full, d_pre)

    def up_back(start, count):
        return lax.dot_general(
            d_pre, up_weight, (((1,), (1,)), ((), ())), preferred_element_type=jnp.float32
        )

    d_norm_ffn = row_sums(up_back, local_rows)
    gain_ffn_in_local = jnp.sum(d_norm_ffn * normed_ffn, axis=0)
    d_after = grad_out + local_back(d_norm_ffn, normed_ffn, inv_ffn, gain_ffn_in)
    after_full = full_rows(d_after.astype(jnp.bfloat16))
    out_grad = weight_grads(after_full, mid_low).T
    d_mid = lax.dot_general(
        after_full, out_weight, (((1,), (1,)), ((), ())), preferred_element_type=jnp.float32
    )
    gain_attn_out_local = jnp.sum(d_mid * mid_normed, axis=0)
    d_attended = split_back(d_mid, mid_normed, mid_inv, gain_attn_out, width)
    d_attended = d_attended.reshape(seq_len, local_heads, HEAD).astype(jnp.bfloat16)
    d_query, d_keys, d_values = attention_backward(query, keys, values, d_attended, normals, block)
    d_query = rotate_back(d_query, 1.0, positions, center)
    d_keys = rotate_back(d_keys, -1.0, positions, center)
    d_qkv = jnp.stack(
        [
            d_query.reshape(seq_len, local_width),
            d_keys.reshape(seq_len, local_width),
            d_values.reshape(seq_len, local_width),
        ],
        axis=1,
    ).astype(jnp.bfloat16)
    qkv_grad = weight_grads(in_full, d_qkv.reshape(seq_len, 3 * local_width)).reshape(
        -1, 3, local_width
    )

    def qkv_back(start, count):
        return jnp.einsum("sce,dce->sd", d_qkv, qkv_weight, preferred_element_type=jnp.float32)

    d_norm_in = row_sums(qkv_back, local_rows)
    gain_attn_in_local = jnp.sum(d_norm_in * normed_in, axis=0)
    d_mixed = d_after + local_back(d_norm_in, normed_in, inv_in, gain_attn_in)
    text_grad = jnp.where(row_mask[:, None], 0.0, d_mixed)
    type_local = kind_onehot[:, None] * jnp.sum(d_mixed, axis=0)[None, :]
    mixed_blocks = d_mixed.reshape(blocks_here, latent, width)
    image_grad = jnp.einsum(
        "bi,bld->ild", picker, mixed_blocks, precision=lax.Precision.HIGHEST
    ).reshape(image_total * latent, width)
    owned = lax.psum_scatter(image_grad, ("dp", "mp"), scatter_dimension=0, tiled=True).astype(
        jnp.bfloat16
    )
    pool_grad = full_rows(owned)
    res_out_grad = weight_grads(pool_grad, pool_out).T
    d_heads = lax.dot_general(
        pool_grad, res_out, (((1,), (1,)), ((), ())), preferred_element_type=jnp.float32
    )
    d_heads = d_heads.astype(jnp.bfloat16).reshape(image_local, latent, local_heads, HEAD)
    d_pool_shares = jnp.einsum(
        "ilhe,iphe->ihlp", d_heads, value_heads, preferred_element_type=jnp.float32
    )
    pool_inner = jnp.sum(pool_shares * d_pool_shares, axis=-1, keepdims=True)
    d_pool_scores = (pool_shares * (d_pool_shares - pool_inner)).astype(jnp.bfloat16)
    query_local = (
        jnp.einsum("ihlp,iphe->lhe", d_pool_scores, key_heads, preferred_element_type=jnp.float32)
        * 0.125
    )
    query_local = query_local.reshape(latent, local_width)
    d_key_proj = (
        jnp.einsum("ihlp,lhe->iphe", d_pool_scores, query_heads, preferred_element_type=jnp.float32)
        * 0.125
    ).astype(jnp.bfloat16)
    d_value_proj = jnp.einsum(
        "ihlp,ilhe->iphe", pool_low, d_heads, preferred_element_type=jnp.float32
    ).astype(jnp.bfloat16)
    d_key_proj = d_key_proj.reshape(image_local, patches, local_width)
    d_value_proj = d_value_proj.reshape(image_local, patches, local_width)
    kv_right = jnp.concatenate(
        [
            d_key_proj.reshape(image_local * patches, local_width),
            d_value_proj.reshape(image_local * patches, local_width),
        ],
        axis=1,
    )
    kv_grad = weight_grads(clip_feats.reshape(image_local * patches, clip_width), kv_right)
    key_grad = kv_grad[:, :local_width]
    value_grad = kv_grad[:, local_width:]

    def clip_back(start, count):
        return jnp.einsum(
            "ipd,cd->pic", d_key_proj, res_key, preferred_element_type=jnp.float32
        ) + jnp.einsum("ipd,cd->pic", d_value_proj, res_value, preferred_element_type=jnp.float32)

    clip_grad = jnp.transpose(row_sums(clip_back, patches // mp_count), (1, 0, 2))
    small = lax.psum(
        (
            gain_attn_in_local,
            gain_ffn_in_local,
            type_local,
            spread(gain_attn_out_local, part_index, mp_count),
            spread(gain_ffn_out_local, part_index, mp_count),
            spread(query_local, part_index, mp_count),
        ),
        ("dp", "mp"),
    )
    return (
        layer_out,
        text_grad,
        clip_grad,
        small[2],
        small[0],
        qkv_grad,
        small[3],
        out_grad,
        small[1],
        up_grad,
        small[4],
        down_grad,
        small[5],
        key_grad,
        value_grad,
        res_out_grad,
    )


def solution(mesh):
    return jax.shard_map(
        shards,
        mesh=mesh,
        in_specs=(
            P(("dp", "mp"), None),
            P("dp", None, None),
            P(),
            P(),
            P(None, None, "mp"),
            P("mp"),
            P("mp", None),
            P(),
            P(None, "mp"),
            P("mp"),
            P("mp", None),
            P(None, "mp"),
            P(None, "mp"),
            P(None, "mp"),
            P("mp", None),
            P(("dp", "mp"), None),
            P(),
            P(),
            P(),
            P(),
        ),
        out_specs=(
            P(("dp", "mp"), None),
            P(("dp", "mp"), None),
            P("dp", "mp", None),
            P(),
            P(),
            P("dp", None, "mp"),
            P(),
            P("mp", "dp"),
            P(),
            P("dp", "mp"),
            P(),
            P("mp", "dp"),
            P(),
            P("dp", "mp"),
            P("dp", "mp"),
            P("mp", "dp"),
        ),
        check_vma=False,
    )
```

profile of v0, /device:TPU:0, one launch (start us, length us, event | category | flops | bytes accessed | tf_op | source)
XLA Modules:
  0.0 1860.4 jit_solution(4554795062238732925)
XLA Ops:
  22.6 24.4 %reduce-scatter.16.cloned.1.call-done = bf16[32,2048]{1,0:T(8,128)(2,1)} async-done(((bf16[128,2048]{1,0:T(8,128)(2,1)}), bf16[32,2048]{1,0:T(8,128)(2,1)}) %reduce-scatter.16.cloned.1.call-update) | async-done | bytes 131088 | tf_op jit(solution)/shard_map/reduce_scatter | solution.py:19
  50.5 61.9 %all-gather.6.cloned.1.call-done = bf16[1024,2048]{1,0:T(8,128)(2,1)} async-done(((bf16[32,2048]{1,0:T(8,128)(2,1)}), bf16[1024,2048]{1,0:T(8,128)(2,1)}) %all-gather.6.cloned.1.call-update) | async-done | bytes 4194320 | tf_op jit(solution)/shard_map/all_gather | solution.py:266
  125.1 32.0 %all-gather.8.cloned.1.call-done = bf16[1024,2048]{1,0:T(8,128)(2,1)} async-done(((bf16[256,2048]{1,0:T(8,128)(2,1)}), bf16[1024,2048]{1,0:T(8,128)(2,1)}) %all-gather.8.cloned.1.call-update) | async-done | bytes 4194320 | tf_op jit(solution)/shard_map/all_gather | solution.py:15
  178.0 31.3 %while.27 = (s32[]{:T(128)}, f32[2,512,8,64]{1,3,2,0:T(8,128)}, f32[2,8,512]{2,1,0:T(8,128)S(1)}, s32[2]{0:T(128)S(1)}, bf16[2,512,8,64]{1,3,2,0:T(8,128)(2,1)},...) while((s32[]{:T(128)}, f32[2,512,8,64]{1,3,2,0:T(8,128)}, ...), condition=%wide.region_10.11_spmd, body=%wide.region_7.10_spmd.sunk | while | flops 1120436736 | bytes 77271240 | solution.py:125
  229.1 45.5 %reduce-scatter.18.cloned.1.call-done = bf16[256,2048]{1,0:T(8,128)(2,1)} async-done(((bf16[1024,2048]{1,0:T(8,128)(2,1)}), bf16[256,2048]{1,0:T(8,128)(2,1)}) %reduce-scatter.18.cloned.1.call-update) | async-done | bytes 1048592 | tf_op jit(solution)/shard_map/reduce_scatter | solution.py:19
  280.2 34.0 %all-gather.10.cloned.1.call-done = bf16[1024,2048]{1,0:T(8,128)(2,1)} async-done(((bf16[256,2048]{1,0:T(8,128)(2,1)}), bf16[1024,2048]{1,0:T(8,128)(2,1)}) %all-gather.10.cloned.1.call-update) | async-done | bytes 4194320 | tf_op jit(solution)/shard_map/all_gather | solution.py:15
  314.2 32.3 %fusion.106 = (f32[1024]{0:T(1024)S(1)}, f32[1024]{0:T(1024)S(1)}, f32[1024,2048]{1,0:T(8,128)}, f32[1024,2048]{1,0:T(8,128)}, f32[1024,2048]{1,0:T(8,128)}) fusion(bf16[1024,2048]{1,0:T(8,128)(2,1)} %all-gather.10.cloned.1.call-done, bf16[2048,2048]{1,0:T(8,128)(2,1)} %param.32), kind=kOutput, calls=%fused_computation.249 | convolution fusion | flops 8730441728 | bytes 37756928 | tf_op jit(solution)/shard_map/dot_general | solution.py:303
  419.3 30.5 %reduce-scatter.22.cloned.1.call-done = bf16[256,2048]{1,0:T(8,128)(2,1)} async-done(((bf16[1024,2048]{1,0:T(8,128)(2,1)}), bf16[256,2048]{1,0:T(8,128)(2,1)}) %reduce-scatter.22.cloned.1.call-update) | async-done | bytes 1048592 | tf_op jit(solution)/shard_map/reduce_scatter | solution.py:19
  453.3 43.8 %reduce-scatter.20.cloned.1.call-done = bf16[256,2048]{1,0:T(8,128)(2,1)} async-done(((bf16[1024,2048]{1,0:T(8,128)(2,1)}), bf16[256,2048]{1,0:T(8,128)(2,1)}) %reduce-scatter.20.cloned.1.call-update) | async-done | bytes 1048592 | tf_op jit(solution)/shard_map/reduce_scatter | solution.py:19
  502.9 34.6 %all-gather.14.cloned.1.call-done = bf16[1024,2048]{1,0:T(8,128)(2,1)} async-done(((bf16[256,2048]{1,0:T(8,128)(2,1)}), bf16[1024,2048]{1,0:T(8,128)(2,1)}) %all-gather.14.cloned.1.call-update) | async-done | bytes 4194320 | tf_op jit(solution)/shard_map/all_gather | solution.py:15
  555.8 127.4 %while.28 = (s32[]{:T(128)}, f32[1024,8,64]{0,2,1:T(8,128)}, f32[1024,8,64]{0,2,1:T(8,128)}, f32[2,512,8,64]{1,0,3,2:T(2,128)}, bf16[2,512,8,64]{1,3,2,0:T(8,128...) while((s32[]{:T(128)}, f32[1024,8,64]{0,2,1:T(8,128)}, ...), condition=%wide.region_36.37_spmd.clone, body=%wide.region_34.36_spmd.clone.sunk | while | flops 2725507584 | bytes 204558704 | solution.py:162
  599.8 19.5 %dynamic_update_slice.32 = f32[2,512,8,64]{1,0,3,2:T(2,128)} dynamic-update-slice(f32[2,512,8,64]{1,0,3,2:T(2,128)} %get-tuple-element.539, f32[1,512,8,64]{1,0,3,2:T(1,128)} %copy.251, s32[]{:T(128)S(6)} %copy.268, s32[]{:T(128)} %constant.85.clone.1..sunk, s32[]{:T(128)} %constant.85.clone.1..sunk, s32[]{:T(128)} %constant.85.clone.1..sunk) | dynamic-update-slice | bytes 2097156 | tf_op jit(solution)/shard_map/while/body/jit(dynamic_update_index_in_dim)/dynamic_update_slice | solution.py:125
  663.7 19.5 %dynamic_update_slice.32 = f32[2,512,8,64]{1,0,3,2:T(2,128)} dynamic-update-slice(f32[2,512,8,64]{1,0,3,2:T(2,128)} %get-tuple-element.539, f32[1,512,8,64]{1,0,3,2:T(1,128)} %copy.251, s32[]{:T(128)S(6)} %copy.268, s32[]{:T(128)} %constant.85.clone.1..sunk, s32[]{:T(128)} %constant.85.clone.1..sunk, s32[]{:T(128)} %constant.85.clone.1..sunk) | dynamic-update-slice | bytes 2097156 | tf_op jit(solution)/shard_map/while/body/jit(dynamic_update_index_in_dim)/dynamic_update_slice | solution.py:125
  707.6 45.7 %reduce-scatter.24.cloned.1.call-done = bf16[256,2048]{1,0:T(8,128)(2,1)} async-done(((bf16[1024,2048]{1,0:T(8,128)(2,1)}), bf16[256,2048]{1,0:T(8,128)(2,1)}) %reduce-scatter.24.cloned.1.call-update) | async-done | bytes 1048592 | tf_op jit(solution)/shard_map/reduce_scatter | solution.py:19
  826.9 93.6 %reduce-scatter.26.cloned.1.call-done = f32[32,2048]{1,0:T(8,128)} async-done(((f32[1024,2048]{1,0:T(8,128)}), f32[32,2048]{1,0:T(8,128)}) %reduce-scatter.26.cloned.1.call-update) | async-done | bytes 262160 | tf_op jit(solution)/shard_map/reduce_scatter | solution.py:366
  947.2 122.2 %reduce-scatter.34.cloned.1.call-done = bf16[256,2048]{1,0:T(8,128)(2,1)} async-done(((bf16[2048,2048]{1,0:T(8,128)(2,1)}), bf16[256,2048]{1,0:T(8,128)(2,1)}) %reduce-scatter.34.cloned.1.call-update) | async-done | bytes 1048592 | tf_op jit(solution)/shard_map/reduce_scatter | solution.py:32
  1072.1 149.3 %reduce-scatter.36.cloned.1.call-done = bf16[256,2048]{0,1:T(8,128)(2,1)} async-done(((bf16[2048,2048]{0,1:T(8,128)(2,1)}), bf16[256,2048]{0,1:T(8,128)(2,1)}) %reduce-scatter.36.cloned.1.call-update) | async-done | bytes 1048592 | tf_op jit(solution)/shard_map/reduce_scatter | solution.py:32
  1224.1 68.0 %reduce-scatter.32.cloned.1.call-done = bf16[256,512]{1,0:T(8,128)(2,1)} async-done(((bf16[2048,512]{1,0:T(8,128)(2,1)}), bf16[256,512]{1,0:T(8,128)(2,1)}) %reduce-scatter.32.cloned.1.call-update) | async-done | bytes 262160 | tf_op jit(solution)/shard_map/reduce_scatter | solution.py:32
  1296.5 116.6 %reduce-scatter.30.cloned.1.call-done = bf16[256,1536]{1,0:T(8,128)(2,1)} async-done(((bf16[2048,1536]{1,0:T(8,128)(2,1)}), bf16[256,1536]{1,0:T(8,128)(2,1)}) %reduce-scatter.30.cloned.1.call-update) | async-done | bytes 786448 | tf_op jit(solution)/shard_map/reduce_scatter | solution.py:32
  1419.0 20.6 %reduce-scatter.28.cloned.1.call-done = bf16[64,2,1024]{2,0,1:T(8,128)(2,1)} async-done(((bf16[256,2,1024]{2,0,1:T(8,128)(2,1)}), bf16[64,2,1024]{2,0,1:T(8,128)(2,1)}) %reduce-scatter.28.cloned.1.call-update) | async-done | bytes 262160 | tf_op jit(solution)/shard_map/reduce_scatter | solution.py:19
  1441.4 69.3 %reduce-scatter.40.cloned.1.call-done = bf16[128,1024]{1,0:T(8,128)(2,1)} async-done(((bf16[1024,1024]{1,0:T(8,128)(2,1)}), bf16[128,1024]{1,0:T(8,128)(2,1)}) %reduce-scatter.40.cloned.1.call-update) | async-done | bytes 262160
  1513.6 67.4 %reduce-scatter.38.cloned.1.call-done = bf16[256,512]{1,0:T(8,128)(2,1)} async-done(((bf16[2048,512]{1,0:T(8,128)(2,1)}), bf16[256,512]{1,0:T(8,128)(2,1)}) %reduce-scatter.38.cloned.1.call-update) | async-done | bytes 262160 | tf_op jit(solution)/shard_map/reduce_scatter | solution.py:32
  1583.0 126.8 %all-reduce.10.cloned.1.call-done = (f32[3,2048]{1,0:T(4,128)}, f32[2048]{0:T(1024)}, f32[2048]{0:T(1024)}, f32[2048]{0:T(1024)}, f32[8192]{0:T(1024)}) async-done(((f32[3,2048]{1,0:T(4,128)}, f32[2048]{0:T(1024)}, f32[2048]{0:T(1024)}, f32[2048]{0:T(1024)}, f32[8192]{0:T(1024)}), (f32[3,2048]{1,0:T(4,128)}, f32[2048]{0:T(1024)}, f32[2048]{0:T(1024)}, f32[2048]{0:T(1024)}, ...) | async-done | bytes 81936 | tf_op jit(solution)/shard_map/psum | solution.py:411
  1709.8 134.9 %all-reduce.8.cloned.1.call-done = f32[64,2048]{1,0:T(8,128)} async-done(((f32[64,2048]{1,0:T(8,128)}), f32[64,2048]{1,0:T(8,128)}) %all-reduce.8.cloned.1.call-update) | async-done | bytes 524304 | tf_op jit(solution)/shard_map/psum | solution.py:411
  (428 shorter events, 451.1 us)
Async XLA Ops:
  7.2 39.8 %reduce-scatter.16.cloned.1.call-start = ((), (), s32[]{:S(2)}) async-start(), calls=%async_computation.13 | async-start | bytes 655360 | tf_op jit(solution)/shard_map/reduce_scatter | solution.py:19
  22.5 89.8 %all-gather.6.cloned.1.call-start = ((), (), s32[]{:S(2)}) async-start(), calls=%async_computation.14 | async-start | bytes 4325376 | tf_op jit(solution)/shard_map/all_gather | solution.py:266
  47.0 110.0 %all-gather.8.cloned.1.call-start = ((), (), s32[]{:S(2)}) async-start(), calls=%async_computation.15 | async-start | bytes 5242880 | tf_op jit(solution)/shard_map/all_gather | solution.py:15
  123.9 150.8 %reduce-scatter.18.cloned.1.call-start = ((), (), s32[]{:S(2)}) async-start(), calls=%async_computation.16 | async-start | bytes 5242880 | tf_op jit(solution)/shard_map/reduce_scatter | solution.py:19
  228.9 85.3 %all-gather.10.cloned.1.call-start = ((), (), s32[]{:S(2)}) async-start(), calls=%async_computation.17 | async-start | bytes 5242880 | tf_op jit(solution)/shard_map/all_gather | solution.py:15
  279.6 73.1 %all-gather.12.cloned.1.call-start = ((), (), s32[]{:S(2)}) async-start(), calls=%async_computation.19 | async-start | bytes 5242880 | tf_op jit(solution)/shard_map/all_gather | solution.py:15
  280.2 169.7 %reduce-scatter.22.cloned.1.call-start = ((), (), s32[]{:S(2)}) async-start(), calls=%async_computation.20 | async-start | bytes 5242880 | tf_op jit(solution)/shard_map/reduce_scatter | solution.py:19
  403.9 93.2 %reduce-scatter.20.cloned.1.call-start = ((), (), s32[]{:S(2)}) async-start(), calls=%async_computation.18 | async-start | bytes 5242880 | tf_op jit(solution)/shard_map/reduce_scatter | solution.py:19
  419.3 118.2 %all-gather.14.cloned.1.call-start = ((), (), s32[]{:S(2)}) async-start(), calls=%async_computation.21 | async-start | bytes 5242880 | tf_op jit(solution)/shard_map/all_gather | solution.py:15
  502.8 250.5 %reduce-scatter.24.cloned.1.call-start = ((), (), s32[]{:S(2)}) async-start(), calls=%async_computation.22 | async-start | bytes 5242880 | tf_op jit(solution)/shard_map/reduce_scatter | solution.py:19
  707.6 212.9 %reduce-scatter.26.cloned.1.call-start = ((), (), s32[]{:S(2)}) async-start(), calls=%async_computation.23 | async-start | bytes 8650752 | tf_op jit(solution)/shard_map/reduce_scatter | solution.py:366
  771.4 298.0 %reduce-scatter.34.cloned.1.call-start = ((), (), s32[]{:S(2)}) async-start(), calls=%async_computation.27 | async-start | bytes 9437184 | tf_op jit(solution)/shard_map/reduce_scatter | solution.py:32
  785.7 435.8 %reduce-scatter.36.cloned.1.call-start = ((), (), s32[]{:S(2)}) async-start(), calls=%async_computation.28 | async-start | bytes 9437184 | tf_op jit(solution)/shard_map/reduce_scatter | solution.py:32
  801.8 490.3 %reduce-scatter.32.cloned.1.call-start = ((), (), s32[]{:S(2)}) async-start(), calls=%async_computation.26 | async-start | bytes 2359296 | tf_op jit(solution)/shard_map/reduce_scatter | solution.py:32
  809.6 603.4 %reduce-scatter.30.cloned.1.call-start = ((), (), s32[]{:S(2)}) async-start(), calls=%async_computation.25 | async-start | bytes 7077888 | tf_op jit(solution)/shard_map/reduce_scatter | solution.py:32
  826.9 612.7 %reduce-scatter.28.cloned.1.call-start = ((), (), s32[]{:S(2)}) async-start(), calls=%async_computation.24 | async-start | bytes 1310720 | tf_op jit(solution)/shard_map/reduce_scatter | solution.py:19
  935.1 575.6 %reduce-scatter.40.cloned.1.call-start = ((), (), s32[]{:S(2)}) async-start(), calls=%async_computation.31 | async-start | bytes 2359296
  943.1 637.9 %reduce-scatter.38.cloned.1.call-start = ((), (), s32[]{:S(2)}) async-start(), calls=%async_computation.30 | async-start | bytes 2359296 | tf_op jit(solution)/shard_map/reduce_scatter | solution.py:32
  945.3 349.5 %copy-start.19 = (f32[256,2048]{1,0:T(8,128)S(1)}, f32[256,2048]{1,0:T(8,128)}, u32[]{:S(2)}) copy-start(f32[256,2048]{1,0:T(8,128)} %copy-done.18) | copy-start | bytes 6291460
  945.3 349.5 %copy-start.80 = (pred[256]{0:T(512)(128)(4,1)S(1)}, pred[256]{0:T(512)(128)(4,1)}, u32[]{:S(2)}) copy-start(pred[256]{0:T(512)(128)(4,1)} %copy-done.79) | copy-start | bytes 772
  945.3 764.4 %all-reduce.10.cloned.1.call-start = ((), (), s32[]{:S(2)}) async-start(), calls=%async_computation.32 | async-start | bytes 180224 | tf_op jit(solution)/shard_map/psum | solution.py:411
  946.9 349.5 %copy-start.54 = (f32[8192]{0:T(1024)}, f32[8192]{0:T(1024)S(1)}, u32[]{:S(2)}) copy-start(f32[8192]{0:T(1024)S(1)} %dynamic_update_slice.21) | copy-start | bytes 98308
  1296.4 548.2 %all-reduce.8.cloned.1.call-start = ((), (), s32[]{:S(2)}) async-start(), calls=%async_computation.29 | async-start | bytes 1048576 | tf_op jit(solution)/shard_map/psum | solution.py:411
  1416.1 437.1 %copy-start.1 = (bf16[512,2048]{1,0:T(8,128)(2,1)S(1)}, bf16[512,2048]{1,0:T(8,128)(2,1)}, u32[]{:S(2)}) copy-start(bf16[512,2048]{1,0:T(8,128)(2,1)} %param.30) | copy-start | bytes 6291460
  (95 other events, 3132.2 us)
Sparse Core Ops, SparseCore 0:
  22.6 24.3 reduce-scatter.15
  50.3 62.0 all-gather.5
  124.0 33.0 all-gather.7
  229.0 45.5 reduce-scatter.17
  279.7 34.4 all-gather.9
  315.7 34.4 all-gather.11
  404.0 45.8 reduce-scatter.21
  452.5 44.5 reduce-scatter.19
  502.9 34.4 all-gather.13
  707.7 45.5 reduce-scatter.23
  771.5 148.9 reduce-scatter.25
  924.4 144.8 reduce-scatter.33
  1073.0 148.4 reduce-scatter.35
  1225.2 66.8 reduce-scatter.31
  1296.0 116.9 reduce-scatter.29
  1415.6 23.9 reduce-scatter.27
  1443.0 67.7 reduce-scatter.39
  1514.1 66.7 reduce-scatter.37
  1588.5 121.1 all-reduce.9
  1715.4 129.1 all-reduce.7
where the time goes:
time: 1870 us; the launch traced here: 1860 us
  waiting for transfers between devices  1320 us (71%)
  matrix products  266 us (14%)
  local copies, waits for them, and re-layouts  125 us (7%)
  other arithmetic  97.5 us (5%)
  blocking collectives  30.7 us (2%)
    reduce_scatter x5, waiting for transfers between devices, weight_grads(): lax.psum_scatter(lax.dot_general(left, right, (((0,), (0,)), ((), ())), p...  523 us
    psum x2, waiting for transfers between devices, shards(): lax.psum((gain_attn_in_local, gain_ffn_in_local, type_local, spread(gain_...  262 us
    reduce_scatter x6, waiting for transfers between devices, row_sums(): lax.psum_scatter(maker(jnp.int32(0), count_rows * lax.axis_size('mp')).as...  211 us
    all_gather x4, waiting for transfers between devices, full_rows(): return lax.all_gather(values, 'mp', axis=0, tiled=True)  101 us
    reduce_scatter x1, waiting for transfers between devices, shards(): lax.psum_scatter(image_grad, ('dp', 'mp'), scatter_dimension=0, tiled=True)  93.6 us
    unnamed x21, waiting for transfers between devices  70.2 us
    all_gather x1, waiting for transfers between devices, shards(): lax.all_gather(pooled_part, ('dp', 'mp'), axis=0, tiled=True)  61.9 us
    dot_general x6, matrix products, weight_grads(): lax.dot_general(left, right, (((0,), (0,)), ((), ())), preferred_element_...  52 us
  transfers between devices with their start and end apart: 20, of which 19 were waited for; matrix products, arithmetic and copies ran while one was open for 8% of the time, Pallas kernels for 0%

commit v1 on v0

v1 whole, which is shorter than its diff:
```python
import functools

import jax
import jax.numpy as jnp
from jax import lax
from jax.experimental import pallas as pl
from jax.experimental.pallas import tpu as pltpu
from jax.sharding import PartitionSpec as P

HEAD = 64
LANES = 128
EPS = 1e-05
NEG = -1e30
XPOS_BASE = 512.0
BF = jnp.bfloat16
F32 = jnp.float32
ROWS_BY_ROWS = (((1,), (1,)), ((), ()))
PLAIN = (((1,), (0,)), ((), ()))
OVER_ROWS = (((0,), (0,)), ((), ()))
KIND, PART, GROUP, REAL, POS, SOURCE, BLOCK, RANK = 0, 1, 2, 4, 8, 12, 16, 32
VMEM_BYTES = 56 * 1024 * 1024


def dot(left, right, form=PLAIN):
    return lax.dot_general(left, right, form, preferred_element_type=F32)


def dot_exact(left, right, form=ROWS_BY_ROWS):
    return lax.dot_general(
        left, right, form, precision=lax.Precision.HIGHEST, preferred_element_type=F32
    )


def swap(values, axis, bit):
    size = lax.axis_size(axis)
    return lax.ppermute(values, axis, [(i, i ^ bit) for i in range(size)])


def bits_of(size):
    return [1 << i for i in range(size.bit_length() - 1)]


def gather_rel(values):
    size = lax.axis_size("mp")
    pieces = {0: values}
    for bit in reversed(bits_of(size)):
        pieces[bit] = swap(values, "mp", bit)
    for j in range(size):
        if j not in pieces:
            low = j & -j
            pieces[j] = swap(pieces[j ^ low], "mp", low)
    return [pieces[j] for j in range(size)]


def add_low(first, second):
    return (first.astype(F32) + second.astype(F32)).astype(BF)


def scatter_rel(parts):
    near = add_low(parts[2], swap(parts[3], "mp", 1))
    last = swap(near, "mp", 2)
    return parts[0], swap(parts[1], "mp", 1), last


def sum_three(parts):
    own, core, far = scatter_rel(parts)
    return own.astype(F32) + core.astype(F32) + far.astype(F32)


def spread_stats(values):
    return [values] + [swap(values, "mp", b) for b in range(1, lax.axis_size("mp"))]


def pick(values, indices):
    return jnp.stack([lax.dynamic_index_in_dim(values, i, 0, keepdims=False) for i in indices])


def by_mp(values):
    me = lax.axis_index("mp")
    return pick(values, [me ^ j for j in range(lax.axis_size("mp"))])


def gather_dp(values):
    size = lax.axis_size("dp")
    depth = len(bits_of(size))
    for level, bit in enumerate(reversed(bits_of(size))):
        values = jnp.stack([values, swap(values, "dp", bit)], axis=level)
    return values.reshape((size,) + values.shape[depth:])


def halve(values, axis):
    return (
        lax.index_in_dim(values, 0, axis, keepdims=False),
        lax.index_in_dim(values, 1, axis, keepdims=False),
    )


def scatter_dp(values, bits, last):
    for bit in bits:
        values = values.reshape((-1, 2) + values.shape[1:])
        keep, send = halve(values, 1)
        got = swap(send, "dp", bit)
        total = keep.astype(F32) + got.astype(F32)
        values = total.astype(last if bit == bits[-1] else BF)
    return values[0]


def sum_small(over_all, over_dp):
    size = lax.axis_size("mp")
    count, width = over_all.shape
    cut = by_mp(jnp.swapaxes(over_all.reshape(count, size, width // size), 0, 1))
    parts = {j: cut[j] for j in range(size)}
    for bit in bits_of(size):
        for j in sorted(parts, reverse=True):
            if j & bit:
                parts[j ^ bit] = parts[j ^ bit] + swap(parts.pop(j), "mp", bit)
    flat = jnp.concatenate([parts[0].reshape(-1), over_dp])
    for bit in bits_of(lax.axis_size("dp")):
        flat = flat + swap(flat, "dp", bit)
    whole = by_mp(jnp.stack(gather_rel(flat)))
    edge = count * (width // size)
    first = jnp.swapaxes(whole[:, :edge].reshape(size, count, width // size), 0, 1)
    return first.reshape(count, width), whole[:, edge:]


def call(body, meta, grid, ins, outs, scratch=(), flops=0, aliases=None, size=None):
    arrays, specs = [], []
    moved = 0
    for item in ins:
        arrays.append(item[0])
        moved += item[0].size * item[0].dtype.itemsize
        if len(item) == 1:
            dims = item[0].ndim
            specs.append(
                pl.BlockSpec(
                    item[0].shape,
                    lambda *_, dims=dims: (0,) * dims,
                    pipeline_mode=pl.Buffered(1),
                )
            )
        elif item[1] is None:
            specs.append(pl.BlockSpec(memory_space=pl.ANY))
        else:
            specs.append(pl.BlockSpec(item[1], item[2]))
    shapes, out_specs = [], []
    for shape, dtype, block, index in outs:
        shapes.append(jax.ShapeDtypeStruct(shape, dtype))
        moved += functools.reduce(lambda a, b: a * b, shape, 1) * jnp.dtype(dtype).itemsize
        if block is None:
            dims = len(shape)
            out_specs.append(pl.BlockSpec(shape, lambda *_, dims=dims: (0,) * dims))
        else:
            out_specs.append(pl.BlockSpec(block, index))
    return pl.pallas_call(
        body,
        out_shape=shapes,
        grid_spec=pltpu.PrefetchScalarGridSpec(
            num_scalar_prefetch=1,
            grid=grid,
            in_specs=specs,
            out_specs=out_specs,
            scratch_shapes=list(scratch),
        ),
        input_output_aliases=aliases or {},
        compiler_params=pltpu.CompilerParams(vmem_limit_bytes=size or VMEM_BYTES),
        cost_estimate=pl.CostEstimate(
            flops=int(flops), bytes_accessed=int(moved), transcendentals=0
        ),
    )(meta, *arrays)


def norm_parts(values):
    width = values.shape[-1]
    mean = jnp.sum(values, axis=-1, keepdims=True) / width
    square = jnp.sum(values * values, axis=-1, keepdims=True) / width
    inv_std = lax.rsqrt(square - mean * mean + EPS)
    return (values - mean) * inv_std, inv_std


def norm_back(upstream, normed, inv_std, gain):
    width = upstream.shape[-1]
    scaled = upstream * gain
    first = jnp.sum(scaled, axis=-1, keepdims=True) / width
    second = jnp.sum(scaled * normed, axis=-1, keepdims=True) / width
    return inv_std * (scaled - first - normed * second)


def columns_of(rows):
    count, length = rows.shape
    full = jnp.concatenate([rows, jnp.zeros((LANES - count, length), F32)], axis=0)
    return full.T


def lane_sums(values):
    total = values[:, :LANES]
    for start in range(LANES, values.shape[1], LANES):
        total = total + values[:, start : start + LANES]
    return total


def rows_from(partials):
    return dot_exact(jnp.ones((8, LANES), F32), partials)


def two_rows(first, second):
    row = lax.broadcasted_iota(jnp.int32, first.shape, 0)
    return jnp.where(row == 0, first, jnp.where(row == 1, second, 0.0))


def meta_body(count_ref, seq_ref, slot_ref, kind_ref, me_ref, out_ref, *, image_local, slots, images):
    me_m, me_d = me_ref[0], me_ref[1]

    def clear(i, _):
        out_ref[i] = 0
        return 0

    lax.fori_loop(0, BLOCK, clear, 0)

    def absent(i, _):
        out_ref[BLOCK + i] = -1
        return 0

    lax.fori_loop(0, RANK - BLOCK + images, absent, 0)
    out_ref[KIND] = kind_ref[me_d]
    out_ref[PART] = me_m
    out_ref[GROUP] = me_d
    for s in range(slots):
        out_ref[POS + s] = slot_ref[me_d, s]

    def one(i, found):
        owner = i // image_local
        inside = i - owner * image_local
        here = jnp.logical_and(inside < count_ref[owner], seq_ref[i] == me_d)
        rank = jnp.minimum(found, slots - 1)

        @pl.when(here)
        def _():
            out_ref[REAL + rank] = 1
            out_ref[SOURCE + rank] = (owner ^ me_d) * image_local + inside
            out_ref[BLOCK + slot_ref[me_d, rank]] = rank
            out_ref[RANK + i] = rank

        return found + here.astype(jnp.int32)

    lax.fori_loop(0, images, one, jnp.int32(0))


def make_meta(owner_count, image_seq, slot_block, seq_kind, image_local):
    me = jnp.stack([lax.axis_index("mp"), lax.axis_index("dp")]).astype(jnp.int32)
    images = image_seq.shape[0]
    smem = pl.BlockSpec(memory_space=pltpu.SMEM)
    return pl.pallas_call(
        functools.partial(
            meta_body, image_local=image_local, slots=slot_block.shape[1], images=images
        ),
        out_shape=jax.ShapeDtypeStruct((RANK + images,), jnp.int32),
        in_specs=[smem] * 5,
        out_specs=smem,
    )(owner_count, image_seq, slot_block, seq_kind, me)


def kind_of(meta, table_ref):
    return table_ref[pl.ds(meta[KIND], 1), :]


def text_body(meta, text_ref, table_ref, gain_ref, out_ref):
    mixed = text_ref[...].astype(F32) + kind_of(meta, table_ref)
    out_ref[...] = (norm_parts(mixed)[0] * gain_ref[...]).astype(BF)


def rotated(values, cosine, sine):
    width = values.shape[1]
    lane = lax.broadcasted_iota(jnp.int32, values.shape, 1)
    other = jnp.where(
        lane % HEAD < HEAD // 2,
        pltpu.roll(values, width - HEAD // 2, 1),
        pltpu.roll(values, HEAD // 2, 1),
    )
    repeat = width // LANES
    cosine = jnp.concatenate([cosine] * repeat, axis=1)
    sine = jnp.concatenate([sine] * repeat, axis=1)
    return values * cosine + other * sine


def qkv_body(meta, near_ref, far_ref, weight_ref, table_ref, q_ref, k_ref, v_ref, in_ref, *more):
    rows = jnp.where(pl.program_id(0) == 0, near_ref[...], far_ref[...])
    qkv_rows(rows, weight_ref, table_ref, q_ref, k_ref, v_ref)
    in_ref[...] = rows


def qkv_rows(rows, weight_ref, table_ref, q_ref, k_ref, v_ref):
    width = q_ref.shape[1]
    query = dot(rows, weight_ref[:, :width])
    q_ref[...] = rotated(query, table_ref[0], table_ref[1]).astype(BF)
    keys = dot(rows, weight_ref[:, width : 2 * width])
    k_ref[...] = rotated(keys, table_ref[2], table_ref[3]).astype(BF)
    v_ref[...] = dot(rows, weight_ref[:, 2 * width :]).astype(BF)


def slot_body(
    meta, *refs, mp, slots, latent
):
    pieces = refs[:mp]
    table_ref, gain_ref, weight_ref, turn_ref, q_in, k_in, v_in, x_in = refs[mp : mp + 8]
    q_ref, k_ref, v_ref, x_ref, slots_ref, rows_ref, qkv_ref, norm_ref = refs[mp + 8 :]
    step = pl.program_id(0)
    part = latent // mp

    @pl.when(step == 0)
    def _():
        for j in range(mp):
            place = pl.multiple_of((meta[PART] ^ j) * part, part)
            for s in range(slots):
                rows_ref[s, pl.ds(place, part), :] = pieces[j][s].astype(F32)
        mixed = rows_ref[...].reshape(slots * latent, -1)
        slots_ref[...] = mixed.astype(BF).reshape(slots_ref.shape)
        mixed = mixed + kind_of(meta, table_ref)
        normed = (norm_parts(mixed)[0] * gain_ref[...]).astype(BF)
        norm_ref[...] = normed.reshape(norm_ref.shape)
        qkv_ref[...] = dot(normed, weight_ref[...]).reshape(qkv_ref.shape)

    real = meta[REAL + step] > 0
    rows = qkv_ref[step]
    width = q_ref.shape[1]
    query = rotated(rows[:, :width], turn_ref[0], turn_ref[1]).astype(BF)
    keys = rotated(rows[:, width : 2 * width], turn_ref[2], turn_ref[3]).astype(BF)
    q_ref[...] = jnp.where(real, query, q_in[...])
    k_ref[...] = jnp.where(real, keys, k_in[...])
    v_ref[...] = jnp.where(real, rows[:, 2 * width :].astype(BF), v_in[...])
    x_ref[...] = jnp.where(real, norm_ref[step], x_in[...])


def project(meta, pieces, weight, turn, before, which):
    rows, depth = pieces[0].shape
    width = weight.shape[1] // 3
    mp = lax.axis_size("mp")
    block = lambda i, m: (m[PART] ^ (which + i), 0)
    outs = [((rows * mp, width), BF, (rows, width), block)] * 3
    outs.append(((rows * mp, depth), BF, (rows, depth), block))
    ins = [(pieces[0],), (pieces[1],), (weight,)]
    ins.append((turn, (4, rows, LANES), lambda i, m: (0, m[PART] ^ (which + i), 0)))
    aliases = {}
    if before is not None:
        for n, array in enumerate(before):
            ins.append((array, None))
            aliases[5 + n] = n
    return call(
        qkv_body_more if before is not None else qkv_body,
        meta,
        (2,),
        ins,
        outs,
        flops=4 * rows * depth * 3 * width,
        aliases=aliases,
    )


def qkv_body_more(meta, near_ref, far_ref, weight_ref, table_ref, *refs):
    qkv_body(meta, near_ref, far_ref, weight_ref, table_ref, *refs[4:])


def turn_tables(length):
    positions = jnp.arange(length, dtype=F32)[:, None]
    lane = jnp.arange(LANES)
    ladder = (lane % (HEAD // 2)).astype(F32)
    angle = positions * jnp.power(10000.0, -2.0 * ladder / HEAD)[None, :]
    decay = (2.0 * ladder + 0.4 * HEAD) / (1.4 * HEAD)
    power = (positions - length // 2) / XPOS_BASE
    sign = jnp.where(lane % HEAD < HEAD // 2, -1.0, 1.0)[None, :]
    cosine, sine = jnp.cos(angle), jnp.sin(angle) * sign
    up = jnp.power(decay[None, :], power)
    down = jnp.power(decay[None, :], -power)
    return jnp.stack([cosine * up, sine * up, cosine * down, sine * down])


def pool_shares_of(query, keys, head):
    lane = lax.broadcasted_iota(jnp.int32, query.shape, 1)
    masked = jnp.where(lane // HEAD == head, query, jnp.zeros_like(query))
    scores = dot(masked, keys, ROWS_BY_ROWS) * 0.125
    top = jnp.max(scores, axis=-1, keepdims=True)
    weights = jnp.exp(scores - top)
    return weights / jnp.sum(weights, axis=-1, keepdims=True)


def pool_body(
    meta, clip_ref, key_w, value_w, query_ref, out_w, key_ref, value_ref, pool_ref, part_ref, scratch, *, images, mp
):
    clip = clip_ref[...]
    key_ref[...] = dot(clip, key_w[...]).astype(BF)
    value_ref[...] = dot(clip, value_w[...]).astype(BF)
    patches = clip.shape[0] // images
    latent = query_ref.shape[0]
    for i in range(images):
        for pair in range(query_ref.shape[1] // LANES):
            lanes = slice(pair * LANES, (pair + 1) * LANES)
            rows = slice(i * patches, (i + 1) * patches)
            query, keys, values = query_ref[:, lanes], key_ref[rows, lanes], value_ref[rows, lanes]
            lane = lax.broadcasted_iota(jnp.int32, query.shape, 1)
            heads = [
                dot(pool_shares_of(query, keys, h).astype(BF), values) for h in range(2)
            ]
            pool_ref[i * latent : (i + 1) * latent, lanes] = jnp.where(
                lane < HEAD, heads[0], heads[1]
            ).astype(BF)
    scratch[...] = dot(pool_ref[...], out_w[...])
    piece = latent // mp
    for j in range(mp):
        for i in range(images):
            start = pl.multiple_of(i * latent + (meta[PART] ^ j) * piece, piece)
            part_ref[j, i] = scratch[pl.ds(start, piece), :].astype(BF)


def copy_body(meta, in_ref, out_ref):
    out_ref[...] = in_ref[...]


def attend_body(meta, q_ref, k_ref, v_ref, out_ref, lse_ref, stat_ref, first, second, lse, *, block):
    length, width = q_ref.shape
    first[...] = jnp.zeros_like(first)
    second[...] = jnp.zeros_like(second)

    def pair(hp, _):
        lanes = pl.ds(pl.multiple_of(hp * LANES, LANES), LANES)
        keys, values = k_ref[:, lanes], v_ref[:, lanes]
        lane = lax.broadcasted_iota(jnp.int32, (block, LANES), 1)
        row = lax.broadcasted_iota(jnp.int32, (block, block), 0)
        col = lax.broadcasted_iota(jnp.int32, (block, block), 1)
        for b in range(length // block):
            rows = slice(b * block, (b + 1) * block)
            end = (b + 1) * block
            query = q_ref[rows, lanes]
            outs = []
            for h in range(2):
                masked = jnp.where(lane // HEAD == h, query, jnp.zeros_like(query))
                scores = dot(masked, keys[:end], ROWS_BY_ROWS) * 0.125
                edge = jnp.where(row >= col, scores[:, b * block :], NEG)
                scores = edge if b == 0 else jnp.concatenate([scores[:, : b * block], edge], axis=1)
                top = jnp.max(scores, axis=-1, keepdims=True)
                weights = jnp.exp(scores - top)
                total = jnp.sum(weights, axis=-1, keepdims=True)
                outs.append(dot(weights.astype(BF), values[:end]) / total)
                lse[rows, :] = jnp.where(lane == 2 * hp + h, top + jnp.log(total), lse[rows, :])
            out = jnp.where(lane < HEAD, outs[0], outs[1])
            first[rows, :] += out
            second[rows, :] += out * out
            out_ref[rows, lanes] = out.astype(BF)
        return 0

    lax.fori_loop(0, width // LANES, pair, 0)
    lse_ref[...] = lse[...].T[: lse_ref.shape[0]]
    stat_ref[...] = two_rows(rows_from(first[...]), rows_from(second[...]))


def total_columns(stats):
    total = stats[0][...]
    for other in stats[1:]:
        total = total + other[...]
    return columns_of(total)


def stat_norm(values, columns, at, width):
    mean = columns[:, at : at + 1] / width
    square = columns[:, at + 1 : at + 2] / width
    inv_std = lax.rsqrt(square - mean * mean + EPS)
    return (values - mean) * inv_std, inv_std


def mid_body(meta, *refs, mp, width):
    att, gain_ref, weight_ref = refs[:2], refs[2], refs[3]
    stats = (refs[4 : 4 + mp], refs[4 + mp : 4 + 2 * mp])
    mids, outs = refs[4 + 2 * mp : 6 + 2 * mp], refs[6 + 2 * mp :]
    for n in range(2):
        normed, _ = stat_norm(att[n][...].astype(F32), total_columns(stats[n]), 0, width)
        mid = (normed * gain_ref[...]).astype(BF)
        mids[n][...] = mid
        outs[n][...] = dot(mid, weight_ref[...]).astype(BF)


def after_body(meta, own_ref, core_ref, far_ref, text_ref, slots_ref, table_ref, gain_ref, after_ref, low_ref):
    mixed = mixed_rows(meta, text_ref, slots_ref, table_ref)
    after = mixed + (
        own_ref[...].astype(F32) + core_ref[...].astype(F32) + far_ref[...].astype(F32)
    )
    after_ref[...] = after
    low_ref[...] = (norm_parts(after)[0] * gain_ref[...]).astype(BF)


def mixed_rows(meta, text_ref, slots_ref, table_ref):
    block = meta[PART] * pl.num_programs(0) + pl.program_id(0)
    filled = meta[BLOCK + block] >= 0
    return (
        jnp.where(filled, slots_ref[0].astype(F32), text_ref[...].astype(F32))
        + kind_of(meta, table_ref)
    )


def slot_index(blocks):
    return lambda i, m: (jnp.maximum(m[BLOCK + m[PART] * blocks + i], 0), 0, 0)


def times_rows_body(meta, *refs):
    pieces, weight_ref, out_ref = refs[:-2], refs[-2], refs[-1]
    rows = pieces[0].shape[0]
    for n, piece in enumerate(pieces):
        out_ref[n * rows : (n + 1) * rows, :] = dot(
            piece[...], weight_ref[...], ROWS_BY_ROWS
        ).astype(out_ref.dtype)


def up_body(meta, a_ref, b_ref, weight_ref, dup_ref, gain_ref, act_ref, slope_ref, stat_ref, *sums):
    step = pl.program_id(0)
    rows = a_ref.shape[0]

    @pl.when(step == 0)
    def _():
        for ref in sums:
            ref[...] = jnp.zeros_like(ref)

    for n, ref in enumerate((a_ref, b_ref)):
        here = slice(n * rows, (n + 1) * rows)
        pre = dot(ref[...], weight_ref[...])
        share = 0.5 + 0.5 * lax.erf(pre * (0.5**0.5))
        density = jnp.exp(pre * pre * -0.5) * ((2.0 * jnp.pi) ** -0.5)
        act = pre * share
        act_ref[here, :] = act.astype(BF)
        slope_ref[here, :] = (share + pre * density).astype(BF)
        scaled = dup_ref[here, :].astype(F32) * gain_ref[...]
        for ref_sum, term in zip(sums, (act, act * act, scaled, scaled * act)):
            ref_sum[here, :] += lane_sums(term)

    @pl.when(step == pl.num_programs(0) - 1)
    def _():
        for n, ref_sum in enumerate(sums):
            stat_ref[n : n + 1, :] = rows_from(ref_sum[...])[:1]
        stat_ref[4:, :] = jnp.zeros_like(stat_ref[4:, :])


def back_body(meta, act_ref, slope_ref, dup_ref, gain_ref, weight_ref, *refs, mp, width):
    stats, outs = refs[:mp], refs[mp:]
    pre_ref, low_ref, first_ref, second_ref, grad_ref = outs
    step = pl.program_id(0)
    columns = total_columns(stats)
    act = act_ref[...].astype(F32)
    normed, inv_std = stat_norm(act, columns, 0, width)
    gain = gain_ref[...]
    low_ref[...] = (normed * gain).astype(BF)
    upstream = dup_ref[...].astype(F32)
    first = columns[:, 2:3] / width
    mean = columns[:, 0:1] / width
    second = (columns[:, 3:4] - mean * columns[:, 2:3]) * inv_std / width
    d_act = inv_std * (upstream * gain - first - normed * second)
    d_pre = (d_act * slope_ref[...].astype(F32)).astype(BF)
    pre_ref[...] = d_pre
    gained = jnp.sum(upstream * normed, axis=0, keepdims=True)

    @pl.when(step == 0)
    def _():
        grad_ref[...] = gained

    @pl.when(step != 0)
    def _():
        grad_ref[...] += gained

    product = dot(d_pre, weight_ref[...], ROWS_BY_ROWS).astype(BF)

    @pl.when(step == 0)
    def _():
        first_ref[...] = product

    @pl.when(step != 0)
    def _():
        second_ref[...] = product


def down_body(meta, near_ref, far_ref, weight_ref, *outs):
    rows = outs[0].shape[0]
    for n, ref in enumerate((near_ref, far_ref)):
        for m in range(2):
            outs[2 * n + m][...] = dot(
                ref[m * rows : (m + 1) * rows, :], weight_ref[...]
            ).astype(BF)


def ffn_back_body(meta, own_ref, core_ref, far_ref, after_ref, cot_ref, gain_ref, out_ref, low_ref, grad_ref):
    upstream = own_ref[...].astype(F32) + core_ref[...].astype(F32) + far_ref[...].astype(F32)
    normed, inv_std = norm_parts(after_ref[...])
    d_after = cot_ref[...].astype(F32) + norm_back(upstream, normed, inv_std, gain_ref[...])
    out_ref[...] = d_after
    low_ref[...] = d_after.astype(BF)
    add_rows(grad_ref, upstream * normed)


def add_rows(ref, values):
    total = jnp.sum(values, axis=0, keepdims=True)

    @pl.when(pl.program_id(0) == 0)
    def _():
        ref[...] = total

    @pl.when(pl.program_id(0) != 0)
    def _():
        ref[...] += total


def d_mid_body(meta, *refs, mp, width):
    pieces, weight_ref, gain_ref, att_ref = refs[:2], refs[2], refs[3], refs[4]
    stats = refs[5 : 5 + mp]
    out_ref, stat_ref, grad_ref = refs[-3:]
    rows = jnp.where(pl.program_id(0) == 0, pieces[0][...], pieces[1][...])
    d_mid = dot(rows, weight_ref[...], ROWS_BY_ROWS)
    out_ref[...] = d_mid.astype(BF)
    normed, _ = stat_norm(att_ref[...].astype(F32), total_columns(stats), 0, width)
    scaled = d_mid * gain_ref[...]
    add_rows(grad_ref, d_mid * normed)
    stat_ref[...] = two_rows(
        rows_from(lane_sums(scaled)), rows_from(lane_sums(scaled * normed))
    )


def d_mid_body_more(meta, *refs, mp, width):
    d_mid_body(meta, *refs[: 5 + mp], *refs[7 + mp :], mp=mp, width=width)


def attend_back_body(
    meta, q_ref, k_ref, v_ref, att_ref, dmid_ref, lse_ref, gain_ref, turn_ref, *refs, mp, width, block
):
    stats, more = refs[:mp], refs[mp : 2 * mp]
    out_ref, d_att, dq, dk, dv = refs[2 * mp :]
    length, wide = q_ref.shape
    columns = total_columns(stats)
    normed, inv_std = stat_norm(att_ref[...].astype(F32), columns, 0, width)
    sums = total_columns(more)
    scaled = dmid_ref[...].astype(F32) * gain_ref[...]
    d_att[...] = (
        inv_std * (scaled - sums[:, 0:1] / width - normed * (sums[:, 1:2] / width))
    ).astype(BF)

    def pair(hp, _):
        lanes = pl.ds(pl.multiple_of(hp * LANES, LANES), LANES)
        keys, values = k_ref[:, lanes], v_ref[:, lanes]
        lane = lax.broadcasted_iota(jnp.int32, (block, LANES), 1)
        row = lax.broadcasted_iota(jnp.int32, (block, block), 0)
        col = lax.broadcasted_iota(jnp.int32, (block, block), 1)
        dk[...] = jnp.zeros_like(dk)
        dv[...] = jnp.zeros_like(dv)
        both = d_att[:, lanes].astype(F32) * att_ref[:, lanes].astype(F32)
        side = lax.broadcasted_iota(jnp.int32, (8, LANES), 1) // HEAD
        pick_head = lax.broadcasted_iota(jnp.int32, (8, LANES), 0) == side
        inner = dot_exact(pick_head.astype(F32), both)
        for b in range(length // block):
            rows = slice(b * block, (b + 1) * block)
            end = (b + 1) * block
            query, grad = q_ref[rows, lanes], d_att[rows, lanes]
            d_query = jnp.zeros((block, LANES), F32)
            for h in range(2):
                keep = lane // HEAD == h
                q_one = jnp.where(keep, query, jnp.zeros_like(query))
                g_one = jnp.where(keep, grad, jnp.zeros_like(grad))
                scores = dot(keys[:end], q_one, ROWS_BY_ROWS) * 0.125
                shares = jnp.exp(scores - lse_ref[pl.ds(2 * hp + h, 1), rows])
                edge = jnp.where(col >= row, shares[b * block :], 0.0)
                shares = edge if b == 0 else jnp.concatenate([shares[: b * block], edge], axis=0)
                d_shares = dot(values[:end], g_one, ROWS_BY_ROWS)
                d_scores = (shares * (d_shares - inner[h : h + 1, rows])).astype(BF)
                dv[:end, :] += dot(shares.astype(BF), g_one)
                dk[:end, :] += dot(d_scores, q_one)
                turned = dot(d_scores, keys[:end], OVER_ROWS)
                d_query = jnp.where(keep, turned, d_query)
            dq[rows, :] = d_query
        at = pl.multiple_of(hp * LANES, LANES)
        out_ref[:, pl.ds(at, LANES)] = rotated(
            dq[...] * 0.125, turn_ref[0], -turn_ref[1]
        ).astype(BF)
        out_ref[:, pl.ds(wide + at, LANES)] = rotated(
            dk[...] * 0.125, turn_ref[2], -turn_ref[3]
        ).astype(BF)
        out_ref[:, pl.ds(2 * wide + at, LANES)] = dv[...].astype(BF)
        return 0

    lax.fori_loop(0, wide // LANES, pair, 0)


def slot_back_body(meta, *refs, slots, mp):
    pieces, weight_ref, out_ref, scratch = refs[:slots], refs[slots], refs[-2], refs[-1]
    rows = jnp.concatenate([p[...] for p in pieces], axis=0)
    scratch[...] = dot(rows, weight_ref[...], ROWS_BY_ROWS)
    latent = pieces[0].shape[0]
    part = latent // mp
    for j in range(mp):
        for s in range(slots):
            start = pl.multiple_of(s * latent + (meta[PART] ^ j) * part, part)
            out_ref[j, s] = scratch[pl.ds(start, part), :].astype(BF)


def row_back_body(meta, a_ref, b_ref, weight_ref, a_out, b_out):
    a_out[...] = dot(a_ref[...], weight_ref[...], ROWS_BY_ROWS).astype(BF)
    b_out[...] = dot(b_ref[...], weight_ref[...], ROWS_BY_ROWS).astype(BF)


def slot_grad_body(meta, *refs, mp, slots, latent):
    own_ref, core_ref, far_ref, slots_ref, table_ref, gain_ref = refs[:6]
    after, out_ref = refs[6:-1], refs[-1]
    part = latent // mp
    start = pl.multiple_of(meta[PART] * part, part)
    for s in range(slots):
        upstream = (
            own_ref[s].astype(F32) + core_ref[s].astype(F32) + far_ref[s].astype(F32)
        )
        mixed = slots_ref[s, pl.ds(start, part), :].astype(F32) + kind_of(meta, table_ref)
        normed, inv_std = norm_parts(mixed)
        block = meta[POS + s]
        blocks = after[0].shape[0] // latent
        rel = (block // blocks) ^ meta[PART]
        row = pl.multiple_of((block % blocks) * latent + start, part)
        d_after = after[0][pl.ds(row, part), :]
        for j in range(1, mp):
            d_after = jnp.where(rel == j, after[j][pl.ds(row, part), :], d_after)
        out_ref[s] = (
            d_after.astype(F32) + norm_back(upstream, normed, inv_std, gain_ref[...])
        ).astype(BF)


def place_body(meta, in_ref, out_ref, *, image_local):
    k = pl.program_id(0)
    image = ((k // image_local) ^ meta[GROUP]) * image_local + k % image_local
    out_ref[...] = jnp.where(meta[RANK + image] >= 0, in_ref[...], jnp.zeros_like(in_ref[...]))


def in_back_body(
    meta, own_ref, core_ref, far_ref, after_ref, text_ref, slots_ref, table_ref, gain_ref, out_ref, gain_grad, type_grad
):
    upstream = own_ref[...].astype(F32) + core_ref[...].astype(F32) + far_ref[...].astype(F32)
    normed, inv_std = norm_parts(mixed_rows(meta, text_ref, slots_ref, table_ref))
    d_mixed = after_ref[...] + norm_back(upstream, normed, inv_std, gain_ref[...])
    block = meta[PART] * pl.num_programs(0) + pl.program_id(0)
    out_ref[...] = jnp.where(meta[BLOCK + block] >= 0, 0.0, d_mixed)
    add_rows(gain_grad, upstream * normed)
    add_rows(type_grad, d_mixed)


def pool_back_body(
    meta, grad_ref, out_w, key_ref, value_ref, query_ref, key_w, value_w, kv_ref, query_grad, clip_ref, scratch, *, images, mp
):
    d_heads = dot(grad_ref[...], out_w[...], ROWS_BY_ROWS).astype(BF)
    patches = key_ref.shape[0] // images
    latent, wide = query_ref.shape
    for pair in range(wide // LANES):
        lanes = slice(pair * LANES, (pair + 1) * LANES)
        query = query_ref[:, lanes]
        lane = lax.broadcasted_iota(jnp.int32, query.shape, 1)
        d_query = jnp.zeros((latent, LANES), F32)
        for i in range(images):
            rows = slice(i * patches, (i + 1) * patches)
            keys, values = key_ref[rows, lanes], value_ref[rows, lanes]
            grad = d_heads[i * latent : (i + 1) * latent, lanes]
            d_keys = jnp.zeros((patches, LANES), F32)
            d_values = jnp.zeros((patches, LANES), F32)
            for h in range(2):
                keep = lane // HEAD == h
                shares = pool_shares_of(query, keys, h)
                g_one = jnp.where(keep, grad, jnp.zeros_like(grad))
                q_one = jnp.where(keep, query, jnp.zeros_like(query))
                d_shares = dot(g_one, values, ROWS_BY_ROWS)
                inner = jnp.sum(shares * d_shares, axis=-1, keepdims=True)
                d_scores = (shares * (d_shares - inner)).astype(BF)
                d_query += jnp.where(keep, dot(d_scores, keys), 0.0)
                d_keys += dot(d_scores, q_one, OVER_ROWS)
                d_values += dot(shares.astype(BF), g_one, OVER_ROWS)
            kv_ref[rows, lanes] = (d_keys * 0.125).astype(BF)
            kv_ref[rows, slice(wide + pair * LANES, wide + (pair + 1) * LANES)] = d_values.astype(BF)
        query_grad[:, lanes] = d_query * 0.125
    scratch[...] = dot(kv_ref[:, :wide], key_w[...], ROWS_BY_ROWS) + dot(
        kv_ref[:, wide:], value_w[...], ROWS_BY_ROWS
    )
    piece = patches // mp
    for j in range(mp):
        for i in range(images):
            start = pl.multiple_of(i * patches + (meta[PART] ^ j) * piece, piece)
            clip_ref[j, i] = scratch[pl.ds(start, piece), :].astype(BF)


def weight_body(meta, *refs, lefts, rights):
    left, right, rest = refs[:lefts], refs[lefts : lefts + rights], refs[lefts + rights :]
    depth = sum(r.shape[0] for r in left)
    total = None
    step = depth // max(lefts, rights)
    for start in range(0, depth, step):
        l_ref, l_at = find(left, start)
        r_ref, r_at = find(right, start)
        term = dot(l_ref[l_at : l_at + step, :], r_ref[r_at : r_at + step, :], OVER_ROWS)
        total = term if total is None else total + term
    if len(rest) == 1:
        rest[0][0] = total.astype(BF)
        return
    got, even, odd = rest
    total = (total + got[0].astype(F32)).astype(BF)
    step = pl.program_id(0)

    @pl.when(step % 2 == 0)
    def _():
        even[0] = total

    @pl.when(step % 2 == 1)
    def _():
        odd[0] = total


def find(refs, start):
    for ref in refs:
        if start < ref.shape[0]:
            return ref, start
        start -= ref.shape[0]
    return None


def weight_grads(meta, left, right):
    size = lax.axis_size("dp")
    rows, width = sum(a.shape[0] for a in left), left[0].shape[1]
    inner = right[0].shape[1]
    part = width // size
    bits = bits_of(size)
    if part % LANES or size < 4:
        whole = dot(jnp.concatenate(left), jnp.concatenate(right), OVER_ROWS).astype(BF)
        whole = whole.reshape(size, part, inner)
        me = lax.axis_index("dp")
        return scatter_dp(pick(whole, [me ^ k for k in range(size)]), bits, F32)
    half = size // 2

    def run(odd, got):
        ins = [
            (a, (a.shape[0], part), lambda i, m: (0, m[GROUP] ^ (2 * i + odd))) for a in left
        ] + [(a,) for a in right]
        if got is None:
            outs = [((half, part, inner), BF, (1, part, inner), lambda i, m: (i, 0, 0))]
        else:
            ins.append((got, (1, part, inner), lambda i, m: (i, 0, 0)))
            outs = [
                ((half // 2, part, inner), BF, (1, part, inner), lambda i, m: (i // 2, 0, 0))
            ] * 2
        return call(
            functools.partial(weight_body, lefts=len(left), rights=len(right)),
            meta,
            (half,),
            ins,
            outs,
            flops=rows * width * inner,
        )

    send = run(1, None)[0]
    keep, send = run(0, swap(send, "dp", 1))
    for bit in bits[1:]:
        got = swap(send, "dp", bit)
        if bit == bits[-1]:
            return (keep.astype(F32) + got.astype(F32))[0]
        values = add_low(keep, got)
        values = values.reshape((-1, 2) + values.shape[1:])
        keep, send = halve(values, 1)


def shards(
    text_embed,
    clip_feats,
    type_table,
    gain_attn_in,
    qkv_weight,
    gain_attn_out,
    out_weight,
    gain_ffn_in,
    up_weight,
    gain_ffn_out,
    down_weight,
    res_query,
    res_key,
    res_value,
    res_out,
    cotangent,
    owner_count,
    image_seq,
    slot_block,
    seq_kind,
):
    mp = lax.axis_size("mp")
    dp = lax.axis_size("dp")
    rows, width = text_embed.shape
    length = rows * mp
    latent = res_query.shape[0]
    slots = slot_block.shape[1]
    images, patches, clip_width = clip_feats.shape
    wide = qkv_weight.shape[2]
    heads = wide // HEAD
    ff = up_weight.shape[1]
    ff_all = ff * mp
    here = rows // latent
    part = latent // mp
    tile = 512

    meta = make_meta(owner_count, image_seq, slot_block, seq_kind, images)
    table = type_table.astype(F32)
    gain_in, gain_out = gain_attn_in[None], gain_attn_out[None]
    gain_ffn, gain_ff = gain_ffn_in[None], gain_ffn_out[None]
    row_block = lambda i, m: (i, 0)

    text_in = call(
        text_body,
        meta,
        (4,),
        [(text_embed, (rows // 4, width), row_block), (table,), (gain_in,)],
        [((rows, width), BF, (rows // 4, width), row_block)],
    )[0]
    text_pieces = gather_rel(text_in)

    clip = clip_feats.reshape(images * patches, clip_width)
    key_proj, value_proj, pool_out, pool_part = call(
        functools.partial(pool_body, images=images, mp=mp),
        meta,
        (1,),
        [(clip,), (res_key,), (res_value,), (res_query,), (res_out,)],
        [
            ((images * patches, wide), BF, None, None),
            ((images * patches, wide), BF, None, None),
            ((images * latent, wide), BF, None, None),
            ((mp, images, part, width), BF, None, None),
        ],
        scratch=[pltpu.VMEM((images * latent, width), F32)],
        flops=4 * images * patches * clip_width * wide,
    )
    pooled = sum_three([pool_part[j] for j in range(mp)]).astype(BF)
    pooled = gather_dp(pooled).reshape(dp * images, part, width)
    slot_piece = call(
        copy_body,
        meta,
        (slots,),
        [(pooled, (1, part, width), lambda i, m: (m[SOURCE + i], 0, 0))],
        [((slots, part, width), BF, (1, part, width), lambda i, m: (i, 0, 0))],
    )[0]
    slot_pieces = gather_rel(slot_piece)
    cot_pieces = gather_rel(cotangent)

    weight = qkv_weight.reshape(width, 3 * wide)
    turn = turn_tables(length)
    state = project(meta, text_pieces[:2], weight, turn, None, 0)
    state = project(meta, text_pieces[2:], weight, turn, state, 2)
    at_slot = lambda i, m: (m[POS + i], 0)
    state = call(
        functools.partial(slot_body, mp=mp, slots=slots, latent=latent),
        meta,
        (slots,),
        [(p,) for p in slot_pieces]
        + [(table,), (gain_in,), (weight,)]
        + [(turn, (4, latent, LANES), lambda i, m: (0, m[POS + i], 0))]
        + [(a, (latent, a.shape[1]), at_slot) for a in state],
        [(a.shape, BF, (latent, a.shape[1]), at_slot) for a in state]
        + [((slots, latent, width), BF, None, None)],
        scratch=[
            pltpu.VMEM((slots, latent, width), F32),
            pltpu.VMEM((slots, latent, 3 * wide), F32),
            pltpu.VMEM((slots, latent, width), BF),
        ],
        flops=6 * slots * latent * width * wide,
        aliases={mp + 5 + n: n for n in range(4)},
    )
    query, keys, values, in_full, slot_rows = state

    att, lse, att_stats = call(
        functools.partial(attend_body, block=rows),
        meta,
        (1,),
        [(query,), (keys,), (values,)],
        [
            ((length, wide), BF, None, None),
            ((heads, length), F32, None, None),
            ((8, length), F32, None, None),
        ],
        scratch=[pltpu.VMEM((length, LANES), F32)] * 3,
        flops=4 * length * length * wide,
    )
    att_stats = spread_stats(att_stats)

    def mid_terms(which):
        places = [which, which + 1]
        block = [lambda i, m, j=j: (m[PART] ^ j, 0) for j in places]
        lane_block = [lambda i, m, j=j: (0, m[PART] ^ j) for j in places]
        return call(
            functools.partial(mid_body, mp=mp, width=width),
            meta,
            (1,),
            [(att, (rows, wide), block[n]) for n in range(2)]
            + [(gain_out,), (out_weight,)]
            + [(s, (8, rows), lane_block[n]) for n in range(2) for s in att_stats],
            [((rows, wide), BF, None, None)] * 2 + [((rows, width), BF, None, None)] * 2,
            flops=4 * rows * wide * width,
        )

    mid_2, mid_3, out_2, out_3 = mid_terms(2)
    mid_0, mid_1, out_0, out_1 = mid_terms(0)
    mids = [mid_0, mid_1, mid_2, mid_3]
    out_terms = scatter_rel([out_0, out_1, out_2, out_3])
    few = (latent, width)
    after_attn, ffn_in = call(
        after_body,
        meta,
        (here,),
        [(t, few, row_block) for t in out_terms]
        + [(text_embed, few, row_block), (slot_rows, (1,) + few, slot_index(here))]
        + [(table,), (gain_ffn,)],
        [((rows, width), F32, few, row_block), ((rows, width), BF, few, row_block)],
    )
    ffn_pieces = gather_rel(ffn_in)

    d_up = call(
        times_rows_body,
        meta,
        (ff // tile,),
        [(p,) for p in cot_pieces] + [(down_weight, (tile, width), row_block)],
        [((length, ff), BF, (length, tile), lambda i, m: (0, i))],
        flops=2 * length * width * ff,
    )[0]

    def up_half(which):
        return call(
            up_body,
            meta,
            (ff // tile,),
            [(ffn_pieces[which],), (ffn_pieces[which + 1],)]
            + [(up_weight, (width, tile), lambda i, m: (0, i))]
            + [(d_up, (2 * rows, tile), lambda i, m: (which // 2, i))]
            + [(gain_ff, (1, tile), lambda i, m: (0, i))],
            [
                ((2 * rows, ff), BF, (2 * rows, tile), lambda i, m: (0, i)),
                ((2 * rows, ff), BF, (2 * rows, tile), lambda i, m: (0, i)),
                ((8, 2 * rows), F32, None, None),
            ],
            scratch=[pltpu.VMEM((2 * rows, LANES), F32)] * 4,
            flops=4 * rows * width * ff,
        )

    act_near, slope_near, stat_near = up_half(0)
    act_far, slope_far, stat_far = up_half(2)
    ff_stats = spread_stats(jnp.concatenate([stat_near, stat_far], axis=1))

    def back_half(act, slope, which):
        block = (rows, ff)
        flip = lambda i, m: (1 - i, 0)
        return call(
            functools.partial(back_body, mp=mp, width=ff_all),
            meta,
            (2,),
            [(act, block, flip), (slope, block, flip)]
            + [(d_up, block, lambda i, m: (which + 1 - i, 0)), (gain_ff,), (up_weight,)]
            + [
                (s, (8, rows), lambda i, m, b=b: (0, (which + 1 - i) ^ b))
                for b, s in enumerate(ff_stats)
            ],
            [((2 * rows, ff), BF, block, flip)] * 2
            + [((rows, width), BF, None, None)] * 2
            + [((1, ff), F32, None, None)],
            flops=4 * rows * width * ff,
        )

    pre_far, low_far, back_3, back_2, gain_far = back_half(act_far, slope_far, 2)
    pre_near, low_near, back_1, back_0, gain_near = back_half(act_near, slope_near, 0)
    ffn_terms = scatter_rel([back_0, back_1, back_2, back_3])
    down_grad = weight_grads(meta, cot_pieces, [low_near, low_far]).T
    up_grad = weight_grads(meta, ffn_pieces, [pre_near, pre_far])
    d_after, d_after_low, gain_ffn_local = call(
        ffn_back_body,
        meta,
        (here,),
        [(t, few, row_block) for t in ffn_terms]
        + [(after_attn, few, row_block), (cotangent, few, row_block), (gain_ffn,)],
        [
            ((rows, width), F32, few, row_block),
            ((rows, width), BF, few, row_block),
            ((1, width), F32, None, None),
        ],
    )
    after_pieces = gather_rel(d_after_low)

    down_terms = call(
        down_body,
        meta,
        (width // tile,),
        [(low_near,), (low_far,), (down_weight, (ff, tile), lambda i, m: (0, i))],
        [((rows, width), BF, (rows, tile), lambda i, m: (0, i))] * mp,
        flops=2 * length * width * ff,
    )
    layer_out = after_attn + sum_three(down_terms)

    def d_mid_half(which, before):
        block = lambda i, m: (m[PART] ^ (which + i), 0)
        lane_block = lambda i, m: (0, m[PART] ^ (which + i))
        body, aliases = d_mid_body, {}
        ins = [(after_pieces[which],), (after_pieces[which + 1],), (out_weight,), (gain_out,)]
        ins += [(att, (rows, wide), block)] + [(s, (8, rows), lane_block) for s in att_stats]
        if before is not None:
            body = d_mid_body_more
            aliases = {len(ins) + 1 + n: n for n in range(2)}
            ins += [(a, None) for a in before]
        return call(
            functools.partial(body, mp=mp, width=width),
            meta,
            (2,),
            ins,
            [
                ((length, wide), BF, (rows, wide), block),
                ((8, length), F32, (8, rows), lane_block),
                ((1, wide), F32, None, None),
            ],
            flops=4 * rows * wide * width,
            aliases=aliases,
        )

    d_mid, mid_stats, gain_mid_near = d_mid_half(0, None)
    d_mid, mid_stats, gain_mid_far = d_mid_half(2, (d_mid, mid_stats))
    mid_stats = spread_stats(mid_stats)
    out_grad = weight_grads(meta, after_pieces, mids).T
    d_qkv = call(
        functools.partial(attend_back_body, mp=mp, width=width, block=rows),
        meta,
        (1,),
        [(a,) for a in (query, keys, values, att, d_mid, lse, gain_out, turn)]
        + [(s,) for s in att_stats]
        + [(s,) for s in mid_stats],
        [((length, 3 * wide), BF, None, None)],
        scratch=[pltpu.VMEM((length, wide), BF)] + [pltpu.VMEM((length, LANES), F32)] * 3,
        flops=10 * length * length * wide,
    )[0]

    slot_terms = call(
        functools.partial(slot_back_body, slots=slots, mp=mp),
        meta,
        (1,),
        [
            (d_qkv, (latent, 3 * wide), lambda i, m, s=s: (m[POS + s], 0))
            for s in range(slots)
        ]
        + [(weight,)],
        [((mp, slots, part, width), BF, None, None)],
        scratch=[pltpu.VMEM((slots * latent, width), F32)],
        flops=6 * slots * latent * width * wide,
    )[0]
    slot_terms = scatter_rel([slot_terms[j] for j in range(mp)])
    slot_grad = call(
        functools.partial(slot_grad_body, mp=mp, slots=slots, latent=latent),
        meta,
        (1,),
        [(t,) for t in slot_terms]
        + [(slot_rows,), (table,), (gain_in,)]
        + [(a,) for a in after_pieces],
        [((slots, part, width), BF, None, None)],
    )[0]
    image_of = lambda k, m: ((k // images) ^ m[GROUP]) * images + k % images
    image_grad = call(
        functools.partial(place_body, image_local=images),
        meta,
        (dp * images,),
        [
            (
                slot_grad,
                (1, part, width),
                lambda k, m: (jnp.maximum(m[RANK + image_of(k, m)], 0), 0, 0),
            )
        ],
        [((dp * images, part, width), BF, (1, part, width), lambda k, m: (k, 0, 0))],
    )[0]
    owned = scatter_dp(image_grad.reshape(dp, images, part, width), bits_of(dp), BF)
    pool_grad = jnp.swapaxes(by_mp(jnp.stack(gather_rel(owned))), 0, 1).reshape(
        images * latent, width
    )
    d_kv, query_local, clip_terms = call(
        functools.partial(pool_back_body, images=images, mp=mp),
        meta,
        (1,),
        [(a,) for a in (pool_grad, res_out, key_proj, value_proj, res_query, res_key, res_value)],
        [
            ((images * patches, 2 * wide), BF, None, None),
            ((latent, wide), F32, None, None),
            ((mp, images, patches // mp, clip_width), BF, None, None),
        ],
        scratch=[pltpu.VMEM((images * patches, clip_width), F32)],
        flops=4 * images * patches * clip_width * wide,
    )
    res_out_grad = weight_grads(meta, [pool_grad], [pool_out]).T
    kv_grad = weight_grads(meta, [clip], [d_kv])
    clip_grad = sum_three([clip_terms[j] for j in range(mp)])

    def row_terms(which):
        return call(
            row_back_body,
            meta,
            (1,),
            [
                (d_qkv, (rows, 3 * wide), lambda i, m, j=j: (m[PART] ^ j, 0))
                for j in (which, which + 1)
            ]
            + [(weight,)],
            [((rows, width), BF, None, None)] * 2,
            flops=12 * rows * width * wide,
        )

    in_2, in_3 = row_terms(2)
    in_0, in_1 = row_terms(0)
    in_terms = scatter_rel([in_0, in_1, in_2, in_3])
    qkv_grad = weight_grads(meta, [in_full], [d_qkv]).reshape(-1, 3, wide)
    text_grad, gain_in_local, type_local = call(
        in_back_body,
        meta,
        (here,),
        [(t, few, row_block) for t in in_terms]
        + [(d_after, few, row_block), (text_embed, few, row_block)]
        + [(slot_rows, (1,) + few, slot_index(here)), (table,), (gain_in,)],
        [
            ((rows, width), F32, few, row_block),
            ((1, width), F32, None, None),
            ((1, width), F32, None, None),
        ],
    )
    kind = (jnp.arange(3) == meta[KIND]).astype(F32)[:, None]
    sums, parts = sum_small(
        jnp.concatenate([kind * type_local, gain_in_local, gain_ffn_local]),
        jnp.concatenate(
            [
                (gain_mid_near + gain_mid_far)[0],
                (gain_near + gain_far)[0],
                query_local.reshape(-1),
            ]
        ),
    )
    query_grad = jnp.swapaxes(parts[:, wide + ff :].reshape(mp, latent, wide), 0, 1)
    return (
        layer_out,
        text_grad,
        clip_grad,
        sums[:3],
        sums[3],
        qkv_grad,
        parts[:, :wide].reshape(-1),
        out_grad,
        sums[4],
        up_grad,
        parts[:, wide : wide + ff].reshape(-1),
        down_grad,
        query_grad.reshape(latent, width),
        kv_grad[:, :wide],
        kv_grad[:, wide:],
        res_out_grad,
    )


def solution(mesh):
    return jax.shard_map(
        shards,
        mesh=mesh,
        in_specs=(
            P(("dp", "mp"), None),
            P("dp", None, None),
            P(),
            P(),
            P(None, None, "mp"),
            P("mp"),
            P("mp", None),
            P(),
            P(None, "mp"),
            P("mp"),
            P("mp", None),
            P(None, "mp"),
            P(None, "mp"),
            P(None, "mp"),
            P("mp", None),
            P(("dp", "mp"), None),
            P(),
            P(),
            P(),
            P(),
        ),
        out_specs=(
            P(("dp", "mp"), None),
            P(("dp", "mp"), None),
            P("dp", "mp", None),
            P(),
            P(),
            P("dp", None, "mp"),
            P(),
            P("mp", "dp"),
            P(),
            P("dp", "mp"),
            P(),
            P("mp", "dp"),
            P(),
            P("dp", "mp"),
            P("dp", "mp"),
            P("mp", "dp"),
        ),
        check_vma=False,
    )
```

time: 1870 us -> 888 us (0.47)
  waiting for transfers between devices: 1320 us -> 349 us
  Pallas kernels: 0 us -> 360 us
  matrix products: 266 us -> 0 us
  local copies, waits for them, and re-layouts: 125 us -> 61.1 us
  starting transfers between devices: 1.85 us -> 59.1 us
  other arithmetic: 97.5 us -> 43.9 us
  blocking collectives: 30.7 us -> 0 us
    reduce_scatter x12 -> x0, waiting for transfers between devices: 828 us -> none  [the longest x5 523 us: weight_grads(): lax.psum_scatter(lax.dot_general(left, right, (((0,), (0,)), ((), ())), p...]
    pallas_call x0 -> x40, Pallas kernels: none -> 360 us  [the longest x39 358 us: call(): pl.pallas_call(body, out_shape=shapes, grid_spec=pltpu.PrefetchScalarGrid...]
    ppermute x0 -> x81, waiting for transfers between devices: none -> 349 us  [swap(): return lax.ppermute(values, axis, [(i, i ^ bit) for i in range(size)])]
    dot_general x43 -> x0, matrix products: 266 us -> none  [the longest x6 52 us: weight_grads(): lax.dot_general(left, right, (((0,), (0,)), ((), ())), preferred_element_...]
    psum x2 -> x0, waiting for transfers between devices: 262 us -> none  [shards(): lax.psum((gain_attn_in_local, gain_ffn_in_local, type_local, spread(gain_...]
    all_gather x5 -> x0, waiting for transfers between devices: 162 us -> none  [the longest x4 101 us: full_rows(): return lax.all_gather(values, 'mp', axis=0, tiled=True)]
    unnamed x21 -> x0, waiting for transfers between devices: 70.2 us -> none
    ppermute x0 -> x81, starting transfers between devices: none -> 59.1 us  [swap(): return lax.ppermute(values, axis, [(i, i ^ bit) for i in range(size)])]
  transfers between devices with their start and end apart: 20 -> 81, of which waited for: 19 -> 28; matrix products, arithmetic and copies ran while one was open for 8% -> 9% of each run, Pallas kernels for 0% -> 33%
where the time goes in v1:
time: 888 us; the launch traced here: 875 us
  Pallas kernels  360 us (41%)
  waiting for transfers between devices  349 us (39%)
  local copies, waits for them, and re-layouts  61.1 us (7%)
  starting transfers between devices  59.1 us (7%)
  other arithmetic  43.9 us (5%)
    pallas_call x39, Pallas kernels, call(): pl.pallas_call(body, out_shape=shapes, grid_spec=pltpu.PrefetchScalarGrid...  358 us
    ppermute x81, waiting for transfers between devices, swap(): return lax.ppermute(values, axis, [(i, i ^ bit) for i in range(size)])  349 us
    ppermute x81, starting transfers between devices, swap(): return lax.ppermute(values, axis, [(i, i ^ bit) for i in range(size)])  59.1 us
    unnamed x144, local copies, waits for them, and re-layouts  38.9 us
  transfers between devices with their start and end apart: 81, of which 28 were waited for; matrix products, arithmetic and copies ran while one was open for 9% of the time, Pallas kernels for 33%

profile of v1, /device:TPU:0, one launch (start us, length us, event | category | flops | bytes accessed | tf_op | source)
XLA Modules:
  0.0 875.4 jit_solution(2101983512803772608)
XLA Ops:
  4.5 10.7 %shard_map.316 = (bf16[512,512]{1,0:T(8,128)(2,1)}, bf16[512,512]{1,0:T(8,128)(2,1)}, bf16[128,512]{1,0:T(8,128)(2,1)}, bf16[4,2,16,2048]{3,2,1,0:T(8,128)(2,1)}) custom-call(s32[48]{0:T(128)} %shard_map.315.meta, bf16[512,1024]{1,0:T(8,128)(2,1)} %bitcast.204, bf16[1024,512]{1,0:T(8,128)(2,1)} %key_w.3, bf16[1024,512]{1,0:T(8,128)(2,1)} %value_w.3, ...), custom_call_target="tpu_custom_call" | custom-call | flops 1073741824 | bytes 7012352 | tf_op jit(solution)/shard_map/pallas_call | solution.py:154
  100.9 10.4 %shard_map.321 = (bf16[1024,512]{1,0:T(8,128)(2,1)}, bf16[1024,512]{1,0:T(8,128)(2,1)}, bf16[1024,512]{1,0:T(8,128)(2,1)}, bf16[1024,2048]{1,0:T(8,128)(2,1)}, bf16[4,64,2048]{2,1,0:T(8,128)(2,1)}) custom-call(s32[48]{0:T(128)} %shard_map.315.meta, ...), custom_call_target="tpu_custom_call", output_to_operand_aliasing={{0}: (9, {}), {1}: (10, {}), {2}: (11, {}), {3}: (12, {})} | custom-call | flops 1610612736 | bytes 25198592 | tf_op jit(solution)/shard_map/pallas_call | solution.py:154
  111.2 17.9 %shard_map.322 = (bf16[1024,512]{1,0:T(8,128)(2,1)}, f32[8,1024]{1,0:T(8,128)}, f32[8,1024]{1,0:T(8,128)}) custom-call(s32[48]{0:T(128)} %shard_map.315.meta, bf16[1024,512]{1,0:T(8,128)(2,1)} %get-tuple-element.106.q_ref, bf16[1024,512]{1,0:T(8,128)(2,1)} %get-tuple-element.107.k_ref, bf16[1024,512]{1,0:T(8,128)(2,1)} %get-tuple-element.108.v_ref), custom_call_target="tpu_custom_call" | custom-call | flops 2147483648 | bytes 4259840 | tf_op jit(solution)/shard_map/pallas_call | solution.py:154
  148.1 23.8 %collective-permute-done.17.far_ref = bf16[256,2048]{1,0:T(8,128)(2,1)S(1)} collective-permute-done((bf16[256,2048]{1,0:T(8,128)(2,1)S(1)}, bf16[256,2048]{1,0:T(8,128)(2,1)S(1)}, u32[]{:S(2)}, u32[]{:S(2)}) %collective-permute-start.17) | collective-permute-done | bytes 1048608 | tf_op jit(solution)/shard_map/ppermute | solution.py:36
  179.3 15.1 %collective-permute-done.20.refs_2_ = bf16[256,2048]{1,0:T(8,128)(2,1)S(1)} collective-permute-done((bf16[256,2048]{1,0:T(8,128)(2,1)S(1)}, bf16[256,2048]{1,0:T(8,128)(2,1)S(1)}, u32[]{:S(2)}, u32[]{:S(2)}) %collective-permute-start.20) | collective-permute-done | bytes 1048608 | tf_op jit(solution)/shard_map/ppermute | solution.py:36
  194.9 21.3 %collective-permute-done.22.a_ref.refs_2_ = bf16[256,2048]{1,0:T(8,128)(2,1)S(1)} collective-permute-done((bf16[256,2048]{1,0:T(8,128)(2,1)}, bf16[256,2048]{1,0:T(8,128)(2,1)S(1)}, u32[]{:S(2)}, u32[]{:S(2)}) %collective-permute-start.22) | collective-permute-done | bytes 1048608 | tf_op jit(solution)/shard_map/ppermute | solution.py:36
  218.2 14.2 %shard_map.326.dup_ref = bf16[1024,2048]{1,0:T(8,128)(2,1)} custom-call(s32[48]{0:T(128)} %shard_map.315.meta, bf16[256,2048]{1,0:T(8,128)(2,1)} %refs_0_.5, bf16[256,2048]{1,0:T(8,128)(2,1)} %copy-done.57, bf16[256,2048]{1,0:T(8,128)(2,1)} %copy-done.55, bf16[256,2048]{1,0:T(8,128)(2,1)} %copy-done.58, bf16[2048,2048]{1,0:T(8,128)(2,1)} %weight_ref.9), custom_call_target="tpu_custom_call" | custom-call | flops 8589934592 | bytes 16777216 | tf_op jit(solution)/shard_map/pallas_call | solution.py:154
  233.4 13.0 %shard_map.327 = (bf16[512,2048]{1,0:T(8,128)(2,1)}, bf16[512,2048]{1,0:T(8,128)(2,1)}, f32[8,512]{1,0:T(8,128)}) custom-call(s32[48]{0:T(128)} %shard_map.315.meta, bf16[256,2048]{1,0:T(8,128)(2,1)} %get-tuple-element.117.a_ref.refs_0_, bf16[256,2048]{1,0:T(8,128)(2,1)} %copy-done.54, bf16[2048,2048]{1,0:T(8,128)(2,1)} %weight_ref.8, ...), custom_call_target="tpu_custom_call" | custom-call | flops 4294967296 | bytes 18898944 | tf_op jit(solution)/shard_map/pallas_call | solution.py:154
  248.1 13.0 %shard_map.328 = (bf16[512,2048]{1,0:T(8,128)(2,1)}, bf16[512,2048]{1,0:T(8,128)(2,1)}, f32[8,512]{1,0:T(8,128)}) custom-call(s32[48]{0:T(128)} %shard_map.315.meta, bf16[256,2048]{1,0:T(8,128)(2,1)} %copy-done.53, bf16[256,2048]{1,0:T(8,128)(2,1)} %copy-done.56, bf16[2048,2048]{1,0:T(8,128)(2,1)} %weight_ref.8, bf16[1024,2048]{1,0:T(8,128)(2,1)} %shard_map.326.dup_ref, ...), custom_call_target="tpu_custom_call" | custom-call | flops 4294967296 | bytes 18898944 | tf_op jit(solution)/shard_map/pallas_call | solution.py:154
  267.3 16.4 %shard_map.330 = (bf16[512,2048]{1,0:T(8,128)(2,1)}, bf16[512,2048]{1,0:T(8,128)(2,1)}, bf16[256,2048]{1,0:T(8,128)(2,1)}, bf16[256,2048]{1,0:T(8,128)(2,1)}, f32[1,2048]{1,0:T(1,128)}) custom-call(s32[48]{0:T(128)} %shard_map.315.meta, bf16[512,2048]{1,0:T(8,128)(2,1)} %get-tuple-element.123.act_ref, bf16[512,2048]{1,0:T(8,128)(2,1)} %get-tuple-element.124.slope_ref, ...), custom_call_target="tpu_custom_call" | custom-call | flops 4294967296 | bytes 23216128 | tf_op jit(solution)/shard_map/pallas_call | solution.py:154
  283.9 16.1 %shard_map.329 = (bf16[512,2048]{1,0:T(8,128)(2,1)}, bf16[512,2048]{1,0:T(8,128)(2,1)}, bf16[256,2048]{1,0:T(8,128)(2,1)}, bf16[256,2048]{1,0:T(8,128)(2,1)}, f32[1,2048]{1,0:T(1,128)}) custom-call(s32[48]{0:T(128)} %shard_map.315.meta, bf16[512,2048]{1,0:T(8,128)(2,1)} %get-tuple-element.118.act_ref, bf16[512,2048]{1,0:T(8,128)(2,1)} %get-tuple-element.119.slope_ref, ...), custom_call_target="tpu_custom_call" | custom-call | flops 4294967296 | bytes 23216128 | tf_op jit(solution)/shard_map/pallas_call | solution.py:154
  302.2 13.7 %shard_map.331 = (bf16[256,2048]{1,0:T(8,128)(2,1)}, bf16[256,2048]{1,0:T(8,128)(2,1)}, bf16[256,2048]{1,0:T(8,128)(2,1)}, bf16[256,2048]{1,0:T(8,128)(2,1)}) custom-call(s32[48]{0:T(128)} %shard_map.315.meta, bf16[512,2048]{1,0:T(8,128)(2,1)} %get-tuple-element.122.near_ref.refs_4_, bf16[512,2048]{1,0:T(8,128)(2,1)} %get-tuple-element.125.far_ref.refs_5_, ...), custom_call_target="tpu_custom_call" | custom-call | flops 8589934592 | bytes 16777216 | tf_op jit(solution)/shard_map/pallas_call | solution.py:154
  326.3 9.7 %shard_map.347 = bf16[4,256,2048]{2,1,0:T(8,128)(2,1)} custom-call(s32[48]{0:T(128)} %shard_map.315.meta, bf16[256,2048]{1,0:T(8,128)(2,1)} %get-tuple-element.117.a_ref.refs_0_, bf16[256,2048]{1,0:T(8,128)(2,1)} %copy-done.54, bf16[256,2048]{1,0:T(8,128)(2,1)} %copy-done.53, bf16[256,2048]{1,0:T(8,128)(2,1)} %copy-done.56, ...), custom_call_target="tpu_custom_call" | custom-call | flops 4294967296 | bytes 12582912 | tf_op jit(solution)/shard_map/pallas_call | solution.py:154
  348.9 22.7 %collective-permute-done.33.refs_0_.refs_8_.refs_2_ = bf16[256,2048]{1,0:T(8,128)(2,1)S(1)} collective-permute-done((bf16[256,2048]{1,0:T(8,128)(2,1)}, bf16[256,2048]{1,0:T(8,128)(2,1)S(1)}, u32[]{:S(2)}, u32[]{:S(2)}) %collective-permute-start.33) | collective-permute-done | bytes 1048608 | tf_op jit(solution)/shard_map/ppermute | solution.py:36
  372.5 21.1 %collective-permute-done.29 = bf16[256,2048]{1,0:T(8,128)(2,1)} collective-permute-done((bf16[256,2048]{1,0:T(8,128)(2,1)}, bf16[256,2048]{1,0:T(8,128)(2,1)}, u32[]{:S(2)}, u32[]{:S(2)}) %collective-permute-start.29) | collective-permute-done | bytes 1048608 | tf_op jit(solution)/shard_map/ppermute | solution.py:36
  420.3 25.2 %shard_map.335.a_ref.b_ref.refs_0_.refs_1_.refs_2_.refs_3_ = bf16[1024,1536]{1,0:T(8,128)(2,1)} custom-call(s32[48]{0:T(128)} %shard_map.315.meta, bf16[1024,512]{1,0:T(8,128)(2,1)} %get-tuple-element.106.q_ref, bf16[1024,512]{1,0:T(8,128)(2,1)} %get-tuple-element.107.k_ref, bf16[1024,512]{1,0:T(8,128)(2,1)} %get-tuple-element.108.v_ref, ...), custom_call_target="tpu_custom_call" | custom-call | flops 5368709120 | bytes 10782720 | tf_op jit(solution)/shard_map/pallas_call | solution.py:154
  454.2 11.4 %shard_map.350 = (bf16[2,256,2048]{2,1,0:T(8,128)(2,1)}, bf16[2,256,2048]{2,1,0:T(8,128)(2,1)}) custom-call(s32[48]{0:T(128)} %shard_map.315.meta, bf16[256,2048]{1,0:T(8,128)(2,1)} %refs_0_.5, bf16[256,2048]{1,0:T(8,128)(2,1)} %copy-done.57, bf16[256,2048]{1,0:T(8,128)(2,1)} %copy-done.55, bf16[256,2048]{1,0:T(8,128)(2,1)} %copy-done.58, ...), custom_call_target="tpu_custom_call" | custom-call | flops 4294967296 | bytes 16777216 | tf_op jit(solution)/shard_map/pallas_call | solution.py:154
  469.2 40.0 %collective-permute-done.69.refs_6_ = bf16[4,256,2048]{2,1,0:T(8,128)(2,1)} collective-permute-done((bf16[4,256,2048]{2,1,0:T(8,128)(2,1)}, bf16[4,256,2048]{2,1,0:T(8,128)(2,1)}, u32[]{:S(2)}, u32[]{:S(2)}) %collective-permute-start.69) | collective-permute-done | bytes 4194336 | tf_op jit(solution)/shard_map/ppermute | solution.py:36
  509.2 11.5 %shard_map.348 = (bf16[2,256,2048]{2,1,0:T(8,128)(2,1)}, bf16[2,256,2048]{2,1,0:T(8,128)(2,1)}) custom-call(s32[48]{0:T(128)} %shard_map.315.meta, bf16[256,2048]{1,0:T(8,128)(2,1)} %get-tuple-element.117.a_ref.refs_0_, bf16[256,2048]{1,0:T(8,128)(2,1)} %copy-done.54, bf16[256,2048]{1,0:T(8,128)(2,1)} %copy-done.53, bf16[256,2048]{1,0:T(8,128)(2,1)} %copy-done.56, ...), custom_call_target="tpu_custom_call" | custom-call | flops 4294967296 | bytes 16777216 | tf_op jit(solution)/shard_map/pallas_call | solution.py:154
  597.8 12.3 %shard_map.342 = (bf16[512,1024]{1,0:T(8,128)(2,1)}, f32[64,512]{1,0:T(8,128)}, bf16[4,2,64,1024]{3,2,1,0:T(8,128)(2,1)}) custom-call(s32[48]{0:T(128)} %shard_map.315.meta, bf16[128,2048]{1,0:T(8,128)(2,1)} %bitcast.207, bf16[512,2048]{1,0:T(8,128)(2,1)} %out_w.3, bf16[512,512]{1,0:T(8,128)(2,1)} %get-tuple-element.146.key_ref, ...), custom_call_target="tpu_custom_call" | custom-call | flops 1073741824 | bytes 8060928 | tf_op jit(solution)/shard_map/pallas_call | solution.py:154
  647.2 25.1 %collective-permute-done.57 = f32[37888]{0:T(1024)S(1)} collective-permute-done((f32[37888]{0:T(1024)S(1)}, f32[37888]{0:T(1024)S(1)}, u32[]{:S(2)}, u32[]{:S(2)}) %collective-permute-start.57) | collective-permute-done | bytes 151584 | tf_op jit(solution)/shard_map/ppermute | solution.py:36
  710.5 46.5 %collective-permute-done.63.refs_2_ = bf16[4,256,1536]{2,1,0:T(8,128)(2,1)} collective-permute-done((bf16[4,256,1536]{2,1,0:T(8,128)(2,1)}, bf16[4,256,1536]{2,1,0:T(8,128)(2,1)}, u32[]{:S(2)}, u32[]{:S(2)}) %collective-permute-start.63) | collective-permute-done | bytes 3145760 | tf_op jit(solution)/shard_map/ppermute | solution.py:36
  781.1 51.3 %collective-permute-done.64 = bf16[2,256,1536]{2,1,0:T(8,128)(2,1)S(1)} collective-permute-done((bf16[2,256,1536]{2,1,0:T(8,128)(2,1)}, bf16[2,256,1536]{2,1,0:T(8,128)(2,1)S(1)}, u32[]{:S(2)}, u32[]{:S(2)}) %collective-permute-start.64) | collective-permute-done | bytes 1572896 | tf_op jit(solution)/shard_map/ppermute | solution.py:36
  843.6 27.9 %collective-permute-done.65 = bf16[1,256,1536]{2,1,0:T(8,128)(2,1)} collective-permute-done((bf16[1,256,1536]{2,1,0:T(8,128)(2,1)}, bf16[1,256,1536]{2,1,0:T(8,128)(2,1)}, u32[]{:S(2)}, u32[]{:S(2)}) %collective-permute-start.65) | collective-permute-done | bytes 786464 | tf_op jit(solution)/shard_map/ppermute | solution.py:36
  (398 shorter events, 383.2 us)
Async XLA Ops:
  37.6 43.0 %collective-permute-start.11 = (bf16[256,2048]{1,0:T(8,128)(2,1)}, bf16[256,2048]{1,0:T(8,128)(2,1)}, u32[]{:S(2)}, u32[]{:S(2)}) collective-permute-start(bf16[256,2048]{1,0:T(8,128)(2,1)} %shard_map.318.near_ref), channel_id=1, source_target_pairs={{0,1},{1,0},{2,3},{3,2},{4,5},{5,4},{6,7},{7,6},{8,9},{9,8},{10,11... | collective-permute-start | bytes 3145736 | tf_op jit(solution)/shard_map/ppermute | solution.py:36
  146.6 47.7 %collective-permute-start.20 = (bf16[256,2048]{1,0:T(8,128)(2,1)S(1)}, bf16[256,2048]{1,0:T(8,128)(2,1)S(1)}, u32[]{:S(2)}, u32[]{:S(2)}) collective-permute-start(bf16[256,2048]{1,0:T(8,128)(2,1)S(1)} %copy-done.13), channel_id=1, source_target_pairs={{0,2},{1,3},{2,0},{3,1},{4,6},{5,7},{6,4},{7,5},{8,10},{9,11},{10,... | collective-permute-start | bytes 3145736 | tf_op jit(solution)/shard_map/ppermute | solution.py:36
  325.6 128.5 %collective-permute-start.72 = (bf16[4,256,2048]{2,1,0:T(8,128)(2,1)}, bf16[4,256,2048]{2,1,0:T(8,128)(2,1)}, u32[]{:S(2)}, u32[]{:S(2)}) collective-permute-start(bf16[4,256,2048]{2,1,0:T(8,128)(2,1)} %shard_map.349), channel_id=1, source_target_pairs={{0,4},{4,0},{8,12},{12,8},{16,20},{20,16},{24,28},{28,24},{1,5},{5... | collective-permute-start | bytes 12582920 | tf_op jit(solution)/shard_map/ppermute | solution.py:36
  336.0 173.2 %collective-permute-start.69 = (bf16[4,256,2048]{2,1,0:T(8,128)(2,1)}, bf16[4,256,2048]{2,1,0:T(8,128)(2,1)}, u32[]{:S(2)}, u32[]{:S(2)}) collective-permute-start(bf16[4,256,2048]{2,1,0:T(8,128)(2,1)} %shard_map.347), channel_id=1, source_target_pairs={{0,4},{4,0},{8,12},{12,8},{16,20},{20,16},{24,28},{28,24},{1,5},{5... | collective-permute-start | bytes 12582920 | tf_op jit(solution)/shard_map/ppermute | solution.py:36
  347.6 45.9 %collective-permute-start.29 = (bf16[256,2048]{1,0:T(8,128)(2,1)}, bf16[256,2048]{1,0:T(8,128)(2,1)}, u32[]{:S(2)}, u32[]{:S(2)}) collective-permute-start(bf16[256,2048]{1,0:T(8,128)(2,1)} %add_convert_fusion.5), channel_id=1, source_target_pairs={{0,2},{1,3},{2,0},{3,1},{4,6},{5,7},{6,4},{7,5},{8,10},{9,11},{10,... | collective-permute-start | bytes 3145736 | tf_op jit(solution)/shard_map/ppermute | solution.py:36
  348.8 49.1 %collective-permute-start.35 = (bf16[256,2048]{1,0:T(8,128)(2,1)S(1)}, bf16[256,2048]{1,0:T(8,128)(2,1)S(1)}, u32[]{:S(2)}, u32[]{:S(2)}) collective-permute-start(bf16[256,2048]{1,0:T(8,128)(2,1)S(1)} %copy-done), channel_id=1, source_target_pairs={{0,1},{1,0},{2,3},{3,2},{4,5},{5,4},{6,7},{7,6},{8,9},{9,8},{10,11... | collective-permute-start | bytes 3145736 | tf_op jit(solution)/shard_map/ppermute | solution.py:36
  419.0 143.0 %collective-permute-start.66 = (bf16[4,256,512]{2,1,0:T(8,128)(2,1)}, bf16[4,256,512]{2,1,0:T(8,128)(2,1)S(1)}, u32[]{:S(2)}, u32[]{:S(2)}) collective-permute-start(bf16[4,256,512]{2,1,0:T(8,128)(2,1)} %shard_map.345), channel_id=1, source_target_pairs={{0,4},{4,0},{8,12},{12,8},{16,20},{20,16},{24,28},{28,24},{1,5},{5... | collective-permute-start | bytes 3145736 | tf_op jit(solution)/shard_map/ppermute | solution.py:36
  465.5 178.5 %collective-permute-start.73 = (bf16[2,256,2048]{2,1,0:T(8,128)(2,1)}, bf16[2,256,2048]{2,1,0:T(8,128)(2,1)}, u32[]{:S(2)}, u32[]{:S(2)}) collective-permute-start(bf16[2,256,2048]{2,1,0:T(8,128)(2,1)} %get-tuple-element.171), channel_id=1, source_target_pairs={{0,8},{4,12},{8,0},{12,4},{16,24},{20,28},{24,16},{28,20},{1,9},{5... | collective-permute-start | bytes 6291464 | tf_op jit(solution)/shard_map/ppermute | solution.py:36
  467.1 54.3 %collective-permute-start.42 = (bf16[4,16,2048]{2,1,0:T(8,128)(2,1)S(1)}, bf16[4,16,2048]{2,1,0:T(8,128)(2,1)S(1)}, u32[]{:S(2)}, u32[]{:S(2)}) collective-permute-start(bf16[4,16,2048]{2,1,0:T(8,128)(2,1)S(1)} %get-tuple-element.213), channel_id=1, source_target_pairs={{0,1},{1,0},{2,3},{3,2},{4,5},{5,4},{6,7},{7,6},{8,9},{9,8},{10,11... | collective-permute-start | bytes 786440 | tf_op jit(solution)/shard_map/ppermute | solution.py:36
  468.3 53.2 %collective-permute-start.44 = (bf16[4,16,2048]{2,1,0:T(8,128)(2,1)S(1)}, bf16[4,16,2048]{2,1,0:T(8,128)(2,1)S(1)}, u32[]{:S(2)}, u32[]{:S(2)}) collective-permute-start(bf16[4,16,2048]{2,1,0:T(8,128)(2,1)S(1)} %fusion.15), channel_id=1, source_target_pairs={{0,2},{1,3},{2,0},{3,1},{4,6},{5,7},{6,4},{7,5},{8,10},{9,11},{10,... | collective-permute-start | bytes 786440 | tf_op jit(solution)/shard_map/ppermute | solution.py:36
  520.7 152.5 %collective-permute-start.70 = (bf16[2,256,2048]{2,1,0:T(8,128)(2,1)}, bf16[2,256,2048]{2,1,0:T(8,128)(2,1)}, u32[]{:S(2)}, u32[]{:S(2)}) collective-permute-start(bf16[2,256,2048]{2,1,0:T(8,128)(2,1)} %get-tuple-element.169), channel_id=1, source_target_pairs={{0,8},{4,12},{8,0},{12,4},{16,24},{20,28},{24,16},{28,20},{1,9},{5... | collective-permute-start | bytes 6291464 | tf_op jit(solution)/shard_map/ppermute | solution.py:36
  561.9 59.5 %collective-permute-start.39 = (bf16[256,2048]{1,0:T(8,128)(2,1)}, bf16[256,2048]{1,0:T(8,128)(2,1)S(1)}, u32[]{:S(2)}, u32[]{:S(2)}) collective-permute-start(bf16[256,2048]{1,0:T(8,128)(2,1)} %get-tuple-element.141), channel_id=1, source_target_pairs={{0,1},{1,0},{2,3},{3,2},{4,5},{5,4},{6,7},{7,6},{8,9},{9,8},{10,11... | collective-permute-start | bytes 3145736 | tf_op jit(solution)/shard_map/ppermute | solution.py:36
  593.4 40.2 %collective-permute-start.68 = (bf16[1,256,512]{2,1,0:T(8,128)(2,1)S(1)}, bf16[1,256,512]{2,1,0:T(8,128)(2,1)}, u32[]{:S(2)}, u32[]{:S(2)}) collective-permute-start(bf16[1,256,512]{2,1,0:T(8,128)(2,1)S(1)} %slice_bitcast_fusion.12), channel_id=1, source_target_pairs={{0,16},{4,20},{8,24},{12,28},{16,0},{20,4},{24,8},{28,12},{1,17},{... | collective-permute-start | bytes 786440 | tf_op jit(solution)/shard_map/ppermute | solution.py:36
  621.4 72.2 %collective-permute-start.78 = (bf16[4,256,512]{2,1,0:T(8,128)(2,1)}, bf16[4,256,512]{2,1,0:T(8,128)(2,1)}, u32[]{:S(2)}, u32[]{:S(2)}) collective-permute-start(bf16[4,256,512]{2,1,0:T(8,128)(2,1)} %shard_map.353), channel_id=1, source_target_pairs={{0,4},{4,0},{8,12},{12,8},{16,20},{20,16},{24,28},{28,24},{1,5},{5... | collective-permute-start | bytes 3145736 | tf_op jit(solution)/shard_map/ppermute | solution.py:36
  639.7 58.7 %collective-permute-start.75 = (bf16[4,128,1024]{2,1,0:T(8,128)(2,1)}, bf16[4,128,1024]{2,1,0:T(8,128)(2,1)S(1)}, u32[]{:S(2)}, u32[]{:S(2)}) collective-permute-start(bf16[4,128,1024]{2,1,0:T(8,128)(2,1)} %shard_map.351), channel_id=1, source_target_pairs={{0,4},{4,0},{8,12},{12,8},{16,20},{20,16},{24,28},{28,24},{1,5},{5... | collective-permute-start | bytes 3145736 | tf_op jit(solution)/shard_map/ppermute | solution.py:36
  641.3 47.4 %collective-permute-start.51 = (bf16[2,64,1024]{2,1,0:T(8,128)(2,1)}, bf16[2,64,1024]{2,1,0:T(8,128)(2,1)}, u32[]{:S(2)}, u32[]{:S(2)}) collective-permute-start(bf16[2,64,1024]{2,1,0:T(8,128)(2,1)} %get-tuple-element.210), channel_id=1, source_target_pairs={{0,1},{1,0},{2,3},{3,2},{4,5},{5,4},{6,7},{7,6},{8,9},{9,8},{10,11... | collective-permute-start | bytes 786440 | tf_op jit(solution)/shard_map/ppermute | solution.py:36
  688.7 68.4 %collective-permute-start.63 = (bf16[4,256,1536]{2,1,0:T(8,128)(2,1)}, bf16[4,256,1536]{2,1,0:T(8,128)(2,1)}, u32[]{:S(2)}, u32[]{:S(2)}) collective-permute-start(bf16[4,256,1536]{2,1,0:T(8,128)(2,1)} %shard_map.343), channel_id=1, source_target_pairs={{0,4},{4,0},{8,12},{12,8},{16,20},{20,16},{24,28},{28,24},{1,5},{5... | collective-permute-start | bytes 9437192 | tf_op jit(solution)/shard_map/ppermute | solution.py:36
  693.6 77.4 %collective-permute-start.74 = (bf16[1,256,2048]{2,1,0:T(8,128)(2,1)S(1)}, bf16[1,256,2048]{2,1,0:T(8,128)(2,1)}, u32[]{:S(2)}, u32[]{:S(2)}) collective-permute-start(bf16[1,256,2048]{2,1,0:T(8,128)(2,1)S(1)} %slice_bitcast_fusion), channel_id=1, source_target_pairs={{0,16},{4,20},{8,24},{12,28},{16,0},{20,4},{24,8},{28,12},{1,17},{... | collective-permute-start | bytes 3145736 | tf_op jit(solution)/shard_map/ppermute | solution.py:36
  698.4 136.5 %collective-permute-start.71 = (bf16[1,256,2048]{2,1,0:T(8,128)(2,1)}, bf16[1,256,2048]{2,1,0:T(8,128)(2,1)}, u32[]{:S(2)}, u32[]{:S(2)}) collective-permute-start(bf16[1,256,2048]{2,1,0:T(8,128)(2,1)} %slice_bitcast_fusion.2), channel_id=1, source_target_pairs={{0,16},{4,20},{8,24},{12,28},{16,0},{20,4},{24,8},{28,12},{1,17},{... | collective-permute-start | bytes 3145736 | tf_op jit(solution)/shard_map/ppermute | solution.py:36
  706.7 65.9 %collective-permute-start.79 = (bf16[2,256,512]{2,1,0:T(8,128)(2,1)}, bf16[2,256,512]{2,1,0:T(8,128)(2,1)S(1)}, u32[]{:S(2)}, u32[]{:S(2)}) collective-permute-start(bf16[2,256,512]{2,1,0:T(8,128)(2,1)} %get-tuple-element.177), channel_id=1, source_target_pairs={{0,8},{4,12},{8,0},{12,4},{16,24},{20,28},{24,16},{28,20},{1,9},{5... | collective-permute-start | bytes 1572872 | tf_op jit(solution)/shard_map/ppermute | solution.py:36
  708.3 70.0 %collective-permute-start.76 = (bf16[2,128,1024]{2,1,0:T(8,128)(2,1)}, bf16[2,128,1024]{2,1,0:T(8,128)(2,1)S(1)}, u32[]{:S(2)}, u32[]{:S(2)}) collective-permute-start(bf16[2,128,1024]{2,1,0:T(8,128)(2,1)} %get-tuple-element.174), channel_id=1, source_target_pairs={{0,8},{4,12},{8,0},{12,4},{16,24},{20,28},{24,16},{28,20},{1,9},{5... | collective-permute-start | bytes 1572872 | tf_op jit(solution)/shard_map/ppermute | solution.py:36
  766.4 65.9 %collective-permute-start.64 = (bf16[2,256,1536]{2,1,0:T(8,128)(2,1)}, bf16[2,256,1536]{2,1,0:T(8,128)(2,1)S(1)}, u32[]{:S(2)}, u32[]{:S(2)}) collective-permute-start(bf16[2,256,1536]{2,1,0:T(8,128)(2,1)} %get-tuple-element.159), channel_id=1, source_target_pairs={{0,8},{4,12},{8,0},{12,4},{16,24},{20,28},{24,16},{28,20},{1,9},{5... | collective-permute-start | bytes 4718600 | tf_op jit(solution)/shard_map/ppermute | solution.py:36
  774.7 64.9 %collective-permute-start.80 = (bf16[1,256,512]{2,1,0:T(8,128)(2,1)S(1)}, bf16[1,256,512]{2,1,0:T(8,128)(2,1)}, u32[]{:S(2)}, u32[]{:S(2)}) collective-permute-start(bf16[1,256,512]{2,1,0:T(8,128)(2,1)S(1)} %slice_bitcast_fusion.8), channel_id=1, source_target_pairs={{0,16},{4,20},{8,24},{12,28},{16,0},{20,4},{24,8},{28,12},{1,17},{... | collective-permute-start | bytes 786440 | tf_op jit(solution)/shard_map/ppermute | solution.py:36
  781.1 60.6 %collective-permute-start.77 = (bf16[1,128,1024]{2,1,0:T(8,128)(2,1)}, bf16[1,128,1024]{2,1,0:T(8,128)(2,1)}, u32[]{:S(2)}, u32[]{:S(2)}) collective-permute-start(bf16[1,128,1024]{2,1,0:T(8,128)(2,1)} %slice_bitcast_fusion.10), channel_id=1, source_target_pairs={{0,16},{4,20},{8,24},{12,28},{16,0},{20,4},{24,8},{28,12},{1,17},{... | collective-permute-start | bytes 786440 | tf_op jit(solution)/shard_map/ppermute | solution.py:36
  (120 other events, 1459.5 us)

commit v2 on v1

v2 whole, which is shorter than its diff:
```python
import functools

import jax
import jax.numpy as jnp
from jax import lax
from jax.experimental import pallas as pl
from jax.experimental.pallas import tpu as pltpu
from jax.sharding import PartitionSpec as P

HEAD = 64
LANES = 128
EPS = 1e-05
NEG = -1e30
XPOS_BASE = 512.0
BF = jnp.bfloat16
F32 = jnp.float32
ROWS_BY_ROWS = (((1,), (1,)), ((), ()))
PLAIN = (((1,), (0,)), ((), ()))
OVER_ROWS = (((0,), (0,)), ((), ()))
KIND, PART, GROUP, REAL, POS, SOURCE, BLOCK, RANK = 0, 1, 2, 4, 8, 12, 16, 32
VMEM_BYTES = 28 * 1024 * 1024


def dot(left, right, form=PLAIN):
    return lax.dot_general(left, right, form, preferred_element_type=F32)


def dot_exact(left, right, form=ROWS_BY_ROWS):
    return lax.dot_general(
        left, right, form, precision=lax.Precision.HIGHEST, preferred_element_type=F32
    )


def swap(values, axis, bit):
    size = lax.axis_size(axis)
    return lax.ppermute(values, axis, [(i, i ^ bit) for i in range(size)])


def bits_of(size):
    return [1 << i for i in range(size.bit_length() - 1)]


def gather_rel(values):
    size = lax.axis_size("mp")
    pieces = {0: values}
    for bit in reversed(bits_of(size)):
        pieces[bit] = swap(values, "mp", bit)
    for j in range(size):
        if j not in pieces:
            low = j & -j
            pieces[j] = swap(pieces[j ^ low], "mp", low)
    return [pieces[j] for j in range(size)]


def add_low(first, second):
    return (first.astype(F32) + second.astype(F32)).astype(BF)


def scatter_pairs(even, odd):
    near = add_low(even, swap(odd, "mp", 1))
    return near[0], swap(near[1], "mp", 2), near


def sum_pairs(even, odd):
    own, far, _ = scatter_pairs(even, odd)
    return own.astype(F32) + far.astype(F32)


def pick(values, indices):
    return jnp.stack([lax.dynamic_index_in_dim(values, i, 0, keepdims=False) for i in indices])


def by_mp(values):
    me = lax.axis_index("mp")
    return pick(values, [me ^ j for j in range(lax.axis_size("mp"))])


def halve(values, axis):
    return (
        lax.index_in_dim(values, 0, axis, keepdims=False),
        lax.index_in_dim(values, 1, axis, keepdims=False),
    )


def scatter_dp(values, bits, last):
    for bit in bits:
        values = values.reshape((-1, 2) + values.shape[1:])
        keep, send = halve(values, 1)
        got = swap(send, "dp", bit)
        total = keep.astype(F32) + got.astype(F32)
        values = total.astype(last if bit == bits[-1] else BF)
    return values[0]


class Order:
    mark = None
    channel = 0


def call(body, meta, grid, ins, outs, scratch=(), aliases=None, remote=False, after=(), cost=1):
    arrays, specs = [], []
    for item in ins:
        arrays.append(item[0])
        if len(item) == 1:
            dims = item[0].ndim
            specs.append(
                pl.BlockSpec(
                    item[0].shape,
                    lambda *_, dims=dims: (0,) * dims,
                    pipeline_mode=pl.Buffered(1),
                )
            )
        elif item[1] is None:
            specs.append(pl.BlockSpec(memory_space=pl.ANY))
        else:
            specs.append(pl.BlockSpec(item[1], item[2]))
    shapes, out_specs = [], []
    for shape, dtype, block, index in list(outs) + [((8, LANES), F32, None, None)]:
        shapes.append(jax.ShapeDtypeStruct(shape, dtype))
        if index == "any":
            out_specs.append(pl.BlockSpec(memory_space=pl.ANY))
        elif block is None:
            dims = len(shape)
            out_specs.append(pl.BlockSpec(shape, lambda *_, dims=dims: (0,) * dims))
        else:
            out_specs.append(pl.BlockSpec(block, index))
    count, after = len(ins), list(after)
    if Order.mark is not None:
        after.append(Order.mark)
    specs += [pl.BlockSpec(memory_space=pl.ANY)] * len(after)

    params = pltpu.CompilerParams(vmem_limit_bytes=VMEM_BYTES)
    if remote:
        Order.channel += 1
        params = pltpu.CompilerParams(
            vmem_limit_bytes=VMEM_BYTES, collective_id=Order.channel, has_side_effects=True
        )

    def marked(meta_ref, *refs):
        refs = refs[:count] + refs[count + len(after) :]
        place = count + len(outs)
        refs[place][...] = jnp.zeros((8, LANES), F32)
        body(meta_ref, *refs[:place], *refs[place + 1 :])

    result = pl.pallas_call(
        marked,
        out_shape=shapes,
        grid_spec=pltpu.PrefetchScalarGridSpec(
            num_scalar_prefetch=1,
            grid=grid,
            in_specs=specs,
            out_specs=out_specs,
            scratch_shapes=list(scratch),
        ),
        input_output_aliases=aliases or {},
        compiler_params=params,
        cost_estimate=pl.CostEstimate(
            flops=cost * 40000000, bytes_accessed=1024, transcendentals=0
        ),
        name=getattr(body, "func", body).__name__,
    )(meta, *arrays, *after)
    Order.mark = result[-1]
    return result[:-1]


def norm_parts(values):
    width = values.shape[-1]
    mean = jnp.sum(values, axis=-1, keepdims=True) / width
    square = jnp.sum(values * values, axis=-1, keepdims=True) / width
    inv_std = lax.rsqrt(square - mean * mean + EPS)
    return (values - mean) * inv_std, inv_std


def norm_back(upstream, normed, inv_std, gain):
    width = upstream.shape[-1]
    scaled = upstream * gain
    first = jnp.sum(scaled, axis=-1, keepdims=True) / width
    second = jnp.sum(scaled * normed, axis=-1, keepdims=True) / width
    return inv_std * (scaled - first - normed * second)


def columns_of(rows):
    count, length = rows.shape
    full = jnp.concatenate([rows, jnp.zeros((LANES - count, length), F32)], axis=0)
    return full.T


def lane_sums(values):
    total = values[:, :LANES]
    for start in range(LANES, values.shape[1], LANES):
        total = total + values[:, start : start + LANES]
    return total


def rows_from(partials):
    return dot_exact(jnp.ones((8, LANES), F32), partials)


def two_rows(first, second):
    row = lax.broadcasted_iota(jnp.int32, first.shape, 0)
    return jnp.where(row == 0, first, jnp.where(row == 1, second, 0.0))


def meta_body(count_ref, seq_ref, slot_ref, kind_ref, me_ref, out_ref, *, image_local, slots, images):
    me_m, me_d = me_ref[0], me_ref[1]

    def clear(i, _):
        out_ref[i] = 0
        return 0

    lax.fori_loop(0, BLOCK, clear, 0)

    def absent(i, _):
        out_ref[BLOCK + i] = -1
        return 0

    lax.fori_loop(0, RANK - BLOCK + images, absent, 0)
    out_ref[KIND] = kind_ref[me_d]
    out_ref[PART] = me_m
    out_ref[GROUP] = me_d
    for s in range(slots):
        out_ref[POS + s] = slot_ref[me_d, s]

    def one(i, found):
        owner = i // image_local
        inside = i - owner * image_local
        here = jnp.logical_and(inside < count_ref[owner], seq_ref[i] == me_d)
        rank = jnp.minimum(found, slots - 1)

        @pl.when(here)
        def _():
            out_ref[REAL + rank] = 1
            out_ref[SOURCE + rank] = (owner ^ me_d) * image_local + inside
            out_ref[BLOCK + slot_ref[me_d, rank]] = rank
            out_ref[RANK + i] = rank

        return found + here.astype(jnp.int32)

    lax.fori_loop(0, images, one, jnp.int32(0))


def make_meta(owner_count, image_seq, slot_block, seq_kind, image_local):
    me = jnp.stack([lax.axis_index("mp"), lax.axis_index("dp")]).astype(jnp.int32)
    images = image_seq.shape[0]
    smem = pl.BlockSpec(memory_space=pltpu.SMEM)
    return pl.pallas_call(
        functools.partial(
            meta_body, image_local=image_local, slots=slot_block.shape[1], images=images
        ),
        out_shape=jax.ShapeDtypeStruct((RANK + images,), jnp.int32),
        in_specs=[smem] * 5,
        out_specs=smem,
    )(owner_count, image_seq, slot_block, seq_kind, me)


def other_of(me, j):
    return [me, me + 1 - 2 * (me % 2), (me + 2) % 4, 3 - me][j]


def pair_sums(terms, out_refs, scratch):
    sent, came, kept, send_sem, recv_sem = scratch
    step, steps = pl.program_id(0), pl.num_programs(0)
    partner = {"mp": other_of(lax.axis_index("mp"), 1)}

    @pl.when(step == 0)
    def _():
        barrier = pltpu.get_barrier_semaphore()
        pl.semaphore_signal(barrier, inc=1, device_id=partner)
        pl.semaphore_wait(barrier, 1)

    def move(n, place):
        return pltpu.make_async_remote_copy(
            src_ref=sent.at[n, place],
            dst_ref=came.at[n, place],
            send_sem=send_sem.at[n, place],
            recv_sem=recv_sem.at[n, place],
            device_id=partner,
        )

    for n, (mine, theirs) in enumerate(terms):
        sent[n, step] = theirs().astype(BF)
        move(n, step).start()
        kept[n, step] = mine()

    @pl.when(step == steps - 1)
    def _():
        tile = sent.shape[-1]
        for n, out_ref in enumerate(out_refs):
            for place in range(sent.shape[1]):
                move(n, place).wait()
                total = kept[n, place] + came[n, place].astype(F32)
                out_ref[:, place * tile : (place + 1) * tile] = total.astype(BF)


def flipped(me, bit):
    return me + bit * (1 - 2 * ((me // bit) % 2))


def exchange(meta, *items):
    places = sorted({(axis, bit) for _, axis, bit in items})
    count = len(items)

    def body(meta_ref, *refs):
        sources, targets, (send_sem, recv_sem) = refs[:count], refs[count : 2 * count], refs[-2:]

        def partner(axis, bit):
            me = lax.axis_index(axis)
            for one in bits_of(lax.axis_size(axis)):
                if bit & one:
                    me = flipped(me, one)
            return {axis: me}

        barrier = pltpu.get_barrier_semaphore()
        for axis, bit in places:
            pl.semaphore_signal(barrier, inc=1, device_id=partner(axis, bit))
        pl.semaphore_wait(barrier, len(places))
        copies = [
            pltpu.make_async_remote_copy(
                src_ref=sources[n],
                dst_ref=targets[n],
                send_sem=send_sem.at[n],
                recv_sem=recv_sem.at[n],
                device_id=partner(axis, bit),
            )
            for n, (_, axis, bit) in enumerate(items)
        ]
        for copy in copies:
            copy.start()
        for copy in copies:
            copy.wait()

    return call(
        body,
        meta,
        (1,),
        [(array, None) for array, _, _ in items],
        [(array.shape, array.dtype, None, "any") for array, _, _ in items],
        scratch=[pltpu.SemaphoreType.DMA((count,)), pltpu.SemaphoreType.DMA((count,))],
        remote=True,
    )


def spread_stats(meta, values):
    others = range(1, lax.axis_size("mp"))
    return [values] + list(exchange(meta, *[(values, "mp", b) for b in others]))


def gather_now(meta, values):
    far, near = exchange(meta, (values, "mp", 2), (values, "mp", 1))
    return [values, near, far, exchange(meta, (far, "mp", 1))[0]]


def scatter_now(meta, even, odd):
    near = add_low(even, exchange(meta, (odd, "mp", 1))[0])
    return near[0], exchange(meta, (near[1], "mp", 2))[0]


def pair_scratch(count, steps, rows, tile):
    shape = (count, steps, rows, tile)
    return [
        pltpu.VMEM(shape, BF),
        pltpu.VMEM(shape, BF),
        pltpu.VMEM(shape, F32),
        pltpu.SemaphoreType.DMA((count, steps)),
        pltpu.SemaphoreType.DMA((count, steps)),
    ]


def kind_of(meta, table_ref):
    return table_ref[pl.ds(meta[KIND], 1), :]


def text_body(meta, text_ref, table_ref, gain_ref, out_ref):
    mixed = text_ref[...].astype(F32) + kind_of(meta, table_ref)
    out_ref[...] = (norm_parts(mixed)[0] * gain_ref[...]).astype(BF)


def rotated(values, cosine, sine):
    width = values.shape[1]
    lane = lax.broadcasted_iota(jnp.int32, values.shape, 1)
    other = jnp.where(
        lane % HEAD < HEAD // 2,
        pltpu.roll(values, width - HEAD // 2, 1),
        pltpu.roll(values, HEAD // 2, 1),
    )
    repeat = width // LANES
    cosine = jnp.concatenate([cosine] * repeat, axis=1)
    sine = jnp.concatenate([sine] * repeat, axis=1)
    return values * cosine + other * sine


def qkv_body(meta, near_ref, far_ref, weight_ref, turn_ref, *refs, which):
    out_ref, in_ref = refs[-2:]
    rows = near_ref.shape[0]
    for n, ref in enumerate((near_ref, far_ref)):
        at = pl.ds(pl.multiple_of(((meta[PART] ^ (which + n)) % 2) * rows, rows), rows)
        product = dot(ref[...], weight_ref[0])
        out_ref[at, :] = rotated(product, turn_ref[0, 0, at, :], turn_ref[0, 1, at, :]).astype(BF)
        in_ref[at, :] = ref[...]


def project(meta, pieces, weight, turn, before, which, after=()):
    rows, depth = pieces[0].shape
    width = weight.shape[2]
    length = rows * lax.axis_size("mp")
    pair = lambda m: (m[PART] ^ which) // 2
    ins = [(pieces[0],), (pieces[1],), (weight, (1, depth, width), lambda i, m: (i, 0, 0))]
    ins.append((turn, (1, 2, 2 * rows, LANES), lambda i, m: (i, 0, pair(m), 0)))
    aliases = {}
    if before is not None:
        for n, array in enumerate(before):
            ins.append((array, None))
            aliases[5 + n] = n
    return call(
        functools.partial(qkv_body, which=which),
        meta,
        (3,),
        ins,
        [
            ((length, 3 * width), BF, (2 * rows, width), lambda i, m: (pair(m), i)),
            ((length, depth), BF, (2 * rows, depth), lambda i, m: (pair(m), 0)),
        ],
        aliases=aliases,
        after=after,
    )


def slot_body(meta, *refs, mp, slots, latent):
    pieces = refs[:mp]
    table_ref, gain_ref, weight_ref, turn_ref, qkv_in, x_in = refs[mp : mp + 6]
    qkv_ref, x_ref, slots_ref, rows_ref, new_ref, norm_ref = refs[mp + 6 :]
    step = pl.program_id(0)
    part = latent // mp

    @pl.when(step == 0)
    def _():
        for j in range(mp):
            place = pl.multiple_of((meta[PART] ^ j) * part, part)
            for s in range(slots):
                rows_ref[s, pl.ds(place, part), :] = pieces[j][s].astype(F32)
        mixed = rows_ref[...].reshape(slots * latent, -1)
        slots_ref[...] = mixed.astype(BF).reshape(slots_ref.shape)
        mixed = mixed + kind_of(meta, table_ref)
        normed = (norm_parts(mixed)[0] * gain_ref[...]).astype(BF)
        norm_ref[...] = normed.reshape(norm_ref.shape)

    @pl.when(step < 3)
    def _():
        product = dot(norm_ref[...].reshape(slots * latent, -1), weight_ref[0])
        new_ref[step] = product.reshape(new_ref.shape[1:])

    @pl.when(step >= 3)
    def _():
        slot = step - 3
        real = meta[REAL + slot] > 0
        width = new_ref.shape[-1]
        for c in range(3):
            at = slice(c * width, (c + 1) * width)
            value = rotated(new_ref[c, slot], turn_ref[c, 0], turn_ref[c, 1]).astype(BF)
            qkv_ref[:, at] = jnp.where(real, value, qkv_in[:, at])
        x_ref[...] = jnp.where(real, norm_ref[slot], x_in[...])


def turn_tables(length):
    positions = jnp.arange(length, dtype=F32)[:, None]
    lane = jnp.arange(LANES)
    ladder = (lane % (HEAD // 2)).astype(F32)
    angle = positions * jnp.power(10000.0, -2.0 * ladder / HEAD)[None, :]
    decay = (2.0 * ladder + 0.4 * HEAD) / (1.4 * HEAD)
    power = (positions - length // 2) / XPOS_BASE
    sign = jnp.where(lane % HEAD < HEAD // 2, -1.0, 1.0)[None, :]
    cosine, sine = jnp.cos(angle), jnp.sin(angle) * sign
    up = jnp.power(decay[None, :], power)
    down = jnp.power(decay[None, :], -power)
    one, zero = jnp.ones_like(cosine), jnp.zeros_like(cosine)
    return jnp.stack(
        [
            jnp.stack([cosine * up, sine * up]),
            jnp.stack([cosine * down, sine * down]),
            jnp.stack([one, zero]),
        ]
    )


def pool_shares_of(query, keys, head):
    lane = lax.broadcasted_iota(jnp.int32, query.shape, 1)
    masked = jnp.where(lane // HEAD == head, query, jnp.zeros_like(query))
    scores = dot(masked, keys, ROWS_BY_ROWS) * 0.125
    top = jnp.max(scores, axis=-1, keepdims=True)
    weights = jnp.exp(scores - top)
    return weights / jnp.sum(weights, axis=-1, keepdims=True)


def pool_body(
    meta, clip_ref, key_w, value_w, query_ref, key_ref, value_ref, pool_ref, *, images
):
    clip = clip_ref[...]
    key_ref[...] = dot(clip, key_w[...]).astype(BF)
    value_ref[...] = dot(clip, value_w[...]).astype(BF)
    patches = clip.shape[0] // images
    latent = query_ref.shape[0]
    for i in range(images):
        for pair in range(query_ref.shape[1] // LANES):
            lanes = slice(pair * LANES, (pair + 1) * LANES)
            rows = slice(i * patches, (i + 1) * patches)
            query, keys, values = query_ref[:, lanes], key_ref[rows, lanes], value_ref[rows, lanes]
            lane = lax.broadcasted_iota(jnp.int32, query.shape, 1)
            heads = [
                dot(pool_shares_of(query, keys, h).astype(BF), values) for h in range(2)
            ]
            pool_ref[i * latent : (i + 1) * latent, lanes] = jnp.where(
                lane < HEAD, heads[0], heads[1]
            ).astype(BF)


def pooled_body(meta, *refs, slots, mp):
    pieces, out_w, even_ref, odd_ref, scratch = refs[:slots], refs[slots], *refs[slots + 1 :]
    rows = jnp.concatenate([p[...] for p in pieces], axis=0)
    scratch[...] = dot(rows, out_w[...])
    latent = pieces[0].shape[0]
    part = latent // mp
    for j in range(mp):
        for s in range(slots):
            start = pl.multiple_of(s * latent + (meta[PART] ^ j) * part, part)
            (odd_ref if j % 2 else even_ref)[j // 2, s] = scratch[pl.ds(start, part), :].astype(BF)


def copy_body(meta, in_ref, out_ref):
    out_ref[...] = in_ref[...]


def head_lanes(pair, width):
    return [
        pl.ds(pl.multiple_of(c * width + pair * LANES, LANES), LANES) for c in range(3)
    ]


def attend_body(meta, qkv_ref, out_ref, lse_ref, stat_ref, first, second, lse, *, block):
    length, width = out_ref.shape
    first[...] = jnp.zeros_like(first)
    second[...] = jnp.zeros_like(second)

    def pair(hp, _):
        lanes, k_lanes, v_lanes = head_lanes(hp, width)
        keys, values = qkv_ref[:, k_lanes], qkv_ref[:, v_lanes]
        lane = lax.broadcasted_iota(jnp.int32, (block, LANES), 1)
        row = lax.broadcasted_iota(jnp.int32, (block, block), 0)
        col = lax.broadcasted_iota(jnp.int32, (block, block), 1)
        for b in range(length // block):
            rows = slice(b * block, (b + 1) * block)
            end = (b + 1) * block
            query = qkv_ref[rows, lanes]
            outs = []
            for h in range(2):
                masked = jnp.where(lane // HEAD == h, query, jnp.zeros_like(query))
                scores = dot(masked, keys[:end], ROWS_BY_ROWS) * 0.125
                edge = jnp.where(row >= col, scores[:, b * block :], NEG)
                scores = edge if b == 0 else jnp.concatenate([scores[:, : b * block], edge], axis=1)
                top = jnp.max(scores, axis=-1, keepdims=True)
                weights = jnp.exp(scores - top)
                total = jnp.sum(weights, axis=-1, keepdims=True)
                outs.append(dot(weights.astype(BF), values[:end]) / total)
                lse[rows, :] = jnp.where(lane == 2 * hp + h, top + jnp.log(total), lse[rows, :])
            out = jnp.where(lane < HEAD, outs[0], outs[1])
            first[rows, :] += out
            second[rows, :] += out * out
            out_ref[rows, lanes] = out.astype(BF)
        return 0

    lax.fori_loop(0, width // LANES, pair, 0)
    lse_ref[...] = lse[...].T[: lse_ref.shape[0]]
    stat_ref[...] = two_rows(rows_from(first[...]), rows_from(second[...]))


def total_columns(stats):
    total = stats[0][...]
    for other in stats[1:]:
        total = total + other[...]
    return columns_of(total)


def stat_norm(values, columns, at, width):
    mean = columns[:, at : at + 1] / width
    square = columns[:, at + 1 : at + 2] / width
    inv_std = lax.rsqrt(square - mean * mean + EPS)
    return (values - mean) * inv_std, inv_std


def mid_body(meta, att_ref, gain_ref, *refs, mp, width):
    normed, _ = stat_norm(att_ref[...].astype(F32), total_columns(refs[:mp]), 0, width)
    refs[mp][...] = (normed * gain_ref[...]).astype(BF)


def out_body(meta, rows_ref, weight_ref, out_ref, *scratch):
    rows = out_ref.shape[0]
    pair_sums(
        [
            (
                lambda: dot(rows_ref[:rows, :], weight_ref[...]),
                lambda: dot(rows_ref[rows:, :], weight_ref[...]),
            )
        ],
        [out_ref],
        scratch,
    )


def back_body(meta, rows_ref, weight_ref, out_ref, *scratch):
    rows = out_ref.shape[0]
    pair_sums(
        [
            (
                lambda: dot(rows_ref[:rows, :], weight_ref[...], ROWS_BY_ROWS),
                lambda: dot(rows_ref[rows:, :], weight_ref[...], ROWS_BY_ROWS),
            )
        ],
        [out_ref],
        scratch,
    )


def after_body(meta, own_ref, far_ref, text_ref, slots_ref, table_ref, gain_ref, after_ref, low_ref):
    mixed = mixed_rows(meta, text_ref, slots_ref, table_ref)
    after = mixed + (own_ref[...].astype(F32) + far_ref[...].astype(F32))
    after_ref[...] = after
    low_ref[...] = (norm_parts(after)[0] * gain_ref[...]).astype(BF)


def mixed_rows(meta, text_ref, slots_ref, table_ref):
    block = meta[PART] * pl.num_programs(0) + pl.program_id(0)
    filled = meta[BLOCK + block] >= 0
    return (
        jnp.where(filled, slots_ref[0].astype(F32), text_ref[...].astype(F32))
        + kind_of(meta, table_ref)
    )


def slot_index(blocks):
    return lambda i, m: (jnp.maximum(m[BLOCK + m[PART] * blocks + i], 0), 0, 0)


def times_rows_body(meta, *refs, count):
    pieces, weight_ref, outs = refs[:count], refs[count], refs[-count:]
    for piece, out_ref in zip(pieces, outs):
        out_ref[...] = dot(piece[...], weight_ref[...], ROWS_BY_ROWS).astype(out_ref.dtype)


def up_body(meta, a_ref, b_ref, weight_ref, dup_a, dup_b, gain_ref, *refs):
    act_ref, slope_ref, stat_ref = refs[-7:-4]
    sums = refs[-4:]
    step = pl.program_id(0)
    rows = a_ref.shape[0]

    @pl.when(step == 0)
    def _():
        for ref in sums:
            ref[...] = jnp.zeros_like(ref)

    for n, (ref, dup_ref) in enumerate(((a_ref, dup_a), (b_ref, dup_b))):
        here = slice(n * rows, (n + 1) * rows)
        pre = dot(ref[...], weight_ref[...])
        share = 0.5 + 0.5 * lax.erf(pre * (0.5**0.5))
        density = jnp.exp(pre * pre * -0.5) * ((2.0 * jnp.pi) ** -0.5)
        act = pre * share
        act_ref[here, :] = act.astype(BF)
        slope_ref[here, :] = (share + pre * density).astype(BF)
        scaled = dup_ref[...].astype(F32) * gain_ref[...]
        for ref_sum, term in zip(sums, (act, act * act, scaled, scaled * act)):
            ref_sum[here, :] += lane_sums(term)

    @pl.when(step == pl.num_programs(0) - 1)
    def _():
        rows_of = [rows_from(ref_sum[...]) for ref_sum in sums]
        row = lax.broadcasted_iota(jnp.int32, rows_of[0].shape, 0)
        total = jnp.zeros_like(rows_of[0])
        for n, value in enumerate(rows_of):
            total = jnp.where(row == n, value, total)
        stat_ref[...] = total


def spread_body(meta, act_ref, slope_ref, dup_0, dup_1, dup_2, dup_3, gain_ref, *refs, mp, width):
    stats = refs[:mp]
    pre_ref, low_ref, grad_ref = refs[mp:]
    columns = total_columns(stats)
    act = act_ref[...].astype(F32)
    normed, inv_std = stat_norm(act, columns, 0, width)
    gain = gain_ref[...]
    low_ref[...] = (normed * gain).astype(BF)
    step = pl.program_id(0) // (pl.num_programs(0) // 4)
    upstream = jnp.where(
        step < 2,
        jnp.where(step == 0, dup_0[...], dup_1[...]),
        jnp.where(step == 2, dup_2[...], dup_3[...]),
    ).astype(F32)
    first = columns[:, 2:3] / width
    mean = columns[:, 0:1] / width
    second = (columns[:, 3:4] - mean * columns[:, 2:3]) * inv_std / width
    d_act = inv_std * (upstream * gain - first - normed * second)
    pre_ref[...] = (d_act * slope_ref[...].astype(F32)).astype(BF)
    add_rows(grad_ref, upstream * normed)


def down_body(meta, low_ref, weight_ref, near_ref, far_ref, *scratch):
    rows = near_ref.shape[0]

    def term(j):
        return lambda: dot(low_ref[j * rows : (j + 1) * rows, :], weight_ref[...])

    pair_sums([(term(2), term(3)), (term(0), term(1))], [far_ref, near_ref], scratch)


def sum_body(meta, first_ref, second_ref, third_ref, out_ref):
    out_ref[...] = first_ref[...] + (second_ref[...].astype(F32) + third_ref[...].astype(F32))


def ffn_back_body(meta, own_ref, far_ref, after_ref, cot_ref, gain_ref, out_ref, low_ref, grad_ref):
    upstream = own_ref[...].astype(F32) + far_ref[...].astype(F32)
    normed, inv_std = norm_parts(after_ref[...])
    d_after = cot_ref[...].astype(F32) + norm_back(upstream, normed, inv_std, gain_ref[...])
    out_ref[...] = d_after
    low_ref[...] = d_after.astype(BF)
    add_rows(grad_ref, upstream * normed)


def add_rows(ref, values):
    total = jnp.sum(values, axis=0, keepdims=True)

    @pl.when(pl.program_id(0) == 0)
    def _():
        ref[...] = total

    @pl.when(pl.program_id(0) != 0)
    def _():
        ref[...] += total


def d_mid_body(meta, *refs, mp, width):
    pieces, weight_ref, gain_ref, att_ref = refs[:2], refs[2], refs[3], refs[4]
    stats = refs[5 : 5 + mp]
    out_ref, stat_ref, grad_ref = refs[-3:]
    rows = jnp.where(pl.program_id(0) == 0, pieces[0][...], pieces[1][...])
    d_mid = dot(rows, weight_ref[...], ROWS_BY_ROWS)
    out_ref[...] = d_mid.astype(BF)
    normed, _ = stat_norm(att_ref[...].astype(F32), total_columns(stats), 0, width)
    scaled = d_mid * gain_ref[...]
    add_rows(grad_ref, d_mid * normed)
    stat_ref[...] = two_rows(
        rows_from(lane_sums(scaled)), rows_from(lane_sums(scaled * normed))
    )


def attend_back_body(
    meta, qkv_ref, att_ref, dmid_ref, lse_ref, gain_ref, turn_ref, *refs, mp, width, block
):
    stats, more = refs[:mp], refs[mp : 2 * mp]
    out_ref, d_att, dq, dk, dv = refs[2 * mp :]
    length, wide = att_ref.shape
    columns = total_columns(stats)
    normed, inv_std = stat_norm(att_ref[...].astype(F32), columns, 0, width)
    sums = total_columns(more)
    scaled = dmid_ref[...].astype(F32) * gain_ref[...]
    d_att[...] = (
        inv_std * (scaled - sums[:, 0:1] / width - normed * (sums[:, 1:2] / width))
    ).astype(BF)

    def pair(hp, _):
        lanes, k_lanes, v_lanes = head_lanes(hp, wide)
        keys, values = qkv_ref[:, k_lanes], qkv_ref[:, v_lanes]
        lane = lax.broadcasted_iota(jnp.int32, (block, LANES), 1)
        row = lax.broadcasted_iota(jnp.int32, (block, block), 0)
        col = lax.broadcasted_iota(jnp.int32, (block, block), 1)
        dk[...] = jnp.zeros_like(dk)
        dv[...] = jnp.zeros_like(dv)
        both = d_att[:, lanes].astype(F32) * att_ref[:, lanes].astype(F32)
        side = lax.broadcasted_iota(jnp.int32, (8, LANES), 1) // HEAD
        pick_head = lax.broadcasted_iota(jnp.int32, (8, LANES), 0) == side
        inner = dot_exact(pick_head.astype(F32), both)
        for b in range(length // block):
            rows = slice(b * block, (b + 1) * block)
            end = (b + 1) * block
            query, grad = qkv_ref[rows, lanes], d_att[rows, lanes]
            d_query = jnp.zeros((block, LANES), F32)
            for h in range(2):
                keep = lane // HEAD == h
                q_one = jnp.where(keep, query, jnp.zeros_like(query))
                g_one = jnp.where(keep, grad, jnp.zeros_like(grad))
                scores = dot(keys[:end], q_one, ROWS_BY_ROWS) * 0.125
                shares = jnp.exp(scores - lse_ref[pl.ds(2 * hp + h, 1), rows])
                edge = jnp.where(col >= row, shares[b * block :], 0.0)
                shares = edge if b == 0 else jnp.concatenate([shares[: b * block], edge], axis=0)
                d_shares = dot(values[:end], g_one, ROWS_BY_ROWS)
                d_scores = (shares * (d_shares - inner[h : h + 1, rows])).astype(BF)
                dv[:end, :] += dot(shares.astype(BF), g_one)
                dk[:end, :] += dot(d_scores, q_one)
                turned = dot(d_scores, keys[:end], OVER_ROWS)
                d_query = jnp.where(keep, turned, d_query)
            dq[rows, :] = d_query
        out_ref[:, lanes] = rotated(
            dq[...] * 0.125, turn_ref[0, 0], -turn_ref[0, 1]
        ).astype(BF)
        out_ref[:, k_lanes] = rotated(
            dk[...] * 0.125, turn_ref[1, 0], -turn_ref[1, 1]
        ).astype(BF)
        out_ref[:, v_lanes] = dv[...].astype(BF)
        return 0

    lax.fori_loop(0, wide // LANES, pair, 0)


def three_dots(rows, weight_ref):
    width = weight_ref.shape[2]
    total = None
    for c in range(3):
        term = dot(rows[:, c * width : (c + 1) * width], weight_ref[c], ROWS_BY_ROWS)
        total = term if total is None else total + term
    return total


def slot_back_body(meta, *refs, slots, mp):
    pieces, weight_ref, even_ref, odd_ref, scratch = refs[:slots], refs[slots], *refs[-3:]
    rows = jnp.concatenate([p[...] for p in pieces], axis=0)
    scratch[...] = three_dots(rows, weight_ref)
    latent = pieces[0].shape[0]
    part = latent // mp
    for j in range(mp):
        for s in range(slots):
            start = pl.multiple_of(s * latent + (meta[PART] ^ j) * part, part)
            (odd_ref if j % 2 else even_ref)[j // 2, s] = scratch[pl.ds(start, part), :].astype(BF)


def row_back_body(meta, rows_ref, weight_ref, out_ref, *scratch, which):
    rows = out_ref.shape[0]
    me = lax.axis_index("mp")

    def term(j):
        at = pl.ds(pl.multiple_of(other_of(me, j) * rows, rows), rows)
        return lambda: three_dots(rows_ref[at, :], weight_ref)

    pair_sums([(term(which), term(which + 1))], [out_ref], scratch)


def slot_grad_body(meta, *refs, mp, slots, latent, images, groups):
    own_ref, far_ref, slots_ref, table_ref, gain_ref = refs[:5]
    after, (keep_ref, send_ref, grad_ref) = refs[5:-3], refs[-3:]
    part = latent // mp
    start = pl.multiple_of(meta[PART] * part, part)
    for s in range(slots):
        upstream = own_ref[s].astype(F32) + far_ref[s].astype(F32)
        mixed = slots_ref[s, pl.ds(start, part), :].astype(F32) + kind_of(meta, table_ref)
        normed, inv_std = norm_parts(mixed)
        block = meta[POS + s]
        blocks = after[0].shape[0] // latent
        rel = (block // blocks) ^ meta[PART]
        row = pl.multiple_of((block % blocks) * latent + start, part)
        d_after = after[0][pl.ds(row, part), :]
        for j in range(1, mp):
            d_after = jnp.where(rel == j, after[j][pl.ds(row, part), :], d_after)
        grad_ref[s] = (
            d_after.astype(F32) + norm_back(upstream, normed, inv_std, gain_ref[...])
        ).astype(BF)
    for k in range(groups):
        for i in range(images):
            rank = meta[RANK + (k ^ meta[GROUP]) * images + i]
            value = grad_ref[jnp.maximum(rank, 0)]
            value = jnp.where(rank >= 0, value, jnp.zeros_like(value))
            (send_ref if k % 2 else keep_ref)[k // 2, i * part : (i + 1) * part, :] = value


def in_back_body(
    meta, own_ref, far_ref, after_ref, text_ref, slots_ref, table_ref, gain_ref, out_ref, gain_grad, type_grad
):
    upstream = own_ref[...].astype(F32) + far_ref[...].astype(F32)
    normed, inv_std = norm_parts(mixed_rows(meta, text_ref, slots_ref, table_ref))
    d_mixed = after_ref[...] + norm_back(upstream, normed, inv_std, gain_ref[...])
    block = meta[PART] * pl.num_programs(0) + pl.program_id(0)
    out_ref[...] = jnp.where(meta[BLOCK + block] >= 0, 0.0, d_mixed)
    add_rows(gain_grad, upstream * normed)
    add_rows(type_grad, d_mixed)


def pool_back_body(
    meta, *refs, images, mp
):
    pieces, out_w, key_ref, value_ref, query_ref, key_w, value_w = refs[:mp], *refs[mp : mp + 6]
    kv_ref, query_grad, clip_even, clip_odd, grad_ref, scratch = refs[mp + 6 :]
    part = pieces[0].shape[1]
    for j in range(mp):
        for i in range(images):
            start = pl.multiple_of(i * part * mp + (meta[PART] ^ j) * part, part)
            grad_ref[pl.ds(start, part), :] = pieces[j][i]
    d_heads = dot(grad_ref[...], out_w[...], ROWS_BY_ROWS).astype(BF)
    patches = key_ref.shape[0] // images
    latent, wide = query_ref.shape
    for pair in range(wide // LANES):
        lanes = slice(pair * LANES, (pair + 1) * LANES)
        query = query_ref[:, lanes]
        lane = lax.broadcasted_iota(jnp.int32, query.shape, 1)
        d_query = jnp.zeros((latent, LANES), F32)
        for i in range(images):
            rows = slice(i * patches, (i + 1) * patches)
            keys, values = key_ref[rows, lanes], value_ref[rows, lanes]
            grad = d_heads[i * latent : (i + 1) * latent, lanes]
            d_keys = jnp.zeros((patches, LANES), F32)
            d_values = jnp.zeros((patches, LANES), F32)
            for h in range(2):
                keep = lane // HEAD == h
                shares = pool_shares_of(query, keys, h)
                g_one = jnp.where(keep, grad, jnp.zeros_like(grad))
                q_one = jnp.where(keep, query, jnp.zeros_like(query))
                d_shares = dot(g_one, values, ROWS_BY_ROWS)
                inner = jnp.sum(shares * d_shares, axis=-1, keepdims=True)
                d_scores = (shares * (d_shares - inner)).astype(BF)
                d_query += jnp.where(keep, dot(d_scores, keys), 0.0)
                d_keys += dot(d_scores, q_one, OVER_ROWS)
                d_values += dot(shares.astype(BF), g_one, OVER_ROWS)
            kv_ref[rows, lanes] = (d_keys * 0.125).astype(BF)
            kv_ref[rows, slice(wide + pair * LANES, wide + (pair + 1) * LANES)] = d_values.astype(BF)
        query_grad[:, lanes] = d_query * 0.125
    scratch[...] = dot(kv_ref[:, :wide], key_w[...], ROWS_BY_ROWS) + dot(
        kv_ref[:, wide:], value_w[...], ROWS_BY_ROWS
    )
    piece = patches // mp
    for j in range(mp):
        for i in range(images):
            start = pl.multiple_of(i * patches + (meta[PART] ^ j) * piece, piece)
            (clip_odd if j % 2 else clip_even)[j // 2, i] = scratch[
                pl.ds(start, piece), :
            ].astype(BF)


def weight_body(meta, *refs, lefts, rights, before, has_got, split):
    left, right = refs[:lefts], refs[lefts : lefts + rights]
    rest = refs[lefts + rights :]
    depth = sum(r.shape[0] for r in left)
    total = None
    step = depth // max(lefts, rights)
    for start in range(0, depth, step):
        l_ref, l_at = find(left, start)
        r_ref, r_at = find(right, start)
        term = dot(l_ref[l_at : l_at + step, :], r_ref[r_at : r_at + step, :], OVER_ROWS)
        total = term if total is None else total + term
    if split:
        wide = total.shape[1] // 2
        total = jnp.concatenate([total[:, :wide], total[:, wide:]], axis=0)
    if not has_got:
        rest[-1][0] = total.astype(BF)
        return
    even, odd = rest[-2:]
    total = (total + rest[0][0].astype(F32)).astype(BF)
    step = pl.program_id(0)

    @pl.when(step % 2 == 0)
    def _():
        even[0] = total

    @pl.when(step % 2 == 1)
    def _():
        odd[0] = total


def find(refs, start):
    for ref in refs:
        if start < ref.shape[0]:
            return ref, start
        start -= ref.shape[0]
    return None


def add_body(meta, keep_ref, got_ref, keep_out, send_out):
    keep_out[0] = (keep_ref[0].astype(F32) + got_ref[0].astype(F32)).astype(BF)
    send_out[0] = (keep_ref[1].astype(F32) + got_ref[1].astype(F32)).astype(BF)


def gathered_body(meta, left_ref, right_ref, out_ref):
    out_ref[...] = dot(left_ref[...], right_ref[...], OVER_ROWS)


def last_body(meta, keep_ref, got_ref, out_ref):
    out_ref[...] = (keep_ref[...].astype(F32) + got_ref[...].astype(F32)).astype(out_ref.dtype)


def plus(meta, first, second, dtype):
    shape = first.shape
    steps = 2 if shape[-2] % 32 == 0 and len(shape) == 2 else 1
    block = (shape[-2] // steps,) + shape[-1:]
    if len(shape) == 3:
        block = shape
    index = lambda i, m: (i,) + (0,) * (len(shape) - 1)
    return call(
        last_body,
        meta,
        (steps,),
        [(first, block, index), (second, block, index)],
        [(shape, dtype, block, index)],
    )[0]


def split_sum(meta, keep, got):
    count, *dims = keep.shape
    pair, one = (2,) + tuple(dims), (1,) + tuple(dims)
    at = lambda i, m: (i, 0, 0)
    return call(
        add_body,
        meta,
        (count // 2,),
        [(keep, pair, at), (got, pair, at)],
        [((count // 2,) + tuple(dims), BF, one, at)] * 2,
    )


def stack_body(meta, first_ref, second_ref, out_ref):
    out_ref[:, 0] = first_ref[...]
    out_ref[:, 1] = second_ref[...]


class GatherDp:
    def __init__(self, meta, values):
        self.meta, self.values = meta, values[None]
        self.pending = list(reversed(bits_of(lax.axis_size("dp"))))
        self.got = swap(self.values, "dp", self.pending.pop(0))

    def step(self):
        count, *dims = self.values.shape
        stacked = call(
            stack_body,
            self.meta,
            (1,),
            [(self.values,), (self.got,)],
            [((count, 2) + tuple(dims), self.values.dtype, None, None)],
        )[0]
        self.values = stacked.reshape((2 * count,) + tuple(dims))
        if self.pending:
            self.got = swap(self.values, "dp", self.pending.pop(0))

    def end(self):
        while self.pending:
            self.step()
        self.step()
        return self.values


class WeightGrads:
    def __init__(self, meta, members, shape, first=1, cost=1):
        self.meta, self.members, self.shape = meta, members, shape
        self.size = lax.axis_size("dp")
        bits = bits_of(self.size)
        widths = [left[0].shape[1] // self.size for left, *_ in members]
        self.plain = any(w % LANES for w in widths) or self.size < 8
        self.first, self.cost = first, cost
        self.order = [first] + [b for b in bits if b != first]
        self.pending = list(self.order)

    def run(self, side, got):
        half, first = self.size // 2, self.first
        before = None
        for left, right, split, at in self.members:
            part = left[0].shape[1] // self.size
            inner = right[0].shape[1]
            block = (1, 2 * part, inner // 2) if split else (1, part, inner)
            place = lambda i, m, at=at: (i,) + at
            pair_place = lambda i, m, at=at: (i // 2,) + at
            column = lambda i, m: (
                0,
                m[GROUP] ^ ((i // first) * 2 * first + side * first + i % first),
            )
            ins = [(a, (a.shape[0], part), column) for a in left] + [(a,) for a in right]
            if got is not None:
                ins.append((got, block, place))
                outs = [((half // 2,) + self.shape, BF, block, pair_place)] * 2
            else:
                outs = [((half,) + self.shape, BF, block, place)]
            aliases = {}
            if before is not None:
                aliases = {len(ins) + 1 + n: n for n in range(len(outs))}
                ins += [(a, None) for a in before]
            before = call(
                functools.partial(
                    weight_body,
                    lefts=len(left),
                    rights=len(right),
                    before=before is not None,
                    has_got=got is not None,
                    split=split,
                ),
                self.meta,
                (half,),
                ins,
                outs,
                aliases=aliases,
                cost=self.cost,
            )
        return before

    def start(self):
        if not self.plain:
            self.got = swap(self.run(1, None)[0], "dp", self.pending.pop(0))

    def step(self):
        if self.plain:
            return
        if len(self.pending) == len(self.order) - 1:
            self.keep, send = self.run(0, self.got)
        else:
            self.keep, send = split_sum(self.meta, self.keep, self.got)
        self.got = swap(send, "dp", self.pending.pop(0))

    def finish(self):
        if not self.plain:
            while self.pending:
                self.step()
            self.total = plus(self.meta, self.keep[0], self.got[0], F32)

    def end(self):
        me = lax.axis_index("dp")
        results = []
        if self.plain:
            for left, right, split, at in self.members:
                whole = dot(jnp.concatenate(left), jnp.concatenate(right), OVER_ROWS).astype(BF)
                whole = whole.reshape(self.size, -1, whole.shape[1])
                whole = pick(whole, [me ^ k for k in range(self.size)])
                results.append(scatter_dp(whole, bits_of(self.size), F32))
            return results
        for left, right, split, at in self.members:
            part = left[0].shape[1] // self.size
            inner = right[0].shape[1]
            high, wide = (2 * part, inner // 2) if split else (part, inner)
            cut = (slice(at[0] * high, (at[0] + 1) * high), slice(at[1] * wide, (at[1] + 1) * wide))
            value = self.total[cut]
            if split:
                value = jnp.concatenate([value[:part], value[part:]], axis=1)
            results.append(value)
        return results


def shards(
    text_embed,
    clip_feats,
    type_table,
    gain_attn_in,
    qkv_weight,
    gain_attn_out,
    out_weight,
    gain_ffn_in,
    up_weight,
    gain_ffn_out,
    down_weight,
    res_query,
    res_key,
    res_value,
    res_out,
    cotangent,
    owner_count,
    image_seq,
    slot_block,
    seq_kind,
):
    mp = lax.axis_size("mp")
    dp = lax.axis_size("dp")
    rows, width = text_embed.shape
    length = rows * mp
    latent = res_query.shape[0]
    slots = slot_block.shape[1]
    images, patches, clip_width = clip_feats.shape
    wide = qkv_weight.shape[2]
    heads = wide // HEAD
    ff = up_weight.shape[1]
    ff_all = ff * mp
    here = rows // latent
    part = latent // mp
    tile = 512

    Order.mark, Order.channel = None, 0
    meta = make_meta(owner_count, image_seq, slot_block, seq_kind, images)
    table = type_table.astype(F32)
    gain_in, gain_out = gain_attn_in[None], gain_attn_out[None]
    gain_ffn, gain_ff = gain_ffn_in[None], gain_ffn_out[None]
    row_block = lambda i, m: (i, 0)
    few = (latent, width)
    weight = jnp.moveaxis(qkv_weight, 1, 0)
    turn = turn_tables(length)

    text_in = call(
        text_body,
        meta,
        (4,),
        [(text_embed, (rows // 4, width), row_block), (table,), (gain_in,)],
        [((rows, width), BF, (rows // 4, width), row_block)],
    )[0]
    text_pieces = gather_rel(text_in)


    clip = clip_feats.reshape(images * patches, clip_width)
    key_proj, value_proj, pool_out = call(
        functools.partial(pool_body, images=images),
        meta,
        (1,),
        [(clip,), (res_key,), (res_value,), (res_query,)],
        [
            ((images * patches, wide), BF, None, None),
            ((images * patches, wide), BF, None, None),
            ((images * latent, wide), BF, None, None),
        ],
    )
    gathering = GatherDp(meta, pool_out)
    cot = call(
        copy_body,
        meta,
        (2,),
        [(cotangent, (rows // 2, width), row_block)],
        [((rows, width), BF, (rows // 2, width), row_block)],
    )[0]
    cot_pieces = gather_rel(cot)

    state = project(meta, text_pieces[:2], weight, turn, None, 0)
    gathering.step()
    state = project(meta, text_pieces[2:], weight, turn, state, 2)
    gathering.step()

    def d_up_half(which):
        return call(
            functools.partial(times_rows_body, count=2),
            meta,
            (ff // tile,),
            [(cot_pieces[which + n],) for n in range(2)]
            + [(down_weight, (tile, width), row_block)],
            [((rows, ff), BF, (rows, tile), lambda i, m: (0, i))] * 2,
        )

    d_up_near = d_up_half(0)
    pool_rows = gathering.end().reshape(dp * images * latent, wide)
    slot_terms = call(
        functools.partial(pooled_body, slots=slots, mp=mp),
        meta,
        (1,),
        [
            (pool_rows, (latent, wide), lambda i, m, s=s: (m[SOURCE + s], 0))
            for s in range(slots)
        ]
        + [(res_out,)],
        [((mp // 2, slots, part, width), BF, None, None)] * 2,
        scratch=[pltpu.VMEM((slots * latent, width), F32)],
    )
    slot_own, slot_far = scatter_now(meta, *slot_terms)
    slot_pieces = gather_now(meta, add_low(slot_own, slot_far))

    at_slot = lambda i, m: (m[POS + jnp.maximum(i - 3, 0)], 0)
    state = call(
        functools.partial(slot_body, mp=mp, slots=slots, latent=latent),
        meta,
        (3 + slots,),
        [(p,) for p in slot_pieces]
        + [(table,), (gain_in,)]
        + [(weight, (1, width, wide), lambda i, m: (jnp.minimum(i, 2), 0, 0))]
        + [(turn, (3, 2, latent, LANES), lambda i, m: (0, 0) + at_slot(i, m))]
        + [(a, (latent, a.shape[1]), at_slot) for a in state],
        [(a.shape, BF, (latent, a.shape[1]), at_slot) for a in state]
        + [((slots, latent, width), BF, None, None)],
        scratch=[
            pltpu.VMEM((slots, latent, width), F32),
            pltpu.VMEM((3, slots, latent, wide), F32),
            pltpu.VMEM((slots, latent, width), BF),
        ],
        aliases={mp + 5 + n: n for n in range(2)},
    )
    qkv, in_full, slot_rows = state

    att, lse, att_stats = call(
        functools.partial(attend_body, block=rows),
        meta,
        (1,),
        [(qkv,)],
        [
            ((length, wide), BF, None, None),
            ((heads, length), F32, None, None),
            ((8, length), F32, None, None),
        ],
        scratch=[pltpu.VMEM((length, LANES), F32)] * 3,
    )
    att_stats = spread_stats(meta, att_stats)

    mids = call(
        functools.partial(mid_body, mp=mp, width=width),
        meta,
        (mp,),
        [(att, (rows, wide), lambda j, m: (m[PART] ^ j, 0)), (gain_out,)]
        + [(s, (8, rows), lambda j, m: (0, m[PART] ^ j)) for s in att_stats],
        [((length, wide), BF, (rows, wide), lambda j, m: (j, 0))],
    )[0]
    steps = width // tile

    def summed(body, array, weights, which):
        return call(
            body,
            meta,
            (steps,),
            [(array, (2 * rows, array.shape[1]), lambda i, m: (which // 2, 0)), weights],
            [((rows, width), BF, None, None)],
            scratch=pair_scratch(1, steps, rows, tile),
            remote=True,
        )[0]

    out_w = (out_weight, (wide, tile), lambda i, m: (0, i))
    out_far = swap(summed(out_body, mids, out_w, 2), "mp", 2)
    out_terms = [summed(out_body, mids, out_w, 0), out_far]
    d_up = d_up_near + d_up_half(2)
    after_attn, ffn_in = call(
        after_body,
        meta,
        (here,),
        [(t, few, row_block) for t in out_terms]
        + [(text_embed, few, row_block), (slot_rows, (1,) + few, slot_index(here))]
        + [(table,), (gain_ffn,)],
        [((rows, width), F32, few, row_block), ((rows, width), BF, few, row_block)],
    )
    ffn_pieces = gather_rel(ffn_in)

    def up_half(which, before):
        lanes_of = lambda i, m: (0, i)
        half = lambda i, m: (which // 2, i)
        ins = [(ffn_pieces[which],), (ffn_pieces[which + 1],)]
        ins += [(up_weight, (width, tile), lanes_of)]
        ins += [(d_up[which + n], (rows, tile), lanes_of) for n in range(2)]
        ins += [(gain_ff, (1, tile), lanes_of)]
        aliases = {}
        if before is not None:
            aliases = {len(ins) + 1 + n: n for n in range(3)}
            ins += [(a, None) for a in before]
        return call(
            up_body,
            meta,
            (ff // tile,),
            ins,
            [
                ((length, ff), BF, (2 * rows, tile), half),
                ((length, ff), BF, (2 * rows, tile), half),
                ((8, length), F32, (8, 2 * rows), lambda i, m: (0, which // 2)),
            ],
            scratch=[pltpu.VMEM((2 * rows, LANES), F32)] * 4,
            aliases=aliases,
        )

    state = up_half(0, None)
    act, slope, ff_stats = up_half(2, state)
    ff_stats = spread_stats(meta, ff_stats)
    cut = rows // 2
    fine = lambda i, m: (i, 0)
    pre, low, gain_ff_local = call(
        functools.partial(spread_body, mp=mp, width=ff_all),
        meta,
        (length // cut,),
        [(act, (cut, ff), fine), (slope, (cut, ff), fine)]
        + [
            (d_up[j], (cut, ff), lambda i, m, j=j: (jnp.clip(i - 2 * j, 0, 1), 0))
            for j in range(mp)
        ]
        + [(gain_ff,)]
        + [
            (s, (8, cut), lambda i, m, b=b: (0, (((i // 2) ^ b) * 2) + i % 2))
            for b, s in enumerate(ff_stats)
        ],
        [((length, ff), BF, (cut, ff), fine)] * 2 + [((1, ff), F32, None, None)],
    )

    up_w = (up_weight, (tile, ff), row_block)
    down_grad = WeightGrads(meta, [(cot_pieces, [low], False, (0, 0))], (width // dp, ff))
    up_grad = WeightGrads(meta, [(ffn_pieces, [pre], False, (0, 0))], (width // dp, ff), 2)
    down_grad.start()
    back_far = swap(summed(back_body, pre, up_w, 2), "mp", 2)
    ffn_terms = [summed(back_body, pre, up_w, 0), back_far]
    d_after, d_after_low, gain_ffn_local = call(
        ffn_back_body,
        meta,
        (here,),
        [(t, few, row_block) for t in ffn_terms]
        + [(after_attn, few, row_block), (cotangent, few, row_block), (gain_ffn,)],
        [
            ((rows, width), F32, few, row_block),
            ((rows, width), BF, few, row_block),
            ((1, width), F32, None, None),
        ],
    )
    after_pieces = gather_rel(d_after_low)
    up_grad.start()

    down_near, down_far = call(
        down_body,
        meta,
        (steps,),
        [(low,), (down_weight, (ff, tile), lambda i, m: (0, i))],
        [((rows, width), BF, None, None)] * 2,
        scratch=pair_scratch(2, steps, rows, tile),
        remote=True,
    )
    down_far = swap(down_far, "mp", 2)
    def d_mid_half(which, before):
        block = lambda i, m: (m[PART] ^ (which + i), 0)
        lane_block = lambda i, m: (0, m[PART] ^ (which + i))
        aliases = {}
        ins = [(after_pieces[which],), (after_pieces[which + 1],), (out_weight,), (gain_out,)]
        ins += [(att, (rows, wide), block)] + [(s, (8, rows), lane_block) for s in att_stats]
        if before is not None:
            aliases = {len(ins) + 1 + n: n for n in range(2)}
            ins += [(a, None) for a in before]
        return call(
            functools.partial(d_mid_body, mp=mp, width=width),
            meta,
            (2,),
            ins,
            [
                ((length, wide), BF, (rows, wide), block),
                ((8, length), F32, (8, rows), lane_block),
                ((1, wide), F32, None, None),
            ],
            aliases=aliases,
        )

    d_mid, mid_stats, gain_mid_near = d_mid_half(0, None)
    d_mid, mid_stats, gain_mid_far = d_mid_half(2, (d_mid, mid_stats))
    mid_stats = spread_stats(meta, mid_stats)
    out_grad = WeightGrads(meta, [(after_pieces, [mids], False, (0, 0))], (width // dp, wide))
    out_grad.start()
    layer_out = call(
        sum_body,
        meta,
        (here,),
        [(after_attn, few, row_block), (down_near, few, row_block), (down_far, few, row_block)],
        [((rows, width), F32, few, row_block)],
    )[0]
    down_grad.step()
    d_qkv = call(
        functools.partial(attend_back_body, mp=mp, width=width, block=rows),
        meta,
        (1,),
        [(a,) for a in (qkv, att, d_mid, lse, gain_out, turn)]
        + [(s,) for s in att_stats]
        + [(s,) for s in mid_stats],
        [((length, 3 * wide), BF, None, None)],
        scratch=[pltpu.VMEM((length, wide), BF)] + [pltpu.VMEM((length, LANES), F32)] * 3,
    )[0]

    slot_terms = call(
        functools.partial(slot_back_body, slots=slots, mp=mp),
        meta,
        (1,),
        [
            (d_qkv, (latent, 3 * wide), lambda i, m, s=s: (m[POS + s], 0))
            for s in range(slots)
        ]
        + [(weight,)],
        [((mp // 2, slots, part, width), BF, None, None)] * 2,
        scratch=[pltpu.VMEM((slots * latent, width), F32)],
    )
    slot_terms = scatter_now(meta, *slot_terms)
    image_keep, image_send, _ = call(
        functools.partial(
            slot_grad_body, mp=mp, slots=slots, latent=latent, images=images, groups=dp
        ),
        meta,
        (1,),
        [(t,) for t in slot_terms]
        + [(slot_rows,), (table,), (gain_in,)]
        + [(a,) for a in after_pieces],
        [((dp // 2, images * part, width), BF, None, None)] * 2
        + [((slots, part, width), BF, None, None)],
    )
    image_got = exchange(meta, (image_send, "dp", 1))[0]
    in_grad = WeightGrads(meta, [([in_full], [d_qkv], False, (0, 0))], (width // dp, 3 * wide))
    def row_terms(which):
        return call(
            functools.partial(row_back_body, which=which),
            meta,
            (steps,),
            [(d_qkv,), (weight, (3, tile, wide), lambda i, m: (0, i, 0))],
            [((rows, width), BF, None, None)],
            scratch=pair_scratch(1, steps, rows, tile),
            remote=True,
        )[0]

    for bit in bits_of(dp)[1:]:
        image_keep, image_send = split_sum(meta, image_keep, image_got)
        image_got = exchange(meta, (image_send, "dp", bit))[0]
        if bit == 2:
            up_grad.step()
            in_grad.start()
            in_far = swap(row_terms(2), "mp", 2)
            down_grad.step()
            out_grad.step()
    owned = plus(meta, image_keep, image_got, BF).reshape(images, part, width)
    owned_pieces = gather_now(meta, owned)
    d_kv, query_local, clip_even, clip_odd, pool_grad = call(
        functools.partial(pool_back_body, images=images, mp=mp),
        meta,
        (1,),
        [(a,) for a in owned_pieces]
        + [(a,) for a in (res_out, key_proj, value_proj, res_query, res_key, res_value)],
        [
            ((images * patches, 2 * wide), BF, None, None),
            ((latent, wide), F32, None, None),
            ((mp // 2, images, patches // mp, clip_width), BF, None, None),
            ((mp // 2, images, patches // mp, clip_width), BF, None, None),
            ((images * latent, width), BF, None, None),
        ],
        scratch=[pltpu.VMEM((images * patches, clip_width), F32)],
    )
    pool_grads = WeightGrads(
        meta, [([clip], [d_kv], False, (0, 0))], (clip_width // dp, 2 * wide)
    )
    pool_grads.start()
    up_grad.step()
    in_terms = [row_terms(0), in_far]
    text_grad, gain_in_local, type_local = call(
        in_back_body,
        meta,
        (here,),
        [(t, few, row_block) for t in in_terms]
        + [(d_after, few, row_block), (text_embed, few, row_block)]
        + [(slot_rows, (1,) + few, slot_index(here)), (table,), (gain_in,)],
        [
            ((rows, width), F32, few, row_block),
            ((1, width), F32, None, None),
            ((1, width), F32, None, None),
        ],
    )
    kind = (jnp.arange(3) == meta[KIND]).astype(F32)[:, None]
    over_all = jnp.concatenate([kind * type_local, gain_in_local, gain_ffn_local])
    flat = jnp.concatenate(
        [
            over_all.reshape(-1),
            (gain_mid_near + gain_mid_far)[0],
            gain_ff_local[0],
            query_local.reshape(-1),
        ]
    ).reshape(-1, LANES)
    group = lax.axis_index("dp")
    columns = pool_grad.reshape(images * latent, dp, width // dp).swapaxes(0, 1)
    columns = pick(columns, [group ^ k for k in range(dp)])
    hops = bits_of(dp)[1:] + [1]
    for bit in hops:
        cut = columns.reshape((-1, 2, bit) + columns.shape[1:])
        stay, send = halve(cut, 1)
        got, flat_got = exchange(meta, (send, "dp", bit), (flat, "dp", bit))
        flat = plus(meta, flat, flat_got, F32)
        columns = jnp.stack([stay, got], axis=1).reshape(columns.shape)
        if bit == hops[-2]:
            in_grad.step()
            out_grad.step()
            pool_grads.step()
    clip_even = add_low(clip_even, exchange(meta, (clip_odd, "mp", 1))[0])
    clip_far, flat_far, flat_near = exchange(
        meta, (clip_even[1], "mp", 2), (flat, "mp", 2), (flat, "mp", 1)
    )
    flat_last = exchange(meta, (flat_far, "mp", 1))[0]
    res_out_grad = call(
        gathered_body,
        meta,
        (1,),
        [(pool_rows,), (columns.reshape(dp * images * latent, width // dp),)],
        [((wide, width // dp), F32, None, None)],
    )[0]
    in_grad.step()
    pool_grads.step()
    down_grad.finish()
    up_grad.finish()
    out_grad.finish()
    pool_grads.finish()
    in_grad.finish()
    clip_grad = clip_even[0].astype(F32) + clip_far.astype(F32)
    flat = by_mp(jnp.stack([flat, flat_near, flat_far, flat_last])).reshape(mp, -1)
    sums = jnp.sum(flat[:, : 5 * width].reshape(mp, 5, width), axis=0)
    parts = flat[:, 5 * width :]
    query_grad = jnp.swapaxes(parts[:, wide + ff :].reshape(mp, latent, wide), 0, 1)
    kv_grad = pool_grads.end()[0]
    qkv_grad, out_grad = in_grad.end()[0], out_grad.end()[0]
    return (
        layer_out,
        text_grad,
        clip_grad,
        sums[:3],
        sums[3],
        qkv_grad.reshape(-1, 3, wide),
        parts[:, :wide].reshape(-1),
        out_grad.T,
        sums[4],
        up_grad.end()[0],
        parts[:, wide : wide + ff].reshape(-1),
        down_grad.end()[0].T,
        query_grad.reshape(latent, width),
        kv_grad[:, :wide],
        kv_grad[:, wide:],
        res_out_grad,
    )


def solution(mesh):
    return jax.shard_map(
        shards,
        mesh=mesh,
        in_specs=(
            P(("dp", "mp"), None),
            P("dp", None, None),
            P(),
            P(),
            P(None, None, "mp"),
            P("mp"),
            P("mp", None),
            P(),
            P(None, "mp"),
            P("mp"),
            P("mp", None),
            P(None, "mp"),
            P(None, "mp"),
            P(None, "mp"),
            P("mp", None),
            P(("dp", "mp"), None),
            P(),
            P(),
            P(),
            P(),
        ),
        out_specs=(
            P(("dp", "mp"), None),
            P(("dp", "mp"), None),
            P("dp", "mp", None),
            P(),
            P(),
            P("dp", None, "mp"),
            P(),
            P("mp", "dp"),
            P(),
            P("dp", "mp"),
            P(),
            P("mp", "dp"),
            P(),
            P("dp", "mp"),
            P("dp", "mp"),
            P("mp", "dp"),
        ),
        check_vma=False,
    )
```

time: 888 us -> 732 us (0.82)
  waiting for transfers between devices: 349 us -> 119 us
  Pallas kernels: 360 us -> 487 us
  other arithmetic: 43.9 us -> 9.65 us
  starting transfers between devices: 59.1 us -> 36.5 us
    ppermute x81 -> x34, waiting for transfers between devices: 349 us -> 119 us  [swap(): return lax.ppermute(values, axis, [(i, i ^ bit) for i in range(size)])]
    pallas_call x39 -> x81, Pallas kernels: 358 us -> 485 us  [call(): pl.pallas_call(marked, out_shape=shapes, grid_spec=pltpu.PrefetchScalarGr...]
    ppermute x81 -> x34, starting transfers between devices: 59.1 us -> 36.5 us  [swap(): return lax.ppermute(values, axis, [(i, i ^ bit) for i in range(size)])]
    unnamed x144 -> x293, local copies, waits for them, and re-layouts: 38.9 us -> 60.4 us
    add x9 -> x1, other arithmetic: 10.5 us -> 0.86 us  [shards(): clip_grad = clip_even[0].astype(F32) + clip_far.astype(F32)]
  transfers between devices with their start and end apart: 81 -> 34, of which waited for: 28 -> 10; matrix products, arithmetic and copies ran while one was open for 9% -> 3% of each run, Pallas kernels for 33% -> 62%
where the time goes in v2:
time: 732 us; the launch traced here: 723 us
  Pallas kernels  487 us (67%)
  waiting for transfers between devices  119 us (16%)
  local copies, waits for them, and re-layouts  66.9 us (9%)
  starting transfers between devices  36.5 us (5%)
  other arithmetic  9.65 us (1%)
    pallas_call x81, Pallas kernels, call(): pl.pallas_call(marked, out_shape=shapes, grid_spec=pltpu.PrefetchScalarGr...  485 us
    ppermute x34, waiting for transfers between devices, swap(): return lax.ppermute(values, axis, [(i, i ^ bit) for i in range(size)])  119 us
    unnamed x293, local copies, waits for them, and re-layouts  60.4 us
    ppermute x34, starting transfers between devices, swap(): return lax.ppermute(values, axis, [(i, i ^ bit) for i in range(size)])  36.5 us
  transfers between devices with their start and end apart: 34, of which 10 were waited for; matrix products, arithmetic and copies ran while one was open for 3% of the time, Pallas kernels for 62%

profile of v2, /device:TPU:0, one launch (start us, length us, event | category | flops | bytes accessed | tf_op | source)
XLA Modules:
  0.0 722.5 jit_solution(10329216174182863027)
XLA Ops:
  27.9 8.4 %collective-permute-done.3.refs_0_ = bf16[256,2048]{1,0:T(8,128)(2,1)S(1)} collective-permute-done((bf16[256,2048]{1,0:T(8,128)(2,1)S(1)}, bf16[256,2048]{1,0:T(8,128)(2,1)S(1)}, u32[]{:S(2)}, u32[]{:S(2)}) %collective-permute-start.3) | collective-permute-done | bytes 1048608 | tf_op jit(solution)/shard_map/ppermute | solution.py:36
  78.5 8.9 %body.21 = (bf16[4,16,2048]{2,1,0:T(8,128)(2,1)S(1)}, f32[8,128]{1,0:T(8,128)S(1)}) custom-call(s32[48]{0:T(128)S(1)} %copy-done.89, bf16[4,16,2048]{2,1,0:T(8,128)(2,1)S(1)} %slice_bitcast_fusion.9.refs_0_, f32[8,128]{1,0:T(8,128)S(1)} %get-tuple-element.256.refs_1_), custom_call_target="tpu_custom_call" | custom-call | flops 40000000 | bytes 1024 | tf_op jit(solution)/shard_map/body/pallas_call | solution.py:145
  87.5 9.1 %body.22 = (bf16[4,16,2048]{2,1,0:T(8,128)(2,1)S(1)}, bf16[4,16,2048]{2,1,0:T(8,128)(2,1)S(1)}, f32[8,128]{1,0:T(8,128)S(1)}) custom-call(s32[48]{0:T(128)S(1)} %copy-done.89, bf16[4,16,2048]{2,1,0:T(8,128)(2,1)S(1)} %fusion.refs_0_.refs_1_, bf16[4,16,2048]{2,1,0:T(8,128)(2,1)S(1)} %fusion.refs_0_.refs_1_, f32[8,128]{1,0:T(8,128)S(1)} %get-tuple-element.258.refs_2_), custom_call_target="tpu_custom_call" | custom-call | flops 40000000 | bytes 1024 | tf_op jit(solution)/shard_map/body/pallas_call | solution.py:145
  106.0 15.3 %attend_body.1 = (bf16[1024,512]{1,0:T(8,128)(2,1)S(1)}, f32[8,1024]{1,0:T(8,128)S(1)}, f32[8,1024]{1,0:T(8,128)S(1)}, f32[8,128]{1,0:T(8,128)S(1)}) custom-call(s32[48]{0:T(128)S(1)} %copy-done.89, bf16[1024,1536]{1,0:T(8,128)(2,1)S(1)} %get-tuple-element.266.refs_0_, f32[8,128]{1,0:T(8,128)S(1)} %get-tuple-element.267.refs_1_), custom_call_target="tpu_custom_call" | custom-call | flops 40000000 | bytes 1024 | tf_op jit(solution)/shard_map/attend_body/pallas_call | solution.py:145
  148.9 9.0 %collective-permute-done.7.refs_1_ = bf16[256,2048]{1,0:T(8,128)(2,1)S(1)} collective-permute-done((bf16[256,2048]{1,0:T(8,128)(2,1)S(1)}, bf16[256,2048]{1,0:T(8,128)(2,1)S(1)}, u32[]{:S(2)}, u32[]{:S(2)}) %collective-permute-start.7) | collective-permute-done | bytes 1048608 | tf_op jit(solution)/shard_map/ppermute | solution.py:36
  161.7 23.8 %collective-permute-done.10.refs_0_.refs_2_ = bf16[256,2048]{1,0:T(8,128)(2,1)S(1)} collective-permute-done((bf16[256,2048]{1,0:T(8,128)(2,1)S(1)}, bf16[256,2048]{1,0:T(8,128)(2,1)S(1)}, u32[]{:S(2)}, u32[]{:S(2)}) %collective-permute-start.10) | collective-permute-done | bytes 1048608 | tf_op jit(solution)/shard_map/ppermute | solution.py:36
  185.6 10.7 %up_body.2 = (bf16[1024,2048]{1,0:T(8,128)(2,1)S(1)}, bf16[1024,2048]{1,0:T(8,128)(2,1)S(1)}, f32[8,1024]{1,0:T(8,128)S(1)}, f32[8,128]{1,0:T(8,128)S(1)}) custom-call(s32[48]{0:T(128)S(1)} %copy-done.89, bf16[256,2048]{1,0:T(8,128)(2,1)S(1)} %get-tuple-element.284.refs_0_, bf16[256,2048]{1,0:T(8,128)(2,1)S(1)} %collective-permute-done.12.refs_1_, ...), custom_call_target="tpu_custom_call" | custom-call | flops 40000000 | bytes 1024 | tf_op jit(solution)/shard_map/up_body/pallas_call | solution.py:145
  196.4 10.2 %up_body.3 = (bf16[1024,2048]{1,0:T(8,128)(2,1)S(1)}, bf16[1024,2048]{1,0:T(8,128)(2,1)S(1)}, f32[8,1024]{1,0:T(8,128)S(1)}, f32[8,128]{1,0:T(8,128)S(1)}) custom-call(s32[48]{0:T(128)S(1)} %copy-done.89, bf16[256,2048]{1,0:T(8,128)(2,1)S(1)} %collective-permute-done.10.refs_0_.refs_2_, ...), custom_call_target="tpu_custom_call", output_to_operand_aliasing={{0}: (7, {}), {1}: (8, {}), {2}: (9, {})} | custom-call | flops 40000000 | bytes 1024 | tf_op jit(solution)/shard_map/up_body/pallas_call | solution.py:145
  256.5 17.1 %collective-permute-done.13.refs_1_ = bf16[256,2048]{1,0:T(8,128)(2,1)S(1)} collective-permute-done((bf16[256,2048]{1,0:T(8,128)(2,1)S(1)}, bf16[256,2048]{1,0:T(8,128)(2,1)S(1)}, u32[]{:S(2)}, u32[]{:S(2)}) %collective-permute-start.13) | collective-permute-done | bytes 1048608 | tf_op jit(solution)/shard_map/ppermute | solution.py:36
  288.0 13.9 %collective-permute-done.16.refs_0_.refs_2_.refs_7_ = bf16[256,2048]{1,0:T(8,128)(2,1)S(1)} collective-permute-done((bf16[256,2048]{1,0:T(8,128)(2,1)S(1)}, bf16[256,2048]{1,0:T(8,128)(2,1)S(1)}, u32[]{:S(2)}, u32[]{:S(2)}) %collective-permute-start.16) | collective-permute-done | bytes 1048608 | tf_op jit(solution)/shard_map/ppermute | solution.py:36
  301.9 13.5 %down_body.1 = (bf16[256,2048]{1,0:T(8,128)(2,1)S(1)}, bf16[256,2048]{1,0:T(8,128)(2,1)S(1)}, f32[8,128]{1,0:T(8,128)S(1)}) custom-call(s32[48]{0:T(128)S(1)} %copy-done.89, bf16[1024,2048]{1,0:T(8,128)(2,1)S(1)} %copy-done.12, bf16[2048,2048]{1,0:T(8,128)(2,1)S(1)} %bitcast.151, f32[8,128]{1,0:T(8,128)S(1)} %get-tuple-element.311.refs_2_), custom_call_target="tpu_custom_call" | custom-call | flops 40000000 | bytes 1024 | tf_op jit(solution)/shard_map/down_body/pallas_call | solution.py:145
  322.7 19.4 %body.26 = (f32[8,1024]{1,0:T(8,128)S(1)}, f32[8,1024]{1,0:T(8,128)S(1)}, f32[8,1024]{1,0:T(8,128)S(1)}, f32[8,128]{1,0:T(8,128)S(1)}) custom-call(s32[48]{0:T(128)S(1)} %copy-done.89, f32[8,1024]{1,0:T(8,128)S(1)} %get-tuple-element.319.refs_0_.refs_1_.refs_2_.refs_10_, f32[8,1024]{1,0:T(8,128)S(1)} %get-tuple-element.319.refs_0_.refs_1_.refs_2_.refs_10_, ...), custom_call_target="tpu_custom_call" | custom-call | flops 40000000 | bytes 1024 | tf_op jit(solution)/shard_map/body/pallas_call | solution.py:145
  348.3 8.8 %weight_body.13 = (bf16[2,256,2048]{2,1,0:T(8,128)(2,1)S(1)}, bf16[2,256,2048]{2,1,0:T(8,128)(2,1)}, f32[8,128]{1,0:T(8,128)S(1)}) custom-call(s32[48]{0:T(128)S(1)} %copy-done.89, bf16[256,2048]{1,0:T(8,128)(2,1)S(1)} %copy-done.46, bf16[256,2048]{1,0:T(8,128)(2,1)S(1)} %copy-done.49, bf16[256,2048]{1,0:T(8,128)(2,1)} %collective-permute-done.8.refs_0_.refs_2_, ...), custom_call_target="tpu_custom_call" | custom-call | flops 40000000 | bytes 1024 | tf_op jit(solution)/shard_map/weight_body/pallas_call | solution.py:145
  366.9 20.8 %attend_back_body.1 = (bf16[1024,1536]{1,0:T(8,128)(2,1)S(1)}, f32[8,128]{1,0:T(8,128)S(1)}) custom-call(s32[48]{0:T(128)S(1)} %copy-done.90, bf16[1024,1536]{1,0:T(8,128)(2,1)S(1)} %copy-done.10, bf16[1024,512]{1,0:T(8,128)(2,1)S(1)} %copy-done.17, bf16[1024,512]{1,0:T(8,128)(2,1)S(1)} %copy-done.71, f32[8,1024]{1,0:T(8,128)S(1)} %get-tuple-element.325.refs_3_, ...), custom_call_target="tpu_custom_call" | custom-call | flops 40000000 | bytes 1024 | tf_op jit(solution)/shard_map/attend_back_body/pallas_call | solution.py:145
  395.8 8.9 %body.28 = (bf16[4,16,2048]{2,1,0:T(8,128)(2,1)S(1)}, f32[8,128]{1,0:T(8,128)S(1)}) custom-call(s32[48]{0:T(128)S(1)} %copy-done.90, bf16[4,16,2048]{2,1,0:T(8,128)(2,1)S(1)} %get-tuple-element.506.refs_0_, f32[8,128]{1,0:T(8,128)S(1)} %get-tuple-element.339.refs_1_), custom_call_target="tpu_custom_call" | custom-call | flops 40000000 | bytes 1024 | tf_op jit(solution)/shard_map/body/pallas_call | solution.py:145
  406.6 13.8 %body.29 = (bf16[4,32,2048]{2,1,0:T(8,128)(2,1)S(1)}, f32[8,128]{1,0:T(8,128)S(1)}) custom-call(s32[48]{0:T(128)S(1)} %copy-done.90, bf16[4,32,2048]{2,1,0:T(8,128)(2,1)S(1)} %get-tuple-element.343.refs_0_, f32[8,128]{1,0:T(8,128)S(1)} %get-tuple-element.344.refs_1_), custom_call_target="tpu_custom_call" | custom-call | flops 40000000 | bytes 1024 | tf_op jit(solution)/shard_map/body/pallas_call | solution.py:145
  430.2 9.1 %weight_body.14 = (bf16[2,256,2048]{2,1,0:T(8,128)(2,1)S(1)}, bf16[2,256,2048]{2,1,0:T(8,128)(2,1)}, f32[8,128]{1,0:T(8,128)S(1)}) custom-call(s32[48]{0:T(128)S(1)} %copy-done.90, bf16[256,2048]{1,0:T(8,128)(2,1)S(1)} %copy-done.61, bf16[256,2048]{1,0:T(8,128)(2,1)S(1)} %copy-done.64, bf16[256,2048]{1,0:T(8,128)(2,1)S(1)} %copy-done.52, ...), custom_call_target="tpu_custom_call" | custom-call | flops 40000000 | bytes 1024 | tf_op jit(solution)/shard_map/weight_body/pallas_call | solution.py:145
  466.2 9.3 %body.31 = (bf16[1,32,2048]{2,1,0:T(8,128)(2,1)S(1)}, f32[8,128]{1,0:T(8,128)S(1)}) custom-call(s32[48]{0:T(128)S(1)} %copy-done.90, bf16[1,32,2048]{2,1,0:T(8,128)(2,1)S(1)} %get-tuple-element.364.refs_0_, f32[8,128]{1,0:T(8,128)S(1)} %get-tuple-element.365.refs_1_), custom_call_target="tpu_custom_call" | custom-call | flops 40000000 | bytes 1024 | tf_op jit(solution)/shard_map/body/pallas_call | solution.py:145
  483.7 8.6 %pool_back_body.1 = (bf16[512,1024]{1,0:T(8,128)(2,1)S(1)}, f32[64,512]{1,0:T(8,128)S(1)}, bf16[2,2,64,1024]{3,2,1,0:T(8,128)(2,1)S(1)}, bf16[2,2,64,1024]{3,2,1...) custom-call(s32[48]{0:T(128)S(1)} %copy-done.90, bf16[2,16,2048]{2,1,0:T(8,128)(2,1)S(1)} %bitcast.166, ...), custom_call_target="tpu_custom_call" | custom-call | flops 40000000 | bytes 1024 | tf_op jit(solution)/shard_map/pool_back_body/pallas_call | solution.py:145
  521.2 23.4 %body.34 = (bf16[2,2,128,256]{3,2,1,0:T(8,128)(2,1)S(1)}, f32[356,128]{1,0:T(8,128)S(1)}, f32[8,128]{1,0:T(8,128)S(1)}) custom-call(s32[48]{0:T(128)S(1)} %copy-done.90, bf16[2,2,128,256]{3,2,1,0:T(8,128)(2,1)S(1)} %get-tuple-element.497.refs_0_, f32[356,128]{1,0:T(8,128)S(1)} %maximum_bitcast_fusion.3.refs_1_.refs_0_, f32[8,128]{1,0:T(8,128)S(1)} %get-tuple-element.396.refs_2_), custom_call_target="tpu_custom_call" | custom-call | flops 40000000 | bytes 1024 | tf_op jit(solution)/shard_map/body/pallas_call | solution.py:145
  546.3 34.4 %body.35 = (bf16[1,4,128,256]{3,2,1,0:T(8,128)(2,1)S(1)}, f32[356,128]{1,0:T(8,128)S(1)}, f32[8,128]{1,0:T(8,128)S(1)}) custom-call(s32[48]{0:T(128)S(1)} %copy-done.90, bf16[1,4,128,256]{3,2,1,0:T(8,128)(2,1)S(1)} %get-tuple-element.495.refs_0_, f32[356,128]{1,0:T(8,128)S(1)} %get-tuple-element.399.refs_1_.refs_0_, f32[8,128]{1,0:T(8,128)S(1)} %get-tuple-element.401.refs_2_), custom_call_target="tpu_custom_call" | custom-call | flops 40000000 | bytes 1024 | tf_op jit(solution)/shard_map/body/pallas_call | solution.py:145
  597.5 15.6 %body.36 = (bf16[4,1,128,256]{3,2,1,0:T(8,128)(2,1)S(1)}, f32[356,128]{1,0:T(8,128)S(1)}, f32[8,128]{1,0:T(8,128)S(1)}) custom-call(s32[48]{0:T(128)S(1)} %copy-done.90, bf16[4,1,128,256]{3,2,1,0:T(8,128)(2,1)S(1)} %get-tuple-element.493.refs_0_, f32[356,128]{1,0:T(8,128)S(1)} %get-tuple-element.404.refs_1_.refs_0_, f32[8,128]{1,0:T(8,128)S(1)} %get-tuple-element.413.refs_2_), custom_call_target="tpu_custom_call" | custom-call | flops 40000000 | bytes 1024 | tf_op jit(solution)/shard_map/body/pallas_call | solution.py:145
  621.9 19.1 %body.38 = (bf16[2,64,1024]{2,1,0:T(8,128)(2,1)S(1)}, f32[356,128]{1,0:T(8,128)S(1)}, f32[356,128]{1,0:T(8,128)S(1)}, f32[8,128]{1,0:T(8,128)S(1)}) custom-call(s32[48]{0:T(128)S(1)} %copy-done.90, bf16[2,64,1024]{2,1,0:T(8,128)(2,1)S(1)} %slice_bitcast_fusion.1.refs_0_, f32[356,128]{1,0:T(8,128)S(1)} %get-tuple-element.418.refs_1_.refs_2_, ...), custom_call_target="tpu_custom_call" | custom-call | flops 40000000 | bytes 1024 | tf_op jit(solution)/shard_map/body/pallas_call | solution.py:145
  677.1 33.5 %collective-permute-done.31 = bf16[1,256,512]{2,1,0:T(8,128)(2,1)S(1)} collective-permute-done((bf16[1,256,512]{2,1,0:T(8,128)(2,1)}, bf16[1,256,512]{2,1,0:T(8,128)(2,1)S(1)}, u32[]{:S(2)}, u32[]{:S(2)}) %collective-permute-start.31) | collective-permute-done | bytes 262176 | tf_op jit(solution)/shard_map/ppermute | solution.py:36
  (467 shorter events, 354.5 us)
Async XLA Ops:
  9.3 27.0 %collective-permute-start.3 = (bf16[256,2048]{1,0:T(8,128)(2,1)S(1)}, bf16[256,2048]{1,0:T(8,128)(2,1)S(1)}, u32[]{:S(2)}, u32[]{:S(2)}) collective-permute-start(bf16[256,2048]{1,0:T(8,128)(2,1)S(1)} %get-tuple-element.237.refs_0_), channel_id=1, source_target_pairs={{0,2},{1,3},{2,0},{3,1},{4,6},{5,7},{6,4},{7,5},{8,10},{9,11},{10,... | collective-permute-start | bytes 3145736 | tf_op jit(solution)/shard_map/ppermute | solution.py:36
  12.3 28.0 %collective-permute-start.1 = (bf16[256,2048]{1,0:T(8,128)(2,1)S(1)}, bf16[256,2048]{1,0:T(8,128)(2,1)S(1)}, u32[]{:S(2)}, u32[]{:S(2)}) collective-permute-start(bf16[256,2048]{1,0:T(8,128)(2,1)S(1)} %get-tuple-element.237.refs_0_), channel_id=1, source_target_pairs={{0,1},{1,0},{2,3},{3,2},{4,5},{5,4},{6,7},{7,6},{8,9},{9,8},{10,11... | collective-permute-start | bytes 3145736 | tf_op jit(solution)/shard_map/ppermute | solution.py:36
  24.2 35.5 %collective-permute-start.6 = (bf16[256,2048]{1,0:T(8,128)(2,1)S(1)}, bf16[256,2048]{1,0:T(8,128)(2,1)S(1)}, u32[]{:S(2)}, u32[]{:S(2)}) collective-permute-start(bf16[256,2048]{1,0:T(8,128)(2,1)S(1)} %get-tuple-element.247.refs_0_), channel_id=1, source_target_pairs={{0,1},{1,0},{2,3},{3,2},{4,5},{5,4},{6,7},{7,6},{8,9},{9,8},{10,11... | collective-permute-start | bytes 3145736 | tf_op jit(solution)/shard_map/ppermute | solution.py:36
  24.7 34.9 %collective-permute-start.8 = (bf16[256,2048]{1,0:T(8,128)(2,1)S(1)}, bf16[256,2048]{1,0:T(8,128)(2,1)}, u32[]{:S(2)}, u32[]{:S(2)}) collective-permute-start(bf16[256,2048]{1,0:T(8,128)(2,1)S(1)} %get-tuple-element.247.refs_0_), channel_id=1, source_target_pairs={{0,2},{1,3},{2,0},{3,1},{4,6},{5,7},{6,4},{7,5},{8,10},{9,11},{10,... | collective-permute-start | bytes 3145736 | tf_op jit(solution)/shard_map/ppermute | solution.py:36
  59.7 78.2 %collective-permute-start.9 = (bf16[256,2048]{1,0:T(8,128)(2,1)}, bf16[256,2048]{1,0:T(8,128)(2,1)S(1)}, u32[]{:S(2)}, u32[]{:S(2)}) collective-permute-start(bf16[256,2048]{1,0:T(8,128)(2,1)} %collective-permute-done.8.refs_0_.refs_2_), channel_id=1, source_target_pairs={{0,1},{1,0},{2,3},{3,2},{4,5},{5,4},{6,7},{7,6},{8,9},{9,8},{10,11... | collective-permute-start | bytes 3145736 | tf_op jit(solution)/shard_map/ppermute | solution.py:36
  132.6 25.3 %collective-permute-start.7 = (bf16[256,2048]{1,0:T(8,128)(2,1)S(1)}, bf16[256,2048]{1,0:T(8,128)(2,1)S(1)}, u32[]{:S(2)}, u32[]{:S(2)}) collective-permute-start(bf16[256,2048]{1,0:T(8,128)(2,1)S(1)} %get-tuple-element.279), channel_id=1, source_target_pairs={{0,2},{1,3},{2,0},{3,1},{4,6},{5,7},{6,4},{7,5},{8,10},{9,11},{10,... | collective-permute-start | bytes 3145736 | tf_op jit(solution)/shard_map/ppermute | solution.py:36
  239.4 108.9 %collective-permute-start.18 = (bf16[4,256,2048]{2,1,0:T(8,128)(2,1)}, bf16[4,256,2048]{2,1,0:T(8,128)(2,1)}, u32[]{:S(2)}, u32[]{:S(2)}) collective-permute-start(bf16[4,256,2048]{2,1,0:T(8,128)(2,1)} %get-tuple-element.329), channel_id=1, source_target_pairs={{0,4},{4,0},{8,12},{12,8},{16,20},{20,16},{24,28},{28,24},{1,5},{5... | collective-permute-start | bytes 12582920 | tf_op jit(solution)/shard_map/ppermute | solution.py:36
  248.3 25.3 %collective-permute-start.13 = (bf16[256,2048]{1,0:T(8,128)(2,1)S(1)}, bf16[256,2048]{1,0:T(8,128)(2,1)S(1)}, u32[]{:S(2)}, u32[]{:S(2)}) collective-permute-start(bf16[256,2048]{1,0:T(8,128)(2,1)S(1)} %get-tuple-element.308), channel_id=1, source_target_pairs={{0,2},{1,3},{2,0},{3,1},{4,6},{5,7},{6,4},{7,5},{8,10},{9,11},{10,... | collective-permute-start | bytes 3145736 | tf_op jit(solution)/shard_map/ppermute | solution.py:36
  286.4 142.5 %collective-permute-start.19 = (bf16[4,256,2048]{2,1,0:T(8,128)(2,1)}, bf16[4,256,2048]{2,1,0:T(8,128)(2,1)}, u32[]{:S(2)}, u32[]{:S(2)}) collective-permute-start(bf16[4,256,2048]{2,1,0:T(8,128)(2,1)} %get-tuple-element.333), channel_id=1, source_target_pairs={{0,8},{4,12},{8,0},{12,4},{16,24},{20,28},{24,16},{28,20},{1,9},{5... | collective-permute-start | bytes 12582920 | tf_op jit(solution)/shard_map/ppermute | solution.py:36
  288.0 28.1 %collective-permute-start.15 = (bf16[256,2048]{1,0:T(8,128)(2,1)S(1)}, bf16[256,2048]{1,0:T(8,128)(2,1)S(1)}, u32[]{:S(2)}, u32[]{:S(2)}) collective-permute-start(bf16[256,2048]{1,0:T(8,128)(2,1)S(1)} %get-tuple-element.314.refs_0_.refs_5_), channel_id=1, source_target_pairs={{0,1},{1,0},{2,3},{3,2},{4,5},{5,4},{6,7},{7,6},{8,9},{9,8},{10,11... | collective-permute-start | bytes 3145736 | tf_op jit(solution)/shard_map/ppermute | solution.py:36
  315.4 30.4 %collective-permute-start.14 = (bf16[256,2048]{1,0:T(8,128)(2,1)S(1)}, bf16[256,2048]{1,0:T(8,128)(2,1)S(1)}, u32[]{:S(2)}, u32[]{:S(2)}) collective-permute-start(bf16[256,2048]{1,0:T(8,128)(2,1)S(1)} %get-tuple-element.313), channel_id=1, source_target_pairs={{0,2},{1,3},{2,0},{3,1},{4,6},{5,7},{6,4},{7,5},{8,10},{9,11},{10,... | collective-permute-start | bytes 3145736 | tf_op jit(solution)/shard_map/ppermute | solution.py:36
  358.5 97.0 %collective-permute-start.22 = (bf16[2,256,2048]{2,1,0:T(8,128)(2,1)}, bf16[2,256,2048]{2,1,0:T(8,128)(2,1)}, u32[]{:S(2)}, u32[]{:S(2)}) collective-permute-start(bf16[2,256,2048]{2,1,0:T(8,128)(2,1)} %get-tuple-element.356), channel_id=1, source_target_pairs={{0,8},{4,12},{8,0},{12,4},{16,24},{20,28},{24,16},{28,20},{1,9},{5... | collective-permute-start | bytes 6291464 | tf_op jit(solution)/shard_map/ppermute | solution.py:36
  360.1 99.8 %collective-permute-start.21 = (bf16[4,256,512]{2,1,0:T(8,128)(2,1)}, bf16[4,256,512]{2,1,0:T(8,128)(2,1)}, u32[]{:S(2)}, u32[]{:S(2)}) collective-permute-start(bf16[4,256,512]{2,1,0:T(8,128)(2,1)} %get-tuple-element.354), channel_id=1, source_target_pairs={{0,4},{4,0},{8,12},{12,8},{16,20},{20,16},{24,28},{28,24},{1,5},{5... | collective-permute-start | bytes 3145736 | tf_op jit(solution)/shard_map/ppermute | solution.py:36
  439.2 62.7 %collective-permute-start.20 = (bf16[2,256,2048]{2,1,0:T(8,128)(2,1)}, bf16[2,256,2048]{2,1,0:T(8,128)(2,1)S(1)}, u32[]{:S(2)}, u32[]{:S(2)}) collective-permute-start(bf16[2,256,2048]{2,1,0:T(8,128)(2,1)} %get-tuple-element.351), channel_id=1, source_target_pairs={{0,4},{4,0},{8,12},{12,8},{16,20},{20,16},{24,28},{28,24},{1,5},{5... | collective-permute-start | bytes 6291464 | tf_op jit(solution)/shard_map/ppermute | solution.py:36
  453.3 61.3 %collective-permute-start.23 = (bf16[256,2048]{1,0:T(8,128)(2,1)S(1)}, bf16[256,2048]{1,0:T(8,128)(2,1)S(1)}, u32[]{:S(2)}, u32[]{:S(2)}) collective-permute-start(bf16[256,2048]{1,0:T(8,128)(2,1)S(1)} %get-tuple-element.382), channel_id=1, source_target_pairs={{0,2},{1,3},{2,0},{3,1},{4,6},{5,7},{6,4},{7,5},{8,10},{9,11},{10,... | collective-permute-start | bytes 3145736 | tf_op jit(solution)/shard_map/ppermute | solution.py:36
  454.1 127.2 %collective-permute-start.26 = (bf16[4,256,1536]{2,1,0:T(8,128)(2,1)}, bf16[4,256,1536]{2,1,0:T(8,128)(2,1)}, u32[]{:S(2)}, u32[]{:S(2)}) collective-permute-start(bf16[4,256,1536]{2,1,0:T(8,128)(2,1)} %get-tuple-element.409), channel_id=1, source_target_pairs={{0,4},{4,0},{8,12},{12,8},{16,20},{20,16},{24,28},{28,24},{1,5},{5... | collective-permute-start | bytes 9437192 | tf_op jit(solution)/shard_map/ppermute | solution.py:36
  499.0 94.8 %collective-permute-start.24 = (bf16[4,128,1024]{2,1,0:T(8,128)(2,1)}, bf16[4,128,1024]{2,1,0:T(8,128)(2,1)}, u32[]{:S(2)}, u32[]{:S(2)}) collective-permute-start(bf16[4,128,1024]{2,1,0:T(8,128)(2,1)} %get-tuple-element.406), channel_id=1, source_target_pairs={{0,4},{4,0},{8,12},{12,8},{16,20},{20,16},{24,28},{28,24},{1,5},{5... | collective-permute-start | bytes 3145736 | tf_op jit(solution)/shard_map/ppermute | solution.py:36
  500.0 92.0 %collective-permute-start.25 = (bf16[2,256,512]{2,1,0:T(8,128)(2,1)}, bf16[2,256,512]{2,1,0:T(8,128)(2,1)}, u32[]{:S(2)}, u32[]{:S(2)}) collective-permute-start(bf16[2,256,512]{2,1,0:T(8,128)(2,1)} %get-tuple-element.408), channel_id=1, source_target_pairs={{0,8},{4,12},{8,0},{12,4},{16,24},{20,28},{24,16},{28,20},{1,9},{5... | collective-permute-start | bytes 1572872 | tf_op jit(solution)/shard_map/ppermute | solution.py:36
  502.0 170.2 %collective-permute-start.33 = (bf16[1,256,2048]{2,1,0:T(8,128)(2,1)}, bf16[1,256,2048]{2,1,0:T(8,128)(2,1)}, u32[]{:S(2)}, u32[]{:S(2)}) collective-permute-start(bf16[1,256,2048]{2,1,0:T(8,128)(2,1)} %get-tuple-element.442), channel_id=1, source_target_pairs={{0,16},{4,20},{8,24},{12,28},{16,0},{20,4},{24,8},{28,12},{1,17},{... | collective-permute-start | bytes 3145736 | tf_op jit(solution)/shard_map/ppermute | solution.py:36
  587.8 65.0 %collective-permute-start.27 = (bf16[2,256,1536]{2,1,0:T(8,128)(2,1)S(1)}, bf16[2,256,1536]{2,1,0:T(8,128)(2,1)S(1)}, u32[]{:S(2)}, u32[]{:S(2)}) collective-permute-start(bf16[2,256,1536]{2,1,0:T(8,128)(2,1)S(1)} %get-tuple-element.426), channel_id=1, source_target_pairs={{0,8},{4,12},{8,0},{12,4},{16,24},{20,28},{24,16},{28,20},{1,9},{5... | collective-permute-start | bytes 4718600 | tf_op jit(solution)/shard_map/ppermute | solution.py:36
  588.6 85.4 %collective-permute-start.32 = (bf16[1,256,2048]{2,1,0:T(8,128)(2,1)}, bf16[1,256,2048]{2,1,0:T(8,128)(2,1)}, u32[]{:S(2)}, u32[]{:S(2)}) collective-permute-start(bf16[1,256,2048]{2,1,0:T(8,128)(2,1)} %get-tuple-element.440), channel_id=1, source_target_pairs={{0,16},{4,20},{8,24},{12,28},{16,0},{20,4},{24,8},{28,12},{1,17},{... | collective-permute-start | bytes 3145736 | tf_op jit(solution)/shard_map/ppermute | solution.py:36
  655.3 62.3 %collective-permute-start.28 = (bf16[1,256,1536]{2,1,0:T(8,128)(2,1)}, bf16[1,256,1536]{2,1,0:T(8,128)(2,1)}, u32[]{:S(2)}, u32[]{:S(2)}) collective-permute-start(bf16[1,256,1536]{2,1,0:T(8,128)(2,1)} %get-tuple-element.431), channel_id=1, source_target_pairs={{0,16},{4,20},{8,24},{12,28},{16,0},{20,4},{24,8},{28,12},{1,17},{... | collective-permute-start | bytes 2359304 | tf_op jit(solution)/shard_map/ppermute | solution.py:36
  659.3 51.3 %collective-permute-start.31 = (bf16[1,256,512]{2,1,0:T(8,128)(2,1)}, bf16[1,256,512]{2,1,0:T(8,128)(2,1)S(1)}, u32[]{:S(2)}, u32[]{:S(2)}) collective-permute-start(bf16[1,256,512]{2,1,0:T(8,128)(2,1)} %copy-done.122), channel_id=1, source_target_pairs={{0,16},{4,20},{8,24},{12,28},{16,0},{20,4},{24,8},{28,12},{1,17},{... | collective-permute-start | bytes 786440 | tf_op jit(solution)/shard_map/ppermute | solution.py:36
  671.0 44.2 %collective-permute-start.30 = (bf16[1,128,1024]{2,1,0:T(8,128)(2,1)}, bf16[1,128,1024]{2,1,0:T(8,128)(2,1)}, u32[]{:S(2)}, u32[]{:S(2)}) collective-permute-start(bf16[1,128,1024]{2,1,0:T(8,128)(2,1)} %get-tuple-element.436), channel_id=1, source_target_pairs={{0,16},{4,20},{8,24},{12,28},{16,0},{20,4},{24,8},{28,12},{1,17},{... | collective-permute-start | bytes 786440 | tf_op jit(solution)/shard_map/ppermute | solution.py:36
  (146 other events, 2634.5 us)

commit v3 on v2

--- a/solution.py
+++ b/solution.py
@@ -18,7 +18,7 @@
 PLAIN = (((1,), (0,)), ((), ()))
 OVER_ROWS = (((0,), (0,)), ((), ()))
 KIND, PART, GROUP, REAL, POS, SOURCE, BLOCK, RANK = 0, 1, 2, 4, 8, 12, 16, 32
-VMEM_BYTES = 28 * 1024 * 1024
+VMEM_BYTES = 14 * 1024 * 1024
 
 
 def dot(left, right, form=PLAIN):
@@ -40,16 +40,13 @@
     return [1 << i for i in range(size.bit_length() - 1)]
 
 
-def gather_rel(values):
-    size = lax.axis_size("mp")
-    pieces = {0: values}
-    for bit in reversed(bits_of(size)):
-        pieces[bit] = swap(values, "mp", bit)
-    for j in range(size):
-        if j not in pieces:
-            low = j & -j
-            pieces[j] = swap(pieces[j ^ low], "mp", low)
-    return [pieces[j] for j in range(size)]
+def gather_start(values):
+    far, near = swap(values, "mp", 2), swap(values, "mp", 1)
+    return [values, near, far]
+
+
+def gather_end(meta, pieces):
+    pieces.append(exchange(meta, (pieces[2], "mp", 1))[0])
 
 
 def add_low(first, second):
@@ -97,7 +94,7 @@
     channel = 0
 
 
-def call(body, meta, grid, ins, outs, scratch=(), aliases=None, remote=False, after=(), cost=1):
+def call(body, meta, grid, ins, outs, scratch=(), aliases=None, remote=False, after=(), cost=1, room=VMEM_BYTES):
     arrays, specs = [], []
     for item in ins:
         arrays.append(item[0])
@@ -129,11 +126,11 @@
         after.append(Order.mark)
     specs += [pl.BlockSpec(memory_space=pl.ANY)] * len(after)
 
-    params = pltpu.CompilerParams(vmem_limit_bytes=VMEM_BYTES)
+    params = pltpu.CompilerParams(vmem_limit_bytes=room)
     if remote:
         Order.channel += 1
         params = pltpu.CompilerParams(
-            vmem_limit_bytes=VMEM_BYTES, collective_id=Order.channel, has_side_effects=True
+            vmem_limit_bytes=room, collective_id=Order.channel, has_side_effects=True
         )
 
     def marked(meta_ref, *refs):
@@ -155,7 +152,7 @@
         input_output_aliases=aliases or {},
         compiler_params=params,
         cost_estimate=pl.CostEstimate(
-            flops=cost * 40000000, bytes_accessed=1024, transcendentals=0
+            flops=cost * 1000000, bytes_accessed=1024, transcendentals=0
         ),
         name=getattr(body, "func", body).__name__,
     )(meta, *arrays, *after)
@@ -971,8 +968,21 @@
     send_out[0] = (keep_ref[1].astype(F32) + got_ref[1].astype(F32)).astype(BF)
 
 
-def gathered_body(meta, left_ref, right_ref, out_ref):
-    out_ref[...] = dot(left_ref[...], right_ref[...], OVER_ROWS)
+def flat_body(meta, kinds, gain_in, gain_ffn, mid_near, mid_far, gain_ff, query_ref, flat_ref, rows_ref):
+    rows_ref[...] = jnp.zeros_like(rows_ref)
+    line = 0
+    lines = [jnp.where(meta[KIND] == c, kinds[...], 0.0) for c in range(3)]
+    lines += [gain_in[...], gain_ffn[...], mid_near[...] + mid_far[...], gain_ff[...]]
+    for value in lines:
+        for start in range(0, value.shape[1], LANES):
+            rows_ref[line : line + 1, :] = value[:, start : start + LANES]
+            line += 1
+    latent, wide = query_ref.shape
+    line = rows_ref.shape[0] - latent * wide // LANES
+    for start in range(0, wide, LANES):
+        rows_ref[line : line + latent, :] = query_ref[:, start : start + LANES]
+        line += latent
+    flat_ref[...] = rows_ref[...].astype(BF)
 
 
 def last_body(meta, keep_ref, got_ref, out_ref):
@@ -1186,7 +1196,7 @@
         [(text_embed, (rows // 4, width), row_block), (table,), (gain_in,)],
         [((rows, width), BF, (rows // 4, width), row_block)],
     )[0]
-    text_pieces = gather_rel(text_in)
+    text_pieces = gather_start(text_in)
 
 
     clip = clip_feats.reshape(images * patches, clip_width)
@@ -1202,17 +1212,9 @@
         ],
     )
     gathering = GatherDp(meta, pool_out)
-    cot = call(
-        copy_body,
-        meta,
-        (2,),
-        [(cotangent, (rows // 2, width), row_block)],
-        [((rows, width), BF, (rows // 2, width), row_block)],
-    )[0]
-    cot_pieces = gather_rel(cot)
-
     state = project(meta, text_pieces[:2], weight, turn, None, 0)
     gathering.step()
+    gather_end(meta, text_pieces)
     state = project(meta, text_pieces[2:], weight, turn, state, 2)
     gathering.step()
 
@@ -1226,7 +1228,6 @@
             [((rows, ff), BF, (rows, tile), lambda i, m: (0, i))] * 2,
         )
 
-    d_up_near = d_up_half(0)
     pool_rows = gathering.end().reshape(dp * images * latent, wide)
     slot_terms = call(
         functools.partial(pooled_body, slots=slots, mp=mp),
@@ -1242,6 +1243,15 @@
     )
     slot_own, slot_far = scatter_now(meta, *slot_terms)
     slot_pieces = gather_now(meta, add_low(slot_own, slot_far))
+
+    cot = call(
+        copy_body,
+        meta,
+        (2,),
+        [(cotangent, (rows // 2, width), row_block)],
+        [((rows, width), BF, (rows // 2, width), row_block)],
+    )[0]
+    cot_pieces = gather_start(cot)
 
     at_slot = lambda i, m: (m[POS + jnp.maximum(i - 3, 0)], 0)
     state = call(
@@ -1302,6 +1312,8 @@
     out_w = (out_weight, (wide, tile), lambda i, m: (0, i))
     out_far = swap(summed(out_body, mids, out_w, 2), "mp", 2)
     out_terms = [summed(out_body, mids, out_w, 0), out_far]
+    d_up_near = d_up_half(0)
+    gather_end(meta, cot_pieces)
     d_up = d_up_near + d_up_half(2)
     after_attn, ffn_in = call(
         after_body,
@@ -1312,7 +1324,7 @@
         + [(table,), (gain_ffn,)],
         [((rows, width), F32, few, row_block), ((rows, width), BF, few, row_block)],
     )
-    ffn_pieces = gather_rel(ffn_in)
+    ffn_pieces = gather_start(ffn_in)
 
     def up_half(which, before):
         lanes_of = lambda i, m: (0, i)
@@ -1340,6 +1352,7 @@
         )
 
     state = up_half(0, None)
+    gather_end(meta, ffn_pieces)
     act, slope, ff_stats = up_half(2, state)
     ff_stats = spread_stats(meta, ff_stats)
     cut = rows // 2
@@ -1365,6 +1378,7 @@
     down_grad = WeightGrads(meta, [(cot_pieces, [low], False, (0, 0))], (width // dp, ff))
     up_grad = WeightGrads(meta, [(ffn_pieces, [pre], False, (0, 0))], (width // dp, ff), 2)
     down_grad.start()
+    up_grad.start()
     back_far = swap(summed(back_body, pre, up_w, 2), "mp", 2)
     ffn_terms = [summed(back_body, pre, up_w, 0), back_far]
     d_after, d_after_low, gain_ffn_local = call(
@@ -1379,19 +1393,8 @@
             ((1, width), F32, None, None),
         ],
     )
-    after_pieces = gather_rel(d_after_low)
-    up_grad.start()
-
-    down_near, down_far = call(
-        down_body,
-        meta,
-        (steps,),
-        [(low,), (down_weight, (ff, tile), lambda i, m: (0, i))],
-        [((rows, width), BF, None, None)] * 2,
-        scratch=pair_scratch(2, steps, rows, tile),
-        remote=True,
-    )
-    down_far = swap(down_far, "mp", 2)
+    after_pieces = gather_start(d_after_low)
+
     def d_mid_half(which, before):
         block = lambda i, m: (m[PART] ^ (which + i), 0)
         lane_block = lambda i, m: (0, m[PART] ^ (which + i))
@@ -1415,17 +1418,31 @@
         )
 
     d_mid, mid_stats, gain_mid_near = d_mid_half(0, None)
+    down_near, down_far = call(
+        down_body,
+        meta,
+        (steps,),
+        [(low,), (down_weight, (ff, tile), lambda i, m: (0, i))],
+        [((rows, width), BF, None, None)] * 2,
+        scratch=pair_scratch(2, steps, rows, tile),
+        remote=True,
+    )
+    gather_end(meta, after_pieces)
     d_mid, mid_stats, gain_mid_far = d_mid_half(2, (d_mid, mid_stats))
     mid_stats = spread_stats(meta, mid_stats)
+    down_far = swap(
+        call(
+            copy_body,
+            meta,
+            (2,),
+            [(down_far, (rows // 2, width), row_block)],
+            [((rows, width), BF, (rows // 2, width), row_block)],
+        )[0],
+        "mp",
+        2,
+    )
     out_grad = WeightGrads(meta, [(after_pieces, [mids], False, (0, 0))], (width // dp, wide))
     out_grad.start()
-    layer_out = call(
-        sum_body,
-        meta,
-        (here,),
-        [(after_attn, few, row_block), (down_near, few, row_block), (down_far, few, row_block)],
-        [((rows, width), F32, few, row_block)],
-    )[0]
     down_grad.step()
     d_qkv = call(
         functools.partial(attend_back_body, mp=mp, width=width, block=rows),
@@ -1480,11 +1497,19 @@
         image_keep, image_send = split_sum(meta, image_keep, image_got)
         image_got = exchange(meta, (image_send, "dp", bit))[0]
         if bit == 2:
+            layer_out = call(
+                sum_body,
+                meta,
+                (here,),
+                [(after_attn, few, row_block), (down_near, few, row_block), (down_far, few, row_block)],
+                [((rows, width), F32, few, row_block)],
+            )[0]
+            out_grad.step()
             up_grad.step()
             in_grad.start()
             in_far = swap(row_terms(2), "mp", 2)
-            down_grad.step()
-            out_grad.step()
+    down_grad.step()
+    out_grad.step()
     owned = plus(meta, image_keep, image_got, BF).reshape(images, part, width)
     owned_pieces = gather_now(meta, owned)
     d_kv, query_local, clip_even, clip_odd, pool_grad = call(
@@ -1503,10 +1528,16 @@
         scratch=[pltpu.VMEM((images * patches, clip_width), F32)],
     )
     pool_grads = WeightGrads(
-        meta, [([clip], [d_kv], False, (0, 0))], (clip_width // dp, 2 * wide)
-    )
+        meta,
+        [
+            ([pool_grad], [pool_out], False, (0, 0)),
+            ([clip], [d_kv], True, (1, 0)),
+        ],
+        (width // dp + 2 * (clip_width // dp), wide),
+    )
+    down_grad.finish()
+    in_grad.step()
     pool_grads.start()
-    up_grad.step()
     in_terms = [row_terms(0), in_far]
     text_grad, gain_in_local, type_local = call(
         in_back_body,
@@ -1521,55 +1552,46 @@
             ((1, width), F32, None, None),
         ],
     )
-    kind = (jnp.arange(3) == meta[KIND]).astype(F32)[:, None]
-    over_all = jnp.concatenate([kind * type_local, gain_in_local, gain_ffn_local])
-    flat = jnp.concatenate(
-        [
-            over_all.reshape(-1),
-            (gain_mid_near + gain_mid_far)[0],
-            gain_ff_local[0],
-            query_local.reshape(-1),
-        ]
-    ).reshape(-1, LANES)
-    group = lax.axis_index("dp")
-    columns = pool_grad.reshape(images * latent, dp, width // dp).swapaxes(0, 1)
-    columns = pick(columns, [group ^ k for k in range(dp)])
+    down_grad.finish()
     hops = bits_of(dp)[1:] + [1]
-    for bit in hops:
-        cut = columns.reshape((-1, 2, bit) + columns.shape[1:])
-        stay, send = halve(cut, 1)
-        got, flat_got = exchange(meta, (send, "dp", bit), (flat, "dp", bit))
-        flat = plus(meta, flat, flat_got, F32)
-        columns = jnp.stack([stay, got], axis=1).reshape(columns.shape)
-        if bit == hops[-2]:
+    small = (type_local, gain_in_local, gain_ffn_local, gain_mid_near, gain_mid_far, gain_ff_local)
+    sizes = 5 * width + wide + ff
+    lines = -(-sizes // (16 * LANES)) * 16 + latent * wide // LANES
+    flat = call(
+        flat_body,
+        meta,
+        (1,),
+        [(x,) for x in small] + [(query_local,)],
+        [((lines, LANES), BF, None, None)],
+        scratch=[pltpu.VMEM((lines, LANES), F32)],
+    )[0]
+    for n, bit in enumerate(hops):
+        got = swap(flat, "dp", bit)
+        if n == 0:
+            up_grad.step()
+            clip_even = add_low(clip_even, exchange(meta, (clip_odd, "mp", 1))[0])
+            clip_far = exchange(meta, (clip_even[1], "mp", 2))[0]
+        elif n == len(hops) - 2:
+            pool_grads.step()
             in_grad.step()
-            out_grad.step()
+        elif n == len(hops) - 1:
+            up_grad.finish()
             pool_grads.step()
-    clip_even = add_low(clip_even, exchange(meta, (clip_odd, "mp", 1))[0])
-    clip_far, flat_far, flat_near = exchange(
-        meta, (clip_even[1], "mp", 2), (flat, "mp", 2), (flat, "mp", 1)
-    )
+        flat = plus(meta, flat, got, BF)
+    flat_far, flat_near = exchange(meta, (flat, "mp", 2), (flat, "mp", 1))
     flat_last = exchange(meta, (flat_far, "mp", 1))[0]
-    res_out_grad = call(
-        gathered_body,
-        meta,
-        (1,),
-        [(pool_rows,), (columns.reshape(dp * images * latent, width // dp),)],
-        [((wide, width // dp), F32, None, None)],
-    )[0]
-    in_grad.step()
-    pool_grads.step()
-    down_grad.finish()
-    up_grad.finish()
     out_grad.finish()
     pool_grads.finish()
     in_grad.finish()
     clip_grad = clip_even[0].astype(F32) + clip_far.astype(F32)
-    flat = by_mp(jnp.stack([flat, flat_near, flat_far, flat_last])).reshape(mp, -1)
-    sums = jnp.sum(flat[:, : 5 * width].reshape(mp, 5, width), axis=0)
-    parts = flat[:, 5 * width :]
-    query_grad = jnp.swapaxes(parts[:, wide + ff :].reshape(mp, latent, wide), 0, 1)
-    kv_grad = pool_grads.end()[0]
+    flat = by_mp(jnp.stack([flat, flat_near, flat_far, flat_last])).astype(F32)
+    edge = flat.shape[1] - latent * wide // LANES
+    parts = flat[:, :edge].reshape(mp, -1)
+    sums = jnp.sum(parts[:, : 5 * width].reshape(mp, 5, width), axis=0)
+    parts = parts[:, 5 * width :]
+    query_grad = flat[:, edge:].reshape(mp, wide // LANES, latent, LANES).swapaxes(1, 2)
+    query_grad = jnp.swapaxes(query_grad.reshape(mp, latent, wide), 0, 1)
+    res_out_grad, kv_grad = pool_grads.end()
     qkv_grad, out_grad = in_grad.end()[0], out_grad.end()[0]
     return (
         layer_out,
@@ -1587,7 +1609,7 @@
         query_grad.reshape(latent, width),
         kv_grad[:, :wide],
         kv_grad[:, wide:],
-        res_out_grad,
+        res_out_grad.T,
     )
 
 

time: 732 us -> 672 us (0.918)
  Pallas kernels: 487 us -> 403 us
  waiting for transfers between devices: 119 us -> 165 us
  local copies, waits for them, and re-layouts: 66.9 us -> 44 us
    pallas_call x81 -> x87, Pallas kernels: 485 us -> 401 us  [call(): pl.pallas_call(marked, out_shape=shapes, grid_spec=pltpu.PrefetchScalarGr...]
    ppermute x34 -> x33, waiting for transfers between devices: 119 us -> 165 us  [swap(): return lax.ppermute(values, axis, [(i, i ^ bit) for i in range(size)])]
    unnamed x293 -> x210, local copies, waits for them, and re-layouts: 60.4 us -> 39 us
    ppermute x34 -> x33, starting transfers between devices: 36.5 us -> 40.2 us  [swap(): return lax.ppermute(values, axis, [(i, i ^ bit) for i in range(size)])]
  transfers between devices with their start and end apart: 34 -> 33, of which waited for: 10 -> 13; matrix products, arithmetic and copies ran while one was open for 3% -> 3% of each run, Pallas kernels for 62% -> 51%
where the time goes in v3:
time: 672 us; the launch traced here: 663 us
  Pallas kernels  403 us (60%)
  waiting for transfers between devices  165 us (25%)
  local copies, waits for them, and re-layouts  44 us (7%)
  starting transfers between devices  40.2 us (6%)
  other arithmetic  8.47 us (1%)
    pallas_call x87, Pallas kernels, call(): pl.pallas_call(marked, out_shape=shapes, grid_spec=pltpu.PrefetchScalarGr...  401 us
    ppermute x33, waiting for transfers between devices, swap(): return lax.ppermute(values, axis, [(i, i ^ bit) for i in range(size)])  165 us
    ppermute x33, starting transfers between devices, swap(): return lax.ppermute(values, axis, [(i, i ^ bit) for i in range(size)])  40.2 us
    unnamed x210, local copies, waits for them, and re-layouts  39 us
  transfers between devices with their start and end apart: 33, of which 13 were waited for; matrix products, arithmetic and copies ran while one was open for 3% of the time, Pallas kernels for 51%

profile of v3, /device:TPU:0, one launch (start us, length us, event | category | flops | bytes accessed | tf_op | source)
XLA Modules:
  0.0 663.0 jit_solution(3510292613291825830)
XLA Ops:
  50.9 12.5 %collective-permute-done.4.refs_1_ = bf16[4,128,512]{2,1,0:T(8,128)(2,1)S(1)} collective-permute-done((bf16[4,128,512]{2,1,0:T(8,128)(2,1)S(1)}, bf16[4,128,512]{2,1,0:T(8,128)(2,1)S(1)}, u32[]{:S(2)}, u32[]{:S(2)}) %collective-permute-start.4) | collective-permute-done | bytes 524320 | tf_op jit(solution)/shard_map/ppermute | solution.py:36
  68.1 8.9 %body.24 = (bf16[4,16,2048]{2,1,0:T(8,128)(2,1)S(1)}, f32[8,128]{1,0:T(8,128)S(1)}) custom-call(s32[48]{0:T(128)S(1)} %copy-done.67, bf16[4,16,2048]{2,1,0:T(8,128)(2,1)S(1)} %slice_bitcast_fusion.5.refs_0_, f32[8,128]{1,0:T(8,128)S(1)} %get-tuple-element.263.refs_1_), custom_call_target="tpu_custom_call" | custom-call | flops 1000000 | bytes 1024 | tf_op jit(solution)/shard_map/body/pallas_call | solution.py:142
  77.1 8.1 %body.25 = (bf16[4,16,2048]{2,1,0:T(8,128)(2,1)S(1)}, bf16[4,16,2048]{2,1,0:T(8,128)(2,1)S(1)}, f32[8,128]{1,0:T(8,128)S(1)}) custom-call(s32[48]{0:T(128)S(1)} %copy-done.67, bf16[4,16,2048]{2,1,0:T(8,128)(2,1)S(1)} %fusion.refs_0_.refs_1_, bf16[4,16,2048]{2,1,0:T(8,128)(2,1)S(1)} %fusion.refs_0_.refs_1_, f32[8,128]{1,0:T(8,128)S(1)} %get-tuple-element.265.refs_2_), custom_call_target="tpu_custom_call" | custom-call | flops 1000000 | bytes 1024 | tf_op jit(solution)/shard_map/body/pallas_call | solution.py:142
  97.0 15.2 %attend_body.1 = (bf16[1024,512]{1,0:T(8,128)(2,1)S(1)}, f32[8,1024]{1,0:T(8,128)S(1)}, f32[8,1024]{1,0:T(8,128)S(1)}, f32[8,128]{1,0:T(8,128)S(1)}) custom-call(s32[48]{0:T(128)S(1)} %copy-done.67, bf16[1024,1536]{1,0:T(8,128)(2,1)S(1)} %get-tuple-element.274.refs_0_, f32[8,128]{1,0:T(8,128)S(1)} %get-tuple-element.275.refs_1_), custom_call_target="tpu_custom_call" | custom-call | flops 1000000 | bytes 1024 | tf_op jit(solution)/shard_map/attend_body/pallas_call | solution.py:142
  156.0 10.6 %up_body.2 = (bf16[1024,2048]{1,0:T(8,128)(2,1)S(1)}, bf16[1024,2048]{1,0:T(8,128)(2,1)S(1)}, f32[8,1024]{1,0:T(8,128)S(1)}, f32[8,128]{1,0:T(8,128)S(1)}) custom-call(s32[48]{0:T(128)S(1)} %copy-done.67, bf16[256,2048]{1,0:T(8,128)(2,1)S(1)} %get-tuple-element.296.refs_0_, bf16[256,2048]{1,0:T(8,128)(2,1)S(1)} %collective-permute-done.9.refs_1_, ...), custom_call_target="tpu_custom_call" | custom-call | flops 1000000 | bytes 1024 | tf_op jit(solution)/shard_map/up_body/pallas_call | solution.py:142
  166.6 12.2 %collective-permute-done.8.refs_0_.refs_2_ = bf16[256,2048]{1,0:T(8,128)(2,1)S(1)} collective-permute-done((bf16[256,2048]{1,0:T(8,128)(2,1)S(1)}, bf16[256,2048]{1,0:T(8,128)(2,1)S(1)}, u32[]{:S(2)}, u32[]{:S(2)}) %collective-permute-start.8) | collective-permute-done | bytes 1048608 | tf_op jit(solution)/shard_map/ppermute | solution.py:36
  182.1 10.2 %up_body.3 = (bf16[1024,2048]{1,0:T(8,128)(2,1)S(1)}, bf16[1024,2048]{1,0:T(8,128)(2,1)S(1)}, f32[8,1024]{1,0:T(8,128)S(1)}, f32[8,128]{1,0:T(8,128)S(1)}) custom-call(s32[48]{0:T(128)S(1)} %copy-done.67, bf16[256,2048]{1,0:T(8,128)(2,1)S(1)} %collective-permute-done.8.refs_0_.refs_2_, ...), custom_call_target="tpu_custom_call", output_to_operand_aliasing={{0}: (7, {}), {1}: (8, {}), {2}: (9, {})} | custom-call | flops 1000000 | bytes 1024 | tf_op jit(solution)/shard_map/up_body/pallas_call | solution.py:142
  209.1 8.0 %spread_body.1 = (bf16[1024,2048]{1,0:T(8,128)(2,1)S(1)}, bf16[1024,2048]{1,0:T(8,128)(2,1)S(1)}, f32[1,2048]{1,0:T(1,128)S(1)}, f32[8,128]{1,0:T(8,128)S(1)}) custom-call(s32[48]{0:T(128)S(1)} %copy-done.67, bf16[1024,2048]{1,0:T(8,128)(2,1)S(1)} %copy-done.15, bf16[1024,2048]{1,0:T(8,128)(2,1)S(1)} %copy-done.17, bf16[256,2048]{1,0:T(8,128)(2,1)S(1)} %copy-done.63, ...), custom_call_target="tpu_custom_call" | custom-call | flops 1000000 | bytes 1024 | tf_op jit(solution)/shard_map/spread_body/pallas_call | solution.py:142
  242.7 7.5 %back_body.3 = (bf16[256,2048]{1,0:T(8,128)(2,1)S(1)}, f32[8,128]{1,0:T(8,128)S(1)}) custom-call(s32[48]{0:T(128)S(1)} %copy-done.67, bf16[1024,2048]{1,0:T(8,128)(2,1)S(1)} %get-tuple-element.317.refs_4_.refs_0_, bf16[2048,2048]{1,0:T(8,128)(2,1)S(1)} %bitcast.81, f32[8,128]{1,0:T(8,128)S(1)} %get-tuple-element.321.refs_2_), custom_call_target="tpu_custom_call" | custom-call | flops 1000000 | bytes 1024 | tf_op jit(solution)/shard_map/back_body/pallas_call | solution.py:142
  250.2 17.1 %collective-permute-done.10.refs_1_ = bf16[256,2048]{1,0:T(8,128)(2,1)S(1)} collective-permute-done((bf16[256,2048]{1,0:T(8,128)(2,1)S(1)}, bf16[256,2048]{1,0:T(8,128)(2,1)S(1)}, u32[]{:S(2)}, u32[]{:S(2)}) %collective-permute-start.10) | collective-permute-done | bytes 1048608 | tf_op jit(solution)/shard_map/ppermute | solution.py:36
  276.7 13.2 %down_body.1 = (bf16[256,2048]{1,0:T(8,128)(2,1)S(1)}, bf16[256,2048]{1,0:T(8,128)(2,1)S(1)}, f32[8,128]{1,0:T(8,128)S(1)}) custom-call(s32[48]{0:T(128)S(1)} %copy-done.67, bf16[1024,2048]{1,0:T(8,128)(2,1)S(1)} %get-tuple-element.316.refs_4_.refs_0_, bf16[2048,2048]{1,0:T(8,128)(2,1)S(1)} %bitcast.83, f32[8,128]{1,0:T(8,128)S(1)} %get-tuple-element.327.refs_2_), custom_call_target="tpu_custom_call" | custom-call | flops 1000000 | bytes 1024 | tf_op jit(solution)/shard_map/down_body/pallas_call | solution.py:142
  319.2 8.0 %weight_body.15 = (bf16[2,256,2048]{2,1,0:T(8,128)(2,1)S(1)}, bf16[2,256,2048]{2,1,0:T(8,128)(2,1)S(1)}, f32[8,128]{1,0:T(8,128)S(1)}) custom-call(s32[48]{0:T(128)S(1)} %copy-done.67, bf16[256,2048]{1,0:T(8,128)(2,1)S(1)} %copy-done.32, bf16[256,2048]{1,0:T(8,128)(2,1)S(1)} %copy-done.35, bf16[256,2048]{1,0:T(8,128)(2,1)S(1)} %copy-done.11, ...), custom_call_target="tpu_custom_call" | custom-call | flops 1000000 | bytes 1024 | tf_op jit(solution)/shard_map/weight_body/pallas_call | solution.py:142
  327.7 20.8 %attend_back_body.1 = (bf16[1024,1536]{1,0:T(8,128)(2,1)S(1)}, f32[8,128]{1,0:T(8,128)S(1)}) custom-call(s32[48]{0:T(128)S(1)} %copy-done.67, bf16[1024,1536]{1,0:T(8,128)(2,1)S(1)} %copy-done.3, bf16[1024,512]{1,0:T(8,128)(2,1)S(1)} %copy-done.13, bf16[1024,512]{1,0:T(8,128)(2,1)S(1)} %copy-done.51, f32[8,1024]{1,0:T(8,128)S(1)} %get-tuple-element.340.refs_3_, ...), custom_call_target="tpu_custom_call" | custom-call | flops 1000000 | bytes 1024 | tf_op jit(solution)/shard_map/attend_back_body/pallas_call | solution.py:142
  353.6 8.9 %body.34 = (bf16[4,16,2048]{2,1,0:T(8,128)(2,1)S(1)}, f32[8,128]{1,0:T(8,128)S(1)}) custom-call(s32[48]{0:T(128)S(1)} %copy-done.67, bf16[4,16,2048]{2,1,0:T(8,128)(2,1)S(1)} %get-tuple-element.520.refs_0_, f32[8,128]{1,0:T(8,128)S(1)} %get-tuple-element.354.refs_1_), custom_call_target="tpu_custom_call" | custom-call | flops 1000000 | bytes 1024 | tf_op jit(solution)/shard_map/body/pallas_call | solution.py:142
  364.4 13.7 %body.35 = (bf16[4,32,2048]{2,1,0:T(8,128)(2,1)S(1)}, f32[8,128]{1,0:T(8,128)S(1)}) custom-call(s32[48]{0:T(128)S(1)} %copy-done.67, bf16[4,32,2048]{2,1,0:T(8,128)(2,1)S(1)} %get-tuple-element.358.refs_0_, f32[8,128]{1,0:T(8,128)S(1)} %get-tuple-element.359.refs_1_), custom_call_target="tpu_custom_call" | custom-call | flops 1000000 | bytes 1024 | tf_op jit(solution)/shard_map/body/pallas_call | solution.py:142
  391.6 8.1 %weight_body.17 = (bf16[2,256,2048]{2,1,0:T(8,128)(2,1)S(1)}, bf16[2,256,2048]{2,1,0:T(8,128)(2,1)S(1)}, f32[8,128]{1,0:T(8,128)S(1)}) custom-call(s32[48]{0:T(128)S(1)} %copy-done.67, bf16[256,2048]{1,0:T(8,128)(2,1)S(1)} %copy-done.41, bf16[256,2048]{1,0:T(8,128)(2,1)S(1)} %copy-done.44, bf16[256,2048]{1,0:T(8,128)(2,1)S(1)} %copy-done.8, ...), custom_call_target="tpu_custom_call" | custom-call | flops 1000000 | bytes 1024 | tf_op jit(solution)/shard_map/weight_body/pallas_call | solution.py:142
  414.0 9.8 %body.37 = (bf16[1,32,2048]{2,1,0:T(8,128)(2,1)S(1)}, f32[8,128]{1,0:T(8,128)S(1)}) custom-call(s32[48]{0:T(128)S(1)} %copy-done.67, bf16[1,32,2048]{2,1,0:T(8,128)(2,1)S(1)} %get-tuple-element.377.refs_0_, f32[8,128]{1,0:T(8,128)S(1)} %get-tuple-element.378.refs_1_), custom_call_target="tpu_custom_call" | custom-call | flops 1000000 | bytes 1024 | tf_op jit(solution)/shard_map/body/pallas_call | solution.py:142
  427.4 31.1 %collective-permute-done.17.refs_1_ = bf16[2,256,512]{2,1,0:T(8,128)(2,1)S(1)} collective-permute-done((bf16[2,256,512]{2,1,0:T(8,128)(2,1)S(1)}, bf16[2,256,512]{2,1,0:T(8,128)(2,1)S(1)}, u32[]{:S(2)}, u32[]{:S(2)}) %collective-permute-start.17) | collective-permute-done | bytes 524320 | tf_op jit(solution)/shard_map/ppermute | solution.py:36
  467.9 8.6 %pool_back_body.1 = (bf16[512,1024]{1,0:T(8,128)(2,1)S(1)}, f32[64,512]{1,0:T(8,128)S(1)}, bf16[2,2,64,1024]{3,2,1,0:T(8,128)(2,1)S(1)}, bf16[2,2,64,1024]{3,2,1...) custom-call(s32[48]{0:T(128)S(1)} %copy-done.67, bf16[2,16,2048]{2,1,0:T(8,128)(2,1)S(1)} %bitcast.100, ...), custom_call_target="tpu_custom_call" | custom-call | flops 1000000 | bytes 1024 | tf_op jit(solution)/shard_map/pool_back_body/pallas_call | solution.py:142
  500.0 14.3 %collective-permute-done.21.refs_1_ = bf16[256,2048]{1,0:T(8,128)(2,1)S(1)} collective-permute-done((bf16[256,2048]{1,0:T(8,128)(2,1)S(1)}, bf16[256,2048]{1,0:T(8,128)(2,1)S(1)}, u32[]{:S(2)}, u32[]{:S(2)}) %collective-permute-start.21) | collective-permute-done | bytes 1048608 | tf_op jit(solution)/shard_map/ppermute | solution.py:36
  527.1 13.4 %body.41 = (bf16[2,64,1024]{2,1,0:T(8,128)(2,1)S(1)}, f32[8,128]{1,0:T(8,128)S(1)}) custom-call(s32[48]{0:T(128)S(1)} %copy-done.67, bf16[2,64,1024]{2,1,0:T(8,128)(2,1)S(1)} %slice_bitcast_fusion.1.refs_0_, f32[8,128]{1,0:T(8,128)S(1)} %get-tuple-element.428.refs_1_), custom_call_target="tpu_custom_call" | custom-call | flops 1000000 | bytes 1024 | tf_op jit(solution)/shard_map/body/pallas_call | solution.py:142
  541.9 20.3 %collective-permute-done.26.refs_2_ = bf16[4,512,512]{2,1,0:T(8,128)(2,1)S(1)} collective-permute-done((bf16[4,512,512]{2,1,0:T(8,128)(2,1)S(1)}, bf16[4,512,512]{2,1,0:T(8,128)(2,1)S(1)}, u32[]{:S(2)}, u32[]{:S(2)}) %collective-permute-start.26) | collective-permute-done | bytes 2097184 | tf_op jit(solution)/shard_map/ppermute | solution.py:36
  575.2 18.9 %collective-permute-done.24.refs_1_ = bf16[368,128]{1,0:T(8,128)(2,1)} collective-permute-done((bf16[368,128]{1,0:T(8,128)(2,1)S(1)}, bf16[368,128]{1,0:T(8,128)(2,1)}, u32[]{:S(2)}, u32[]{:S(2)}) %collective-permute-start.24) | collective-permute-done | bytes 94240 | tf_op jit(solution)/shard_map/ppermute | solution.py:36
  637.4 17.4 %collective-permute-done.31 = bf16[1,512,512]{2,1,0:T(8,128)(2,1)S(1)} collective-permute-done((bf16[1,512,512]{2,1,0:T(8,128)(2,1)}, bf16[1,512,512]{2,1,0:T(8,128)(2,1)S(1)}, u32[]{:S(2)}, u32[]{:S(2)}) %collective-permute-start.31) | collective-permute-done | bytes 524320 | tf_op jit(solution)/shard_map/ppermute | solution.py:36
  (375 shorter events, 343.1 us)
Async XLA Ops:
  9.8 29.7 %collective-permute-start.3 = (bf16[256,2048]{1,0:T(8,128)(2,1)S(1)}, bf16[256,2048]{1,0:T(8,128)(2,1)S(1)}, u32[]{:S(2)}, u32[]{:S(2)}) collective-permute-start(bf16[256,2048]{1,0:T(8,128)(2,1)S(1)} %get-tuple-element.245.refs_0_), channel_id=1, source_target_pairs={{0,2},{1,3},{2,0},{3,1},{4,6},{5,7},{6,4},{7,5},{8,10},{9,11},{10,... | collective-permute-start | bytes 3145736 | tf_op jit(solution)/shard_map/ppermute | solution.py:36
  88.0 47.8 %collective-permute-start.6 = (bf16[256,2048]{1,0:T(8,128)(2,1)S(1)}, bf16[256,2048]{1,0:T(8,128)(2,1)S(1)}, u32[]{:S(2)}, u32[]{:S(2)}) collective-permute-start(bf16[256,2048]{1,0:T(8,128)(2,1)S(1)} %get-tuple-element.289.refs_0_), channel_id=1, source_target_pairs={{0,2},{1,3},{2,0},{3,1},{4,6},{5,7},{6,4},{7,5},{8,10},{9,11},{10,... | collective-permute-start | bytes 3145736 | tf_op jit(solution)/shard_map/ppermute | solution.py:36
  89.6 40.3 %collective-permute-start.7 = (bf16[256,2048]{1,0:T(8,128)(2,1)S(1)}, bf16[256,2048]{1,0:T(8,128)(2,1)S(1)}, u32[]{:S(2)}, u32[]{:S(2)}) collective-permute-start(bf16[256,2048]{1,0:T(8,128)(2,1)S(1)} %get-tuple-element.289.refs_0_), channel_id=1, source_target_pairs={{0,1},{1,0},{2,3},{3,2},{4,5},{5,4},{6,7},{7,6},{8,9},{9,8},{10,11... | collective-permute-start | bytes 3145736 | tf_op jit(solution)/shard_map/ppermute | solution.py:36
  124.7 25.3 %collective-permute-start.5 = (bf16[256,2048]{1,0:T(8,128)(2,1)S(1)}, bf16[256,2048]{1,0:T(8,128)(2,1)S(1)}, u32[]{:S(2)}, u32[]{:S(2)}) collective-permute-start(bf16[256,2048]{1,0:T(8,128)(2,1)S(1)} %get-tuple-element.287), channel_id=1, source_target_pairs={{0,2},{1,3},{2,0},{3,1},{4,6},{5,7},{6,4},{7,5},{8,10},{9,11},{10,... | collective-permute-start | bytes 3145736 | tf_op jit(solution)/shard_map/ppermute | solution.py:36
  153.3 25.6 %collective-permute-start.8 = (bf16[256,2048]{1,0:T(8,128)(2,1)S(1)}, bf16[256,2048]{1,0:T(8,128)(2,1)S(1)}, u32[]{:S(2)}, u32[]{:S(2)}) collective-permute-start(bf16[256,2048]{1,0:T(8,128)(2,1)S(1)} %get-tuple-element.296.refs_0_), channel_id=1, source_target_pairs={{0,2},{1,3},{2,0},{3,1},{4,6},{5,7},{6,4},{7,5},{8,10},{9,11},{10,... | collective-permute-start | bytes 3145736 | tf_op jit(solution)/shard_map/ppermute | solution.py:36
  225.4 93.7 %collective-permute-start.14 = (bf16[4,256,2048]{2,1,0:T(8,128)(2,1)}, bf16[4,256,2048]{2,1,0:T(8,128)(2,1)}, u32[]{:S(2)}, u32[]{:S(2)}) collective-permute-start(bf16[4,256,2048]{2,1,0:T(8,128)(2,1)} %get-tuple-element.344), channel_id=1, source_target_pairs={{0,4},{4,0},{8,12},{12,8},{16,20},{20,16},{24,28},{28,24},{1,5},{5... | collective-permute-start | bytes 12582920 | tf_op jit(solution)/shard_map/ppermute | solution.py:36
  234.1 157.5 %collective-permute-start.15 = (bf16[4,256,2048]{2,1,0:T(8,128)(2,1)}, bf16[4,256,2048]{2,1,0:T(8,128)(2,1)}, u32[]{:S(2)}, u32[]{:S(2)}) collective-permute-start(bf16[4,256,2048]{2,1,0:T(8,128)(2,1)} %get-tuple-element.369), channel_id=1, source_target_pairs={{0,8},{4,12},{8,0},{12,4},{16,24},{20,28},{24,16},{28,20},{1,9},{5... | collective-permute-start | bytes 12582920 | tf_op jit(solution)/shard_map/ppermute | solution.py:36
  242.0 25.3 %collective-permute-start.10 = (bf16[256,2048]{1,0:T(8,128)(2,1)S(1)}, bf16[256,2048]{1,0:T(8,128)(2,1)S(1)}, u32[]{:S(2)}, u32[]{:S(2)}) collective-permute-start(bf16[256,2048]{1,0:T(8,128)(2,1)S(1)} %get-tuple-element.323), channel_id=1, source_target_pairs={{0,2},{1,3},{2,0},{3,1},{4,6},{5,7},{6,4},{7,5},{8,10},{9,11},{10,... | collective-permute-start | bytes 3145736 | tf_op jit(solution)/shard_map/ppermute | solution.py:36
  271.1 25.6 %collective-permute-start.12 = (bf16[256,2048]{1,0:T(8,128)(2,1)S(1)}, bf16[256,2048]{1,0:T(8,128)(2,1)S(1)}, u32[]{:S(2)}, u32[]{:S(2)}) collective-permute-start(bf16[256,2048]{1,0:T(8,128)(2,1)S(1)} %get-tuple-element.325.refs_0_.refs_5_), channel_id=1, source_target_pairs={{0,2},{1,3},{2,0},{3,1},{4,6},{5,7},{6,4},{7,5},{8,10},{9,11},{10,... | collective-permute-start | bytes 3145736 | tf_op jit(solution)/shard_map/ppermute | solution.py:36
  310.0 76.0 %collective-permute-start.13 = (bf16[256,2048]{1,0:T(8,128)(2,1)}, bf16[256,2048]{1,0:T(8,128)(2,1)S(1)}, u32[]{:S(2)}, u32[]{:S(2)}) collective-permute-start(bf16[256,2048]{1,0:T(8,128)(2,1)} %get-tuple-element.338), channel_id=1, source_target_pairs={{0,2},{1,3},{2,0},{3,1},{4,6},{5,7},{6,4},{7,5},{8,10},{9,11},{10,... | collective-permute-start | bytes 3145736 | tf_op jit(solution)/shard_map/ppermute | solution.py:36
  313.5 75.1 %collective-permute-start.16 = (bf16[4,256,512]{2,1,0:T(8,128)(2,1)S(1)}, bf16[4,256,512]{2,1,0:T(8,128)(2,1)S(1)}, u32[]{:S(2)}, u32[]{:S(2)}) collective-permute-start(bf16[4,256,512]{2,1,0:T(8,128)(2,1)S(1)} %get-tuple-element.370), channel_id=1, source_target_pairs={{0,4},{4,0},{8,12},{12,8},{16,20},{20,16},{24,28},{28,24},{1,5},{5... | collective-permute-start | bytes 3145736 | tf_op jit(solution)/shard_map/ppermute | solution.py:36
  327.2 96.6 %collective-permute-start.18 = (bf16[2,256,2048]{2,1,0:T(8,128)(2,1)S(1)}, bf16[2,256,2048]{2,1,0:T(8,128)(2,1)S(1)}, u32[]{:S(2)}, u32[]{:S(2)}) collective-permute-start(bf16[2,256,2048]{2,1,0:T(8,128)(2,1)S(1)} %get-tuple-element.383), channel_id=1, source_target_pairs={{0,8},{4,12},{8,0},{12,4},{16,24},{20,28},{24,16},{28,20},{1,9},{5... | collective-permute-start | bytes 6291464 | tf_op jit(solution)/shard_map/ppermute | solution.py:36
  404.7 73.8 %collective-permute-start.19 = (bf16[4,256,1536]{2,1,0:T(8,128)(2,1)S(1)}, bf16[4,256,1536]{2,1,0:T(8,128)(2,1)S(1)}, u32[]{:S(2)}, u32[]{:S(2)}) collective-permute-start(bf16[4,256,1536]{2,1,0:T(8,128)(2,1)S(1)} %get-tuple-element.398), channel_id=1, source_target_pairs={{0,4},{4,0},{8,12},{12,8},{16,20},{20,16},{24,28},{28,24},{1,5},{5... | collective-permute-start | bytes 9437192 | tf_op jit(solution)/shard_map/ppermute | solution.py:36
  424.9 51.6 %collective-permute-start.20 = (bf16[1,256,2048]{2,1,0:T(8,128)(2,1)S(1)}, bf16[1,256,2048]{2,1,0:T(8,128)(2,1)S(1)}, u32[]{:S(2)}, u32[]{:S(2)}) collective-permute-start(bf16[1,256,2048]{2,1,0:T(8,128)(2,1)S(1)} %get-tuple-element.400), channel_id=1, source_target_pairs={{0,16},{4,20},{8,24},{12,28},{16,0},{20,4},{24,8},{28,12},{1,17},{... | collective-permute-start | bytes 3145736 | tf_op jit(solution)/shard_map/ppermute | solution.py:36
  425.0 33.4 %collective-permute-start.17 = (bf16[2,256,512]{2,1,0:T(8,128)(2,1)S(1)}, bf16[2,256,512]{2,1,0:T(8,128)(2,1)S(1)}, u32[]{:S(2)}, u32[]{:S(2)}) collective-permute-start(bf16[2,256,512]{2,1,0:T(8,128)(2,1)S(1)} %get-tuple-element.381), channel_id=1, source_target_pairs={{0,8},{4,12},{8,0},{12,4},{16,24},{20,28},{24,16},{28,20},{1,9},{5... | collective-permute-start | bytes 1572872 | tf_op jit(solution)/shard_map/ppermute | solution.py:36
  426.9 95.2 %collective-permute-start.22 = (bf16[2,256,2048]{2,1,0:T(8,128)(2,1)}, bf16[2,256,2048]{2,1,0:T(8,128)(2,1)S(1)}, u32[]{:S(2)}, u32[]{:S(2)}) collective-permute-start(bf16[2,256,2048]{2,1,0:T(8,128)(2,1)} %copy-done.87), channel_id=1, source_target_pairs={{0,4},{4,0},{8,12},{12,8},{16,20},{20,16},{24,28},{28,24},{1,5},{5... | collective-permute-start | bytes 6291464 | tf_op jit(solution)/shard_map/ppermute | solution.py:36
  488.8 73.4 %collective-permute-start.26 = (bf16[4,512,512]{2,1,0:T(8,128)(2,1)S(1)}, bf16[4,512,512]{2,1,0:T(8,128)(2,1)S(1)}, u32[]{:S(2)}, u32[]{:S(2)}) collective-permute-start(bf16[4,512,512]{2,1,0:T(8,128)(2,1)S(1)} %get-tuple-element.435), channel_id=1, source_target_pairs={{0,4},{4,0},{8,12},{12,8},{16,20},{20,16},{24,28},{28,24},{1,5},{5... | collective-permute-start | bytes 6291464 | tf_op jit(solution)/shard_map/ppermute | solution.py:36
  489.3 24.9 %collective-permute-start.21 = (bf16[256,2048]{1,0:T(8,128)(2,1)S(1)}, bf16[256,2048]{1,0:T(8,128)(2,1)S(1)}, u32[]{:S(2)}, u32[]{:S(2)}) collective-permute-start(bf16[256,2048]{1,0:T(8,128)(2,1)S(1)} %get-tuple-element.408), channel_id=1, source_target_pairs={{0,2},{1,3},{2,0},{3,1},{4,6},{5,7},{6,4},{7,5},{8,10},{9,11},{10,... | collective-permute-start | bytes 3145736 | tf_op jit(solution)/shard_map/ppermute | solution.py:36
  490.5 82.3 %collective-permute-start.25 = (bf16[2,256,1536]{2,1,0:T(8,128)(2,1)}, bf16[2,256,1536]{2,1,0:T(8,128)(2,1)}, u32[]{:S(2)}, u32[]{:S(2)}) collective-permute-start(bf16[2,256,1536]{2,1,0:T(8,128)(2,1)} %get-tuple-element.434), channel_id=1, source_target_pairs={{0,8},{4,12},{8,0},{12,4},{16,24},{20,28},{24,16},{28,20},{1,9},{5... | collective-permute-start | bytes 4718600 | tf_op jit(solution)/shard_map/ppermute | solution.py:36
  526.6 78.7 %collective-permute-start.29 = (bf16[1,256,2048]{2,1,0:T(8,128)(2,1)}, bf16[1,256,2048]{2,1,0:T(8,128)(2,1)}, u32[]{:S(2)}, u32[]{:S(2)}) collective-permute-start(bf16[1,256,2048]{2,1,0:T(8,128)(2,1)} %get-tuple-element.446), channel_id=1, source_target_pairs={{0,16},{4,20},{8,24},{12,28},{16,0},{20,4},{24,8},{28,12},{1,17},{... | collective-permute-start | bytes 3145736 | tf_op jit(solution)/shard_map/ppermute | solution.py:36
  568.2 40.1 %collective-permute-start.28 = (bf16[2,512,512]{2,1,0:T(8,128)(2,1)}, bf16[2,512,512]{2,1,0:T(8,128)(2,1)}, u32[]{:S(2)}, u32[]{:S(2)}) collective-permute-start(bf16[2,512,512]{2,1,0:T(8,128)(2,1)} %get-tuple-element.444), channel_id=1, source_target_pairs={{0,8},{4,12},{8,0},{12,4},{16,24},{20,28},{24,16},{28,20},{1,9},{5... | collective-permute-start | bytes 3145736 | tf_op jit(solution)/shard_map/ppermute | solution.py:36
  570.1 60.5 %collective-permute-start.32 = (bf16[1,256,512]{2,1,0:T(8,128)(2,1)}, bf16[1,256,512]{2,1,0:T(8,128)(2,1)}, u32[]{:S(2)}, u32[]{:S(2)}) collective-permute-start(bf16[1,256,512]{2,1,0:T(8,128)(2,1)} %get-tuple-element.461), channel_id=1, source_target_pairs={{0,16},{4,20},{8,24},{12,28},{16,0},{20,4},{24,8},{28,12},{1,17},{... | collective-permute-start | bytes 786440 | tf_op jit(solution)/shard_map/ppermute | solution.py:36
  601.9 55.3 %collective-permute-start.30 = (bf16[1,256,1536]{2,1,0:T(8,128)(2,1)}, bf16[1,256,1536]{2,1,0:T(8,128)(2,1)}, u32[]{:S(2)}, u32[]{:S(2)}) collective-permute-start(bf16[1,256,1536]{2,1,0:T(8,128)(2,1)} %copy-done.88), channel_id=1, source_target_pairs={{0,16},{4,20},{8,24},{12,28},{16,0},{20,4},{24,8},{28,12},{1,17},{... | collective-permute-start | bytes 2359304 | tf_op jit(solution)/shard_map/ppermute | solution.py:36
  627.2 27.7 %collective-permute-start.31 = (bf16[1,512,512]{2,1,0:T(8,128)(2,1)}, bf16[1,512,512]{2,1,0:T(8,128)(2,1)S(1)}, u32[]{:S(2)}, u32[]{:S(2)}) collective-permute-start(bf16[1,512,512]{2,1,0:T(8,128)(2,1)} %get-tuple-element.459), channel_id=1, source_target_pairs={{0,16},{4,20},{8,24},{12,28},{16,0},{20,4},{24,8},{28,12},{1,17},{... | collective-permute-start | bytes 1572872 | tf_op jit(solution)/shard_map/ppermute | solution.py:36
  (109 other events, 1633.1 us)

commit v4 on v3

--- a/solution.py
+++ b/solution.py
@@ -334,6 +334,7 @@
         [(array.shape, array.dtype, None, "any") for array, _, _ in items],
         scratch=[pltpu.SemaphoreType.DMA((count,)), pltpu.SemaphoreType.DMA((count,))],
         remote=True,
+        room=2 * 1024 * 1024,
     )
 
 
@@ -1189,16 +1190,6 @@
     weight = jnp.moveaxis(qkv_weight, 1, 0)
     turn = turn_tables(length)
 
-    text_in = call(
-        text_body,
-        meta,
-        (4,),
-        [(text_embed, (rows // 4, width), row_block), (table,), (gain_in,)],
-        [((rows, width), BF, (rows // 4, width), row_block)],
-    )[0]
-    text_pieces = gather_start(text_in)
-
-
     clip = clip_feats.reshape(images * patches, clip_width)
     key_proj, value_proj, pool_out = call(
         functools.partial(pool_body, images=images),
@@ -1212,11 +1203,20 @@
         ],
     )
     gathering = GatherDp(meta, pool_out)
+
+    text_in = call(
+        text_body,
+        meta,
+        (4,),
+        [(text_embed, (rows // 4, width), row_block), (table,), (gain_in,)],
+        [((rows, width), BF, (rows // 4, width), row_block)],
+    )[0]
+    text_pieces = gather_start(text_in)
+    gathering.step()
     state = project(meta, text_pieces[:2], weight, turn, None, 0)
     gathering.step()
     gather_end(meta, text_pieces)
     state = project(meta, text_pieces[2:], weight, turn, state, 2)
-    gathering.step()
 
     def d_up_half(which):
         return call(

time: 672 us -> 665 us (0.990)
  waiting for transfers between devices: 165 us -> 153 us
    ppermute x33, waiting for transfers between devices: 165 us -> 153 us  [swap(): return lax.ppermute(values, axis, [(i, i ^ bit) for i in range(size)])]
    unnamed x210 -> x204, local copies, waits for them, and re-layouts: 39 us -> 35.9 us
  transfers between devices with their start and end apart: 33 -> 33, of which waited for: 13 -> 15; matrix products, arithmetic and copies ran while one was open for 3% -> 3% of each run, Pallas kernels for 51% -> 51%
where the time goes in v4:
time: 665 us; the launch traced here: 656 us
  Pallas kernels  406 us (61%)
  waiting for transfers between devices  153 us (23%)
  starting transfers between devices  44.8 us (7%)
  local copies, waits for them, and re-layouts  40.9 us (6%)
  other arithmetic  8.5 us (1%)
    pallas_call x87, Pallas kernels, call(): pl.pallas_call(marked, out_shape=shapes, grid_spec=pltpu.PrefetchScalarGr...  404 us
    ppermute x33, waiting for transfers between devices, swap(): return lax.ppermute(values, axis, [(i, i ^ bit) for i in range(size)])  153 us
    ppermute x33, starting transfers between devices, swap(): return lax.ppermute(values, axis, [(i, i ^ bit) for i in range(size)])  44.8 us
    unnamed x204, local copies, waits for them, and re-layouts  35.9 us
  transfers between devices with their start and end apart: 33, of which 15 were waited for; matrix products, arithmetic and copies ran while one was open for 3% of the time, Pallas kernels for 51%

profile of v4, /device:TPU:0, one launch (start us, length us, event | category | flops | bytes accessed | tf_op | source)
XLA Modules:
  0.0 655.6 jit_solution(281070825795973658)
XLA Ops:
  59.4 9.0 %body.24 = (bf16[4,16,2048]{2,1,0:T(8,128)(2,1)S(1)}, f32[8,128]{1,0:T(8,128)S(1)}) custom-call(s32[48]{0:T(128)S(1)} %copy-done.64, bf16[4,16,2048]{2,1,0:T(8,128)(2,1)S(1)} %slice_bitcast_fusion.5.refs_0_, f32[8,128]{1,0:T(8,128)S(1)} %get-tuple-element.263.refs_1_), custom_call_target="tpu_custom_call" | custom-call | flops 1000000 | bytes 1024 | tf_op jit(solution)/shard_map/body/pallas_call | solution.py:142
  68.5 9.3 %body.25 = (bf16[4,16,2048]{2,1,0:T(8,128)(2,1)S(1)}, bf16[4,16,2048]{2,1,0:T(8,128)(2,1)S(1)}, f32[8,128]{1,0:T(8,128)S(1)}) custom-call(s32[48]{0:T(128)S(1)} %copy-done.64, bf16[4,16,2048]{2,1,0:T(8,128)(2,1)S(1)} %fusion.refs_0_.refs_1_, bf16[4,16,2048]{2,1,0:T(8,128)(2,1)S(1)} %fusion.refs_0_.refs_1_, f32[8,128]{1,0:T(8,128)S(1)} %get-tuple-element.265.refs_2_), custom_call_target="tpu_custom_call" | custom-call | flops 1000000 | bytes 1024 | tf_op jit(solution)/shard_map/body/pallas_call | solution.py:142
  88.6 15.2 %attend_body.1 = (bf16[1024,512]{1,0:T(8,128)(2,1)S(1)}, f32[8,1024]{1,0:T(8,128)S(1)}, f32[8,1024]{1,0:T(8,128)S(1)}, f32[8,128]{1,0:T(8,128)S(1)}) custom-call(s32[48]{0:T(128)S(1)} %copy-done.64, bf16[1024,1536]{1,0:T(8,128)(2,1)S(1)} %get-tuple-element.274.refs_0_, f32[8,128]{1,0:T(8,128)S(1)} %get-tuple-element.275.refs_1_), custom_call_target="tpu_custom_call" | custom-call | flops 1000000 | bytes 1024 | tf_op jit(solution)/shard_map/attend_body/pallas_call | solution.py:142
  147.6 10.6 %up_body.2 = (bf16[1024,2048]{1,0:T(8,128)(2,1)S(1)}, bf16[1024,2048]{1,0:T(8,128)(2,1)S(1)}, f32[8,1024]{1,0:T(8,128)S(1)}, f32[8,128]{1,0:T(8,128)S(1)}) custom-call(s32[48]{0:T(128)S(1)} %copy-done.64, bf16[256,2048]{1,0:T(8,128)(2,1)S(1)} %get-tuple-element.296.refs_0_, bf16[256,2048]{1,0:T(8,128)(2,1)S(1)} %collective-permute-done.9.refs_1_, ...), custom_call_target="tpu_custom_call" | custom-call | flops 1000000 | bytes 1024 | tf_op jit(solution)/shard_map/up_body/pallas_call | solution.py:142
  158.2 12.3 %collective-permute-done.8.refs_0_.refs_2_ = bf16[256,2048]{1,0:T(8,128)(2,1)S(1)} collective-permute-done((bf16[256,2048]{1,0:T(8,128)(2,1)S(1)}, bf16[256,2048]{1,0:T(8,128)(2,1)S(1)}, u32[]{:S(2)}, u32[]{:S(2)}) %collective-permute-start.8) | collective-permute-done | bytes 1048608 | tf_op jit(solution)/shard_map/ppermute | solution.py:36
  173.7 10.1 %up_body.3 = (bf16[1024,2048]{1,0:T(8,128)(2,1)S(1)}, bf16[1024,2048]{1,0:T(8,128)(2,1)S(1)}, f32[8,1024]{1,0:T(8,128)S(1)}, f32[8,128]{1,0:T(8,128)S(1)}) custom-call(s32[48]{0:T(128)S(1)} %copy-done.64, bf16[256,2048]{1,0:T(8,128)(2,1)S(1)} %collective-permute-done.8.refs_0_.refs_2_, ...), custom_call_target="tpu_custom_call", output_to_operand_aliasing={{0}: (7, {}), {1}: (8, {}), {2}: (9, {})} | custom-call | flops 1000000 | bytes 1024 | tf_op jit(solution)/shard_map/up_body/pallas_call | solution.py:142
  199.4 8.0 %spread_body.1 = (bf16[1024,2048]{1,0:T(8,128)(2,1)S(1)}, bf16[1024,2048]{1,0:T(8,128)(2,1)S(1)}, f32[1,2048]{1,0:T(1,128)S(1)}, f32[8,128]{1,0:T(8,128)S(1)}) custom-call(s32[48]{0:T(128)S(1)} %copy-done.64, bf16[1024,2048]{1,0:T(8,128)(2,1)S(1)} %copy-done.15, bf16[1024,2048]{1,0:T(8,128)(2,1)S(1)} %copy-done.17, ...), custom_call_target="tpu_custom_call" | custom-call | flops 1000000 | bytes 1024 | tf_op jit(solution)/shard_map/spread_body/pallas_call | solution.py:142
  235.0 7.5 %back_body.3 = (bf16[256,2048]{1,0:T(8,128)(2,1)S(1)}, f32[8,128]{1,0:T(8,128)S(1)}) custom-call(s32[48]{0:T(128)S(1)} %copy-done.64, bf16[1024,2048]{1,0:T(8,128)(2,1)S(1)} %get-tuple-element.317.refs_4_.refs_0_, bf16[2048,2048]{1,0:T(8,128)(2,1)S(1)} %bitcast.81, f32[8,128]{1,0:T(8,128)S(1)} %get-tuple-element.321.refs_2_), custom_call_target="tpu_custom_call" | custom-call | flops 1000000 | bytes 1024 | tf_op jit(solution)/shard_map/back_body/pallas_call | solution.py:142
  242.5 16.2 %collective-permute-done.10.refs_1_ = bf16[256,2048]{1,0:T(8,128)(2,1)S(1)} collective-permute-done((bf16[256,2048]{1,0:T(8,128)(2,1)S(1)}, bf16[256,2048]{1,0:T(8,128)(2,1)S(1)}, u32[]{:S(2)}, u32[]{:S(2)}) %collective-permute-start.10) | collective-permute-done | bytes 1048608 | tf_op jit(solution)/shard_map/ppermute | solution.py:36
  268.2 13.2 %down_body.1 = (bf16[256,2048]{1,0:T(8,128)(2,1)S(1)}, bf16[256,2048]{1,0:T(8,128)(2,1)S(1)}, f32[8,128]{1,0:T(8,128)S(1)}) custom-call(s32[48]{0:T(128)S(1)} %copy-done.64, bf16[1024,2048]{1,0:T(8,128)(2,1)S(1)} %get-tuple-element.316.refs_4_.refs_0_, bf16[2048,2048]{1,0:T(8,128)(2,1)S(1)} %bitcast.83, f32[8,128]{1,0:T(8,128)S(1)} %get-tuple-element.327.refs_2_), custom_call_target="tpu_custom_call" | custom-call | flops 1000000 | bytes 1024 | tf_op jit(solution)/shard_map/down_body/pallas_call | solution.py:142
  309.4 8.0 %weight_body.15 = (bf16[2,256,2048]{2,1,0:T(8,128)(2,1)S(1)}, bf16[2,256,2048]{2,1,0:T(8,128)(2,1)S(1)}, f32[8,128]{1,0:T(8,128)S(1)}) custom-call(s32[48]{0:T(128)S(1)} %copy-done.64, bf16[256,2048]{1,0:T(8,128)(2,1)S(1)} %copy-done.31, bf16[256,2048]{1,0:T(8,128)(2,1)S(1)} %copy-done.34, bf16[256,2048]{1,0:T(8,128)(2,1)S(1)} %copy-done.11, ...), custom_call_target="tpu_custom_call" | custom-call | flops 1000000 | bytes 1024 | tf_op jit(solution)/shard_map/weight_body/pallas_call | solution.py:142
  319.2 20.8 %attend_back_body.1 = (bf16[1024,1536]{1,0:T(8,128)(2,1)S(1)}, f32[8,128]{1,0:T(8,128)S(1)}) custom-call(s32[48]{0:T(128)S(1)} %copy-done.64, bf16[1024,1536]{1,0:T(8,128)(2,1)S(1)} %copy-done.3, bf16[1024,512]{1,0:T(8,128)(2,1)S(1)} %copy-done.13, bf16[1024,512]{1,0:T(8,128)(2,1)S(1)} %copy-done.50, f32[8,1024]{1,0:T(8,128)S(1)} %get-tuple-element.340.refs_3_, ...), custom_call_target="tpu_custom_call" | custom-call | flops 1000000 | bytes 1024 | tf_op jit(solution)/shard_map/attend_back_body/pallas_call | solution.py:142
  345.2 8.9 %body.34 = (bf16[4,16,2048]{2,1,0:T(8,128)(2,1)S(1)}, f32[8,128]{1,0:T(8,128)S(1)}) custom-call(s32[48]{0:T(128)S(1)} %copy-done.64, bf16[4,16,2048]{2,1,0:T(8,128)(2,1)S(1)} %get-tuple-element.520.refs_0_, f32[8,128]{1,0:T(8,128)S(1)} %get-tuple-element.354.refs_1_), custom_call_target="tpu_custom_call" | custom-call | flops 1000000 | bytes 1024 | tf_op jit(solution)/shard_map/body/pallas_call | solution.py:142
  356.0 13.7 %body.35 = (bf16[4,32,2048]{2,1,0:T(8,128)(2,1)S(1)}, f32[8,128]{1,0:T(8,128)S(1)}) custom-call(s32[48]{0:T(128)S(1)} %copy-done.64, bf16[4,32,2048]{2,1,0:T(8,128)(2,1)S(1)} %get-tuple-element.358.refs_0_, f32[8,128]{1,0:T(8,128)S(1)} %get-tuple-element.359.refs_1_), custom_call_target="tpu_custom_call" | custom-call | flops 1000000 | bytes 1024 | tf_op jit(solution)/shard_map/body/pallas_call | solution.py:142
  383.2 8.1 %weight_body.17 = (bf16[2,256,2048]{2,1,0:T(8,128)(2,1)S(1)}, bf16[2,256,2048]{2,1,0:T(8,128)(2,1)S(1)}, f32[8,128]{1,0:T(8,128)S(1)}) custom-call(s32[48]{0:T(128)S(1)} %copy-done.64, bf16[256,2048]{1,0:T(8,128)(2,1)S(1)} %copy-done.40, bf16[256,2048]{1,0:T(8,128)(2,1)S(1)} %copy-done.43, bf16[256,2048]{1,0:T(8,128)(2,1)S(1)} %copy-done.8, ...), custom_call_target="tpu_custom_call" | custom-call | flops 1000000 | bytes 1024 | tf_op jit(solution)/shard_map/weight_body/pallas_call | solution.py:142
  405.5 9.7 %body.37 = (bf16[1,32,2048]{2,1,0:T(8,128)(2,1)S(1)}, f32[8,128]{1,0:T(8,128)S(1)}) custom-call(s32[48]{0:T(128)S(1)} %copy-done.64, bf16[1,32,2048]{2,1,0:T(8,128)(2,1)S(1)} %get-tuple-element.377.refs_0_, f32[8,128]{1,0:T(8,128)S(1)} %get-tuple-element.378.refs_1_), custom_call_target="tpu_custom_call" | custom-call | flops 1000000 | bytes 1024 | tf_op jit(solution)/shard_map/body/pallas_call | solution.py:142
  419.8 30.7 %collective-permute-done.17.refs_1_ = bf16[2,256,512]{2,1,0:T(8,128)(2,1)S(1)} collective-permute-done((bf16[2,256,512]{2,1,0:T(8,128)(2,1)S(1)}, bf16[2,256,512]{2,1,0:T(8,128)(2,1)S(1)}, u32[]{:S(2)}, u32[]{:S(2)}) %collective-permute-start.17) | collective-permute-done | bytes 524320 | tf_op jit(solution)/shard_map/ppermute | solution.py:36
  460.6 8.6 %pool_back_body.1 = (bf16[512,1024]{1,0:T(8,128)(2,1)S(1)}, f32[64,512]{1,0:T(8,128)S(1)}, bf16[2,2,64,1024]{3,2,1,0:T(8,128)(2,1)S(1)}, bf16[2,2,64,1024]{3,2,1...) custom-call(s32[48]{0:T(128)S(1)} %copy-done.64, bf16[2,16,2048]{2,1,0:T(8,128)(2,1)S(1)} %bitcast.100, ...), custom_call_target="tpu_custom_call" | custom-call | flops 1000000 | bytes 1024 | tf_op jit(solution)/shard_map/pool_back_body/pallas_call | solution.py:142
  492.4 14.7 %collective-permute-done.21.refs_1_ = bf16[256,2048]{1,0:T(8,128)(2,1)S(1)} collective-permute-done((bf16[256,2048]{1,0:T(8,128)(2,1)S(1)}, bf16[256,2048]{1,0:T(8,128)(2,1)S(1)}, u32[]{:S(2)}, u32[]{:S(2)}) %collective-permute-start.21) | collective-permute-done | bytes 1048608 | tf_op jit(solution)/shard_map/ppermute | solution.py:36
  519.9 13.0 %body.41 = (bf16[2,64,1024]{2,1,0:T(8,128)(2,1)S(1)}, f32[8,128]{1,0:T(8,128)S(1)}) custom-call(s32[48]{0:T(128)S(1)} %copy-done.64, bf16[2,64,1024]{2,1,0:T(8,128)(2,1)S(1)} %slice_bitcast_fusion.1.refs_0_, f32[8,128]{1,0:T(8,128)S(1)} %get-tuple-element.428.refs_1_), custom_call_target="tpu_custom_call" | custom-call | flops 1000000 | bytes 1024 | tf_op jit(solution)/shard_map/body/pallas_call | solution.py:142
  534.2 19.5 %collective-permute-done.26.refs_2_ = bf16[4,512,512]{2,1,0:T(8,128)(2,1)S(1)} collective-permute-done((bf16[4,512,512]{2,1,0:T(8,128)(2,1)S(1)}, bf16[4,512,512]{2,1,0:T(8,128)(2,1)S(1)}, u32[]{:S(2)}, u32[]{:S(2)}) %collective-permute-start.26) | collective-permute-done | bytes 2097184 | tf_op jit(solution)/shard_map/ppermute | solution.py:36
  565.4 19.0 %collective-permute-done.24.refs_1_ = bf16[368,128]{1,0:T(8,128)(2,1)} collective-permute-done((bf16[368,128]{1,0:T(8,128)(2,1)S(1)}, bf16[368,128]{1,0:T(8,128)(2,1)}, u32[]{:S(2)}, u32[]{:S(2)}) %collective-permute-start.24) | collective-permute-done | bytes 94240 | tf_op jit(solution)/shard_map/ppermute | solution.py:36
  602.6 9.9 %body.42 = (bf16[368,128]{1,0:T(8,128)(2,1)S(1)}, bf16[368,128]{1,0:T(8,128)(2,1)S(1)}, f32[8,128]{1,0:T(8,128)S(1)}) custom-call(s32[48]{0:T(128)S(1)} %copy-done.64, bf16[368,128]{1,0:T(8,128)(2,1)S(1)} %get-tuple-element.450.refs_0_.refs_1_, bf16[368,128]{1,0:T(8,128)(2,1)S(1)} %get-tuple-element.450.refs_0_.refs_1_, f32[8,128]{1,0:T(8,128)S(1)} %get-tuple-element.451.refs_2_), custom_call_target="tpu_custom_call" | custom-call | flops 1000000 | bytes 1024 | tf_op jit(solution)/shard_map/body/pallas_call | solution.py:142
  630.9 16.6 %collective-permute-done.31 = bf16[1,512,512]{2,1,0:T(8,128)(2,1)S(1)} collective-permute-done((bf16[1,512,512]{2,1,0:T(8,128)(2,1)}, bf16[1,512,512]{2,1,0:T(8,128)(2,1)S(1)}, u32[]{:S(2)}, u32[]{:S(2)}) %collective-permute-start.31) | collective-permute-done | bytes 524320 | tf_op jit(solution)/shard_map/ppermute | solution.py:36
  (369 shorter events, 340.3 us)
Async XLA Ops:
  19.2 26.3 %collective-permute-start.4 = (bf16[256,2048]{1,0:T(8,128)(2,1)S(1)}, bf16[256,2048]{1,0:T(8,128)(2,1)S(1)}, u32[]{:S(2)}, u32[]{:S(2)}) collective-permute-start(bf16[256,2048]{1,0:T(8,128)(2,1)S(1)} %get-tuple-element.247.refs_0_), channel_id=1, source_target_pairs={{0,2},{1,3},{2,0},{3,1},{4,6},{5,7},{6,4},{7,5},{8,10},{9,11},{10,... | collective-permute-start | bytes 3145736 | tf_op jit(solution)/shard_map/ppermute | solution.py:36
  80.6 47.8 %collective-permute-start.6 = (bf16[256,2048]{1,0:T(8,128)(2,1)S(1)}, bf16[256,2048]{1,0:T(8,128)(2,1)S(1)}, u32[]{:S(2)}, u32[]{:S(2)}) collective-permute-start(bf16[256,2048]{1,0:T(8,128)(2,1)S(1)} %get-tuple-element.289.refs_0_), channel_id=1, source_target_pairs={{0,2},{1,3},{2,0},{3,1},{4,6},{5,7},{6,4},{7,5},{8,10},{9,11},{10,... | collective-permute-start | bytes 3145736 | tf_op jit(solution)/shard_map/ppermute | solution.py:36
  81.2 41.2 %collective-permute-start.7 = (bf16[256,2048]{1,0:T(8,128)(2,1)S(1)}, bf16[256,2048]{1,0:T(8,128)(2,1)S(1)}, u32[]{:S(2)}, u32[]{:S(2)}) collective-permute-start(bf16[256,2048]{1,0:T(8,128)(2,1)S(1)} %get-tuple-element.289.refs_0_), channel_id=1, source_target_pairs={{0,1},{1,0},{2,3},{3,2},{4,5},{5,4},{6,7},{7,6},{8,9},{9,8},{10,11... | collective-permute-start | bytes 3145736 | tf_op jit(solution)/shard_map/ppermute | solution.py:36
  116.3 25.3 %collective-permute-start.5 = (bf16[256,2048]{1,0:T(8,128)(2,1)S(1)}, bf16[256,2048]{1,0:T(8,128)(2,1)S(1)}, u32[]{:S(2)}, u32[]{:S(2)}) collective-permute-start(bf16[256,2048]{1,0:T(8,128)(2,1)S(1)} %get-tuple-element.287), channel_id=1, source_target_pairs={{0,2},{1,3},{2,0},{3,1},{4,6},{5,7},{6,4},{7,5},{8,10},{9,11},{10,... | collective-permute-start | bytes 3145736 | tf_op jit(solution)/shard_map/ppermute | solution.py:36
  144.9 25.6 %collective-permute-start.8 = (bf16[256,2048]{1,0:T(8,128)(2,1)S(1)}, bf16[256,2048]{1,0:T(8,128)(2,1)S(1)}, u32[]{:S(2)}, u32[]{:S(2)}) collective-permute-start(bf16[256,2048]{1,0:T(8,128)(2,1)S(1)} %get-tuple-element.296.refs_0_), channel_id=1, source_target_pairs={{0,2},{1,3},{2,0},{3,1},{4,6},{5,7},{6,4},{7,5},{8,10},{9,11},{10,... | collective-permute-start | bytes 3145736 | tf_op jit(solution)/shard_map/ppermute | solution.py:36
  215.8 93.6 %collective-permute-start.14 = (bf16[4,256,2048]{2,1,0:T(8,128)(2,1)}, bf16[4,256,2048]{2,1,0:T(8,128)(2,1)}, u32[]{:S(2)}, u32[]{:S(2)}) collective-permute-start(bf16[4,256,2048]{2,1,0:T(8,128)(2,1)} %get-tuple-element.344), channel_id=1, source_target_pairs={{0,4},{4,0},{8,12},{12,8},{16,20},{20,16},{24,28},{28,24},{1,5},{5... | collective-permute-start | bytes 12582920 | tf_op jit(solution)/shard_map/ppermute | solution.py:36
  224.5 158.7 %collective-permute-start.15 = (bf16[4,256,2048]{2,1,0:T(8,128)(2,1)}, bf16[4,256,2048]{2,1,0:T(8,128)(2,1)}, u32[]{:S(2)}, u32[]{:S(2)}) collective-permute-start(bf16[4,256,2048]{2,1,0:T(8,128)(2,1)} %get-tuple-element.369), channel_id=1, source_target_pairs={{0,8},{4,12},{8,0},{12,4},{16,24},{20,28},{24,16},{28,20},{1,9},{5... | collective-permute-start | bytes 12582920 | tf_op jit(solution)/shard_map/ppermute | solution.py:36
  233.5 25.3 %collective-permute-start.10 = (bf16[256,2048]{1,0:T(8,128)(2,1)S(1)}, bf16[256,2048]{1,0:T(8,128)(2,1)S(1)}, u32[]{:S(2)}, u32[]{:S(2)}) collective-permute-start(bf16[256,2048]{1,0:T(8,128)(2,1)S(1)} %get-tuple-element.323), channel_id=1, source_target_pairs={{0,2},{1,3},{2,0},{3,1},{4,6},{5,7},{6,4},{7,5},{8,10},{9,11},{10,... | collective-permute-start | bytes 3145736 | tf_op jit(solution)/shard_map/ppermute | solution.py:36
  262.6 25.6 %collective-permute-start.12 = (bf16[256,2048]{1,0:T(8,128)(2,1)S(1)}, bf16[256,2048]{1,0:T(8,128)(2,1)S(1)}, u32[]{:S(2)}, u32[]{:S(2)}) collective-permute-start(bf16[256,2048]{1,0:T(8,128)(2,1)S(1)} %get-tuple-element.325.refs_0_.refs_5_), channel_id=1, source_target_pairs={{0,2},{1,3},{2,0},{3,1},{4,6},{5,7},{6,4},{7,5},{8,10},{9,11},{10,... | collective-permute-start | bytes 3145736 | tf_op jit(solution)/shard_map/ppermute | solution.py:36
  300.6 77.0 %collective-permute-start.13 = (bf16[256,2048]{1,0:T(8,128)(2,1)S(1)}, bf16[256,2048]{1,0:T(8,128)(2,1)S(1)}, u32[]{:S(2)}, u32[]{:S(2)}) collective-permute-start(bf16[256,2048]{1,0:T(8,128)(2,1)S(1)} %get-tuple-element.338), channel_id=1, source_target_pairs={{0,2},{1,3},{2,0},{3,1},{4,6},{5,7},{6,4},{7,5},{8,10},{9,11},{10,... | collective-permute-start | bytes 3145736 | tf_op jit(solution)/shard_map/ppermute | solution.py:36
  305.0 75.1 %collective-permute-start.16 = (bf16[4,256,512]{2,1,0:T(8,128)(2,1)S(1)}, bf16[4,256,512]{2,1,0:T(8,128)(2,1)S(1)}, u32[]{:S(2)}, u32[]{:S(2)}) collective-permute-start(bf16[4,256,512]{2,1,0:T(8,128)(2,1)S(1)} %get-tuple-element.370), channel_id=1, source_target_pairs={{0,4},{4,0},{8,12},{12,8},{16,20},{20,16},{24,28},{28,24},{1,5},{5... | collective-permute-start | bytes 3145736 | tf_op jit(solution)/shard_map/ppermute | solution.py:36
  317.4 97.8 %collective-permute-start.18 = (bf16[2,256,2048]{2,1,0:T(8,128)(2,1)S(1)}, bf16[2,256,2048]{2,1,0:T(8,128)(2,1)S(1)}, u32[]{:S(2)}, u32[]{:S(2)}) collective-permute-start(bf16[2,256,2048]{2,1,0:T(8,128)(2,1)S(1)} %get-tuple-element.383), channel_id=1, source_target_pairs={{0,8},{4,12},{8,0},{12,4},{16,24},{20,28},{24,16},{28,20},{1,9},{5... | collective-permute-start | bytes 6291464 | tf_op jit(solution)/shard_map/ppermute | solution.py:36
  396.3 75.0 %collective-permute-start.19 = (bf16[4,256,1536]{2,1,0:T(8,128)(2,1)S(1)}, bf16[4,256,1536]{2,1,0:T(8,128)(2,1)S(1)}, u32[]{:S(2)}, u32[]{:S(2)}) collective-permute-start(bf16[4,256,1536]{2,1,0:T(8,128)(2,1)S(1)} %get-tuple-element.398), channel_id=1, source_target_pairs={{0,4},{4,0},{8,12},{12,8},{16,20},{20,16},{24,28},{28,24},{1,5},{5... | collective-permute-start | bytes 9437192 | tf_op jit(solution)/shard_map/ppermute | solution.py:36
  416.3 53.0 %collective-permute-start.20 = (bf16[1,256,2048]{2,1,0:T(8,128)(2,1)S(1)}, bf16[1,256,2048]{2,1,0:T(8,128)(2,1)S(1)}, u32[]{:S(2)}, u32[]{:S(2)}) collective-permute-start(bf16[1,256,2048]{2,1,0:T(8,128)(2,1)S(1)} %get-tuple-element.400), channel_id=1, source_target_pairs={{0,16},{4,20},{8,24},{12,28},{16,0},{20,4},{24,8},{28,12},{1,17},{... | collective-permute-start | bytes 3145736 | tf_op jit(solution)/shard_map/ppermute | solution.py:36
  416.3 34.2 %collective-permute-start.17 = (bf16[2,256,512]{2,1,0:T(8,128)(2,1)S(1)}, bf16[2,256,512]{2,1,0:T(8,128)(2,1)S(1)}, u32[]{:S(2)}, u32[]{:S(2)}) collective-permute-start(bf16[2,256,512]{2,1,0:T(8,128)(2,1)S(1)} %get-tuple-element.381), channel_id=1, source_target_pairs={{0,8},{4,12},{8,0},{12,4},{16,24},{20,28},{24,16},{28,20},{1,9},{5... | collective-permute-start | bytes 1572872 | tf_op jit(solution)/shard_map/ppermute | solution.py:36
  419.5 95.5 %collective-permute-start.22 = (bf16[2,256,2048]{2,1,0:T(8,128)(2,1)}, bf16[2,256,2048]{2,1,0:T(8,128)(2,1)S(1)}, u32[]{:S(2)}, u32[]{:S(2)}) collective-permute-start(bf16[2,256,2048]{2,1,0:T(8,128)(2,1)} %copy-done.83), channel_id=1, source_target_pairs={{0,4},{4,0},{8,12},{12,8},{16,20},{20,16},{24,28},{28,24},{1,5},{5... | collective-permute-start | bytes 6291464 | tf_op jit(solution)/shard_map/ppermute | solution.py:36
  481.5 72.2 %collective-permute-start.26 = (bf16[4,512,512]{2,1,0:T(8,128)(2,1)S(1)}, bf16[4,512,512]{2,1,0:T(8,128)(2,1)S(1)}, u32[]{:S(2)}, u32[]{:S(2)}) collective-permute-start(bf16[4,512,512]{2,1,0:T(8,128)(2,1)S(1)} %get-tuple-element.435), channel_id=1, source_target_pairs={{0,4},{4,0},{8,12},{12,8},{16,20},{20,16},{24,28},{28,24},{1,5},{5... | collective-permute-start | bytes 6291464 | tf_op jit(solution)/shard_map/ppermute | solution.py:36
  482.1 24.9 %collective-permute-start.21 = (bf16[256,2048]{1,0:T(8,128)(2,1)S(1)}, bf16[256,2048]{1,0:T(8,128)(2,1)S(1)}, u32[]{:S(2)}, u32[]{:S(2)}) collective-permute-start(bf16[256,2048]{1,0:T(8,128)(2,1)S(1)} %get-tuple-element.408), channel_id=1, source_target_pairs={{0,2},{1,3},{2,0},{3,1},{4,6},{5,7},{6,4},{7,5},{8,10},{9,11},{10,... | collective-permute-start | bytes 3145736 | tf_op jit(solution)/shard_map/ppermute | solution.py:36
  483.0 80.1 %collective-permute-start.25 = (bf16[2,256,1536]{2,1,0:T(8,128)(2,1)}, bf16[2,256,1536]{2,1,0:T(8,128)(2,1)}, u32[]{:S(2)}, u32[]{:S(2)}) collective-permute-start(bf16[2,256,1536]{2,1,0:T(8,128)(2,1)} %get-tuple-element.434), channel_id=1, source_target_pairs={{0,8},{4,12},{8,0},{12,4},{16,24},{20,28},{24,16},{28,20},{1,9},{5... | collective-permute-start | bytes 4718600 | tf_op jit(solution)/shard_map/ppermute | solution.py:36
  519.4 76.2 %collective-permute-start.29 = (bf16[1,256,2048]{2,1,0:T(8,128)(2,1)}, bf16[1,256,2048]{2,1,0:T(8,128)(2,1)}, u32[]{:S(2)}, u32[]{:S(2)}) collective-permute-start(bf16[1,256,2048]{2,1,0:T(8,128)(2,1)} %get-tuple-element.446), channel_id=1, source_target_pairs={{0,16},{4,20},{8,24},{12,28},{16,0},{20,4},{24,8},{28,12},{1,17},{... | collective-permute-start | bytes 3145736 | tf_op jit(solution)/shard_map/ppermute | solution.py:36
  559.8 39.6 %collective-permute-start.28 = (bf16[2,512,512]{2,1,0:T(8,128)(2,1)}, bf16[2,512,512]{2,1,0:T(8,128)(2,1)}, u32[]{:S(2)}, u32[]{:S(2)}) collective-permute-start(bf16[2,512,512]{2,1,0:T(8,128)(2,1)} %get-tuple-element.444), channel_id=1, source_target_pairs={{0,8},{4,12},{8,0},{12,4},{16,24},{20,28},{24,16},{28,20},{1,9},{5... | collective-permute-start | bytes 3145736 | tf_op jit(solution)/shard_map/ppermute | solution.py:36
  562.7 61.3 %collective-permute-start.32 = (bf16[1,256,512]{2,1,0:T(8,128)(2,1)}, bf16[1,256,512]{2,1,0:T(8,128)(2,1)}, u32[]{:S(2)}, u32[]{:S(2)}) collective-permute-start(bf16[1,256,512]{2,1,0:T(8,128)(2,1)} %get-tuple-element.461), channel_id=1, source_target_pairs={{0,16},{4,20},{8,24},{12,28},{16,0},{20,4},{24,8},{28,12},{1,17},{... | collective-permute-start | bytes 786440 | tf_op jit(solution)/shard_map/ppermute | solution.py:36
  592.2 57.6 %collective-permute-start.30 = (bf16[1,256,1536]{2,1,0:T(8,128)(2,1)}, bf16[1,256,1536]{2,1,0:T(8,128)(2,1)}, u32[]{:S(2)}, u32[]{:S(2)}) collective-permute-start(bf16[1,256,1536]{2,1,0:T(8,128)(2,1)} %copy-done.84), channel_id=1, source_target_pairs={{0,16},{4,20},{8,24},{12,28},{16,0},{20,4},{24,8},{28,12},{1,17},{... | collective-permute-start | bytes 2359304 | tf_op jit(solution)/shard_map/ppermute | solution.py:36
  620.6 26.8 %collective-permute-start.31 = (bf16[1,512,512]{2,1,0:T(8,128)(2,1)}, bf16[1,512,512]{2,1,0:T(8,128)(2,1)S(1)}, u32[]{:S(2)}, u32[]{:S(2)}) collective-permute-start(bf16[1,512,512]{2,1,0:T(8,128)(2,1)} %get-tuple-element.459), channel_id=1, source_target_pairs={{0,16},{4,20},{8,24},{12,28},{16,0},{20,4},{24,8},{28,12},{1,17},{... | collective-permute-start | bytes 1572872 | tf_op jit(solution)/shard_map/ppermute | solution.py:36
  (106 other events, 1566.8 us)

commit v5 on v4

--- a/solution.py
+++ b/solution.py
@@ -1193,7 +1193,7 @@
     clip = clip_feats.reshape(images * patches, clip_width)
     key_proj, value_proj, pool_out = call(
         functools.partial(pool_body, images=images),
-        meta,
+        image_seq,
         (1,),
         [(clip,), (res_key,), (res_value,), (res_query,)],
         [
@@ -1201,6 +1201,7 @@
             ((images * patches, wide), BF, None, None),
             ((images * latent, wide), BF, None, None),
         ],
+        room=4 * VMEM_BYTES,
     )
     gathering = GatherDp(meta, pool_out)
 

time: 665 us -> 663 us (level)
    unnamed x204 -> x198, local copies, waits for them, and re-layouts: 35.9 us -> 31.5 us
where the time goes in v5:
time: 663 us; the launch traced here: 654 us
  Pallas kernels  408 us (62%)
  waiting for transfers between devices  153 us (23%)
  starting transfers between devices  45.1 us (7%)
  local copies, waits for them, and re-layouts  36.5 us (6%)
  other arithmetic  8.56 us (1%)
    pallas_call x87, Pallas kernels, call(): pl.pallas_call(marked, out_shape=shapes, grid_spec=pltpu.PrefetchScalarGr...  407 us
    ppermute x33, waiting for transfers between devices, swap(): return lax.ppermute(values, axis, [(i, i ^ bit) for i in range(size)])  153 us
    ppermute x33, starting transfers between devices, swap(): return lax.ppermute(values, axis, [(i, i ^ bit) for i in range(size)])  45.1 us
    unnamed x198, local copies, waits for them, and re-layouts  31.5 us
  transfers between devices with their start and end apart: 33, of which 15 were waited for; matrix products, arithmetic and copies ran while one was open for 3% of the time, Pallas kernels for 51%

profile of v5, /device:TPU:0, one launch (start us, length us, event | category | flops | bytes accessed | tf_op | source)
XLA Modules:
  0.0 654.0 jit_solution(9361238438260343520)
XLA Ops:
  5.3 9.4 %pool_body.1 = (bf16[512,512]{1,0:T(8,128)(2,1)}, bf16[512,512]{1,0:T(8,128)(2,1)}, bf16[128,512]{1,0:T(8,128)(2,1)}, f32[8,128]{1,0:T(8,128)}) custom-call(s32[16]{0:T(128)} %meta_ref.1, bf16[512,1024]{1,0:T(8,128)(2,1)} %bitcast.88, bf16[1024,512]{1,0:T(8,128)(2,1)} %refs_8_.1, bf16[1024,512]{1,0:T(8,128)(2,1)} %refs_9_.1, bf16[64,512]{1,0:T(8,128)(2,1)} %refs_7_.1), custom_call_target="tpu_custom_call" | custom-call | flops 1000000 | bytes 1024 | tf_op jit(solution)/shard_map/pool_body/pallas_call | solution.py:142
  57.7 9.0 %body.24 = (bf16[4,16,2048]{2,1,0:T(8,128)(2,1)S(1)}, f32[8,128]{1,0:T(8,128)S(1)}) custom-call(s32[48]{0:T(128)S(1)} %copy-done.60, bf16[4,16,2048]{2,1,0:T(8,128)(2,1)S(1)} %slice_bitcast_fusion.5.refs_0_, f32[8,128]{1,0:T(8,128)S(1)} %get-tuple-element.263.refs_1_), custom_call_target="tpu_custom_call" | custom-call | flops 1000000 | bytes 1024 | tf_op jit(solution)/shard_map/body/pallas_call | solution.py:142
  66.8 9.3 %body.25 = (bf16[4,16,2048]{2,1,0:T(8,128)(2,1)S(1)}, bf16[4,16,2048]{2,1,0:T(8,128)(2,1)S(1)}, f32[8,128]{1,0:T(8,128)S(1)}) custom-call(s32[48]{0:T(128)S(1)} %copy-done.60, bf16[4,16,2048]{2,1,0:T(8,128)(2,1)S(1)} %fusion.refs_0_.refs_1_, bf16[4,16,2048]{2,1,0:T(8,128)(2,1)S(1)} %fusion.refs_0_.refs_1_, f32[8,128]{1,0:T(8,128)S(1)} %get-tuple-element.265.refs_2_), custom_call_target="tpu_custom_call" | custom-call | flops 1000000 | bytes 1024 | tf_op jit(solution)/shard_map/body/pallas_call | solution.py:142
  87.0 15.3 %attend_body.1 = (bf16[1024,512]{1,0:T(8,128)(2,1)S(1)}, f32[8,1024]{1,0:T(8,128)S(1)}, f32[8,1024]{1,0:T(8,128)S(1)}, f32[8,128]{1,0:T(8,128)S(1)}) custom-call(s32[48]{0:T(128)S(1)} %copy-done.60, bf16[1024,1536]{1,0:T(8,128)(2,1)S(1)} %get-tuple-element.274.refs_0_, f32[8,128]{1,0:T(8,128)S(1)} %get-tuple-element.275.refs_1_), custom_call_target="tpu_custom_call" | custom-call | flops 1000000 | bytes 1024 | tf_op jit(solution)/shard_map/attend_body/pallas_call | solution.py:142
  145.9 10.6 %up_body.2 = (bf16[1024,2048]{1,0:T(8,128)(2,1)S(1)}, bf16[1024,2048]{1,0:T(8,128)(2,1)S(1)}, f32[8,1024]{1,0:T(8,128)S(1)}, f32[8,128]{1,0:T(8,128)S(1)}) custom-call(s32[48]{0:T(128)S(1)} %copy-done.60, bf16[256,2048]{1,0:T(8,128)(2,1)S(1)} %get-tuple-element.296.refs_0_, bf16[256,2048]{1,0:T(8,128)(2,1)S(1)} %collective-permute-done.9.refs_1_, ...), custom_call_target="tpu_custom_call" | custom-call | flops 1000000 | bytes 1024 | tf_op jit(solution)/shard_map/up_body/pallas_call | solution.py:142
  156.6 12.3 %collective-permute-done.8.refs_0_.refs_2_ = bf16[256,2048]{1,0:T(8,128)(2,1)S(1)} collective-permute-done((bf16[256,2048]{1,0:T(8,128)(2,1)S(1)}, bf16[256,2048]{1,0:T(8,128)(2,1)S(1)}, u32[]{:S(2)}, u32[]{:S(2)}) %collective-permute-start.8) | collective-permute-done | bytes 1048608 | tf_op jit(solution)/shard_map/ppermute | solution.py:36
  172.1 10.1 %up_body.3 = (bf16[1024,2048]{1,0:T(8,128)(2,1)S(1)}, bf16[1024,2048]{1,0:T(8,128)(2,1)S(1)}, f32[8,1024]{1,0:T(8,128)S(1)}, f32[8,128]{1,0:T(8,128)S(1)}) custom-call(s32[48]{0:T(128)S(1)} %copy-done.60, bf16[256,2048]{1,0:T(8,128)(2,1)S(1)} %collective-permute-done.8.refs_0_.refs_2_, ...), custom_call_target="tpu_custom_call", output_to_operand_aliasing={{0}: (7, {}), {1}: (8, {}), {2}: (9, {})} | custom-call | flops 1000000 | bytes 1024 | tf_op jit(solution)/shard_map/up_body/pallas_call | solution.py:142
  197.8 8.0 %spread_body.1 = (bf16[1024,2048]{1,0:T(8,128)(2,1)S(1)}, bf16[1024,2048]{1,0:T(8,128)(2,1)S(1)}, f32[1,2048]{1,0:T(1,128)S(1)}, f32[8,128]{1,0:T(8,128)S(1)}) custom-call(s32[48]{0:T(128)S(1)} %copy-done.60, bf16[1024,2048]{1,0:T(8,128)(2,1)S(1)} %copy-done.15, bf16[1024,2048]{1,0:T(8,128)(2,1)S(1)} %copy-done.17, ...), custom_call_target="tpu_custom_call" | custom-call | flops 1000000 | bytes 1024 | tf_op jit(solution)/shard_map/spread_body/pallas_call | solution.py:142
  240.9 16.2 %collective-permute-done.10.refs_1_ = bf16[256,2048]{1,0:T(8,128)(2,1)S(1)} collective-permute-done((bf16[256,2048]{1,0:T(8,128)(2,1)S(1)}, bf16[256,2048]{1,0:T(8,128)(2,1)S(1)}, u32[]{:S(2)}, u32[]{:S(2)}) %collective-permute-start.10) | collective-permute-done | bytes 1048608 | tf_op jit(solution)/shard_map/ppermute | solution.py:36
  266.6 13.2 %down_body.1 = (bf16[256,2048]{1,0:T(8,128)(2,1)S(1)}, bf16[256,2048]{1,0:T(8,128)(2,1)S(1)}, f32[8,128]{1,0:T(8,128)S(1)}) custom-call(s32[48]{0:T(128)S(1)} %copy-done.60, bf16[1024,2048]{1,0:T(8,128)(2,1)S(1)} %get-tuple-element.316.refs_4_.refs_0_, bf16[2048,2048]{1,0:T(8,128)(2,1)S(1)} %bitcast.83, f32[8,128]{1,0:T(8,128)S(1)} %get-tuple-element.327.refs_2_), custom_call_target="tpu_custom_call" | custom-call | flops 1000000 | bytes 1024 | tf_op jit(solution)/shard_map/down_body/pallas_call | solution.py:142
  307.8 8.0 %weight_body.15 = (bf16[2,256,2048]{2,1,0:T(8,128)(2,1)S(1)}, bf16[2,256,2048]{2,1,0:T(8,128)(2,1)S(1)}, f32[8,128]{1,0:T(8,128)S(1)}) custom-call(s32[48]{0:T(128)S(1)} %copy-done.60, bf16[256,2048]{1,0:T(8,128)(2,1)S(1)} %copy-done.30, bf16[256,2048]{1,0:T(8,128)(2,1)S(1)} %copy-done.33, bf16[256,2048]{1,0:T(8,128)(2,1)S(1)} %copy-done.11, ...), custom_call_target="tpu_custom_call" | custom-call | flops 1000000 | bytes 1024 | tf_op jit(solution)/shard_map/weight_body/pallas_call | solution.py:142
  317.6 20.8 %attend_back_body.1 = (bf16[1024,1536]{1,0:T(8,128)(2,1)S(1)}, f32[8,128]{1,0:T(8,128)S(1)}) custom-call(s32[48]{0:T(128)S(1)} %copy-done.60, bf16[1024,1536]{1,0:T(8,128)(2,1)S(1)} %copy-done.3, bf16[1024,512]{1,0:T(8,128)(2,1)S(1)} %copy-done.13, bf16[1024,512]{1,0:T(8,128)(2,1)S(1)} %copy-done.49, f32[8,1024]{1,0:T(8,128)S(1)} %get-tuple-element.340.refs_3_, ...), custom_call_target="tpu_custom_call" | custom-call | flops 1000000 | bytes 1024 | tf_op jit(solution)/shard_map/attend_back_body/pallas_call | solution.py:142
  343.6 8.9 %body.34 = (bf16[4,16,2048]{2,1,0:T(8,128)(2,1)S(1)}, f32[8,128]{1,0:T(8,128)S(1)}) custom-call(s32[48]{0:T(128)S(1)} %copy-done.60, bf16[4,16,2048]{2,1,0:T(8,128)(2,1)S(1)} %get-tuple-element.520.refs_0_, f32[8,128]{1,0:T(8,128)S(1)} %get-tuple-element.354.refs_1_), custom_call_target="tpu_custom_call" | custom-call | flops 1000000 | bytes 1024 | tf_op jit(solution)/shard_map/body/pallas_call | solution.py:142
  354.4 13.7 %body.35 = (bf16[4,32,2048]{2,1,0:T(8,128)(2,1)S(1)}, f32[8,128]{1,0:T(8,128)S(1)}) custom-call(s32[48]{0:T(128)S(1)} %copy-done.60, bf16[4,32,2048]{2,1,0:T(8,128)(2,1)S(1)} %get-tuple-element.358.refs_0_, f32[8,128]{1,0:T(8,128)S(1)} %get-tuple-element.359.refs_1_), custom_call_target="tpu_custom_call" | custom-call | flops 1000000 | bytes 1024 | tf_op jit(solution)/shard_map/body/pallas_call | solution.py:142
  381.6 8.1 %weight_body.17 = (bf16[2,256,2048]{2,1,0:T(8,128)(2,1)S(1)}, bf16[2,256,2048]{2,1,0:T(8,128)(2,1)S(1)}, f32[8,128]{1,0:T(8,128)S(1)}) custom-call(s32[48]{0:T(128)S(1)} %copy-done.60, bf16[256,2048]{1,0:T(8,128)(2,1)S(1)} %copy-done.39, bf16[256,2048]{1,0:T(8,128)(2,1)S(1)} %copy-done.42, bf16[256,2048]{1,0:T(8,128)(2,1)S(1)} %copy-done.8, ...), custom_call_target="tpu_custom_call" | custom-call | flops 1000000 | bytes 1024 | tf_op jit(solution)/shard_map/weight_body/pallas_call | solution.py:142
  403.9 9.8 %body.37 = (bf16[1,32,2048]{2,1,0:T(8,128)(2,1)S(1)}, f32[8,128]{1,0:T(8,128)S(1)}) custom-call(s32[48]{0:T(128)S(1)} %copy-done.60, bf16[1,32,2048]{2,1,0:T(8,128)(2,1)S(1)} %get-tuple-element.377.refs_0_, f32[8,128]{1,0:T(8,128)S(1)} %get-tuple-element.378.refs_1_), custom_call_target="tpu_custom_call" | custom-call | flops 1000000 | bytes 1024 | tf_op jit(solution)/shard_map/body/pallas_call | solution.py:142
  418.6 30.4 %collective-permute-done.17.refs_1_ = bf16[2,256,512]{2,1,0:T(8,128)(2,1)S(1)} collective-permute-done((bf16[2,256,512]{2,1,0:T(8,128)(2,1)S(1)}, bf16[2,256,512]{2,1,0:T(8,128)(2,1)S(1)}, u32[]{:S(2)}, u32[]{:S(2)}) %collective-permute-start.17) | collective-permute-done | bytes 524320 | tf_op jit(solution)/shard_map/ppermute | solution.py:36
  459.0 8.6 %pool_back_body.1 = (bf16[512,1024]{1,0:T(8,128)(2,1)S(1)}, f32[64,512]{1,0:T(8,128)S(1)}, bf16[2,2,64,1024]{3,2,1,0:T(8,128)(2,1)S(1)}, bf16[2,2,64,1024]{3,2,1...) custom-call(s32[48]{0:T(128)S(1)} %copy-done.60, bf16[2,16,2048]{2,1,0:T(8,128)(2,1)S(1)} %bitcast.100, ...), custom_call_target="tpu_custom_call" | custom-call | flops 1000000 | bytes 1024 | tf_op jit(solution)/shard_map/pool_back_body/pallas_call | solution.py:142
  490.8 14.7 %collective-permute-done.21.refs_1_ = bf16[256,2048]{1,0:T(8,128)(2,1)S(1)} collective-permute-done((bf16[256,2048]{1,0:T(8,128)(2,1)S(1)}, bf16[256,2048]{1,0:T(8,128)(2,1)S(1)}, u32[]{:S(2)}, u32[]{:S(2)}) %collective-permute-start.21) | collective-permute-done | bytes 1048608 | tf_op jit(solution)/shard_map/ppermute | solution.py:36
  518.4 13.0 %body.41 = (bf16[2,64,1024]{2,1,0:T(8,128)(2,1)S(1)}, f32[8,128]{1,0:T(8,128)S(1)}) custom-call(s32[48]{0:T(128)S(1)} %copy-done.60, bf16[2,64,1024]{2,1,0:T(8,128)(2,1)S(1)} %slice_bitcast_fusion.1.refs_0_, f32[8,128]{1,0:T(8,128)S(1)} %get-tuple-element.428.refs_1_), custom_call_target="tpu_custom_call" | custom-call | flops 1000000 | bytes 1024 | tf_op jit(solution)/shard_map/body/pallas_call | solution.py:142
  532.6 19.5 %collective-permute-done.26.refs_2_ = bf16[4,512,512]{2,1,0:T(8,128)(2,1)S(1)} collective-permute-done((bf16[4,512,512]{2,1,0:T(8,128)(2,1)S(1)}, bf16[4,512,512]{2,1,0:T(8,128)(2,1)S(1)}, u32[]{:S(2)}, u32[]{:S(2)}) %collective-permute-start.26) | collective-permute-done | bytes 2097184 | tf_op jit(solution)/shard_map/ppermute | solution.py:36
  563.8 19.0 %collective-permute-done.24.refs_1_ = bf16[368,128]{1,0:T(8,128)(2,1)} collective-permute-done((bf16[368,128]{1,0:T(8,128)(2,1)S(1)}, bf16[368,128]{1,0:T(8,128)(2,1)}, u32[]{:S(2)}, u32[]{:S(2)}) %collective-permute-start.24) | collective-permute-done | bytes 94240 | tf_op jit(solution)/shard_map/ppermute | solution.py:36
  601.1 9.9 %body.42 = (bf16[368,128]{1,0:T(8,128)(2,1)S(1)}, bf16[368,128]{1,0:T(8,128)(2,1)S(1)}, f32[8,128]{1,0:T(8,128)S(1)}) custom-call(s32[48]{0:T(128)S(1)} %copy-done.60, bf16[368,128]{1,0:T(8,128)(2,1)S(1)} %get-tuple-element.450.refs_0_.refs_1_, bf16[368,128]{1,0:T(8,128)(2,1)S(1)} %get-tuple-element.450.refs_0_.refs_1_, f32[8,128]{1,0:T(8,128)S(1)} %get-tuple-element.451.refs_2_), custom_call_target="tpu_custom_call" | custom-call | flops 1000000 | bytes 1024 | tf_op jit(solution)/shard_map/body/pallas_call | solution.py:142
  629.3 16.6 %collective-permute-done.31 = bf16[1,512,512]{2,1,0:T(8,128)(2,1)S(1)} collective-permute-done((bf16[1,512,512]{2,1,0:T(8,128)(2,1)}, bf16[1,512,512]{2,1,0:T(8,128)(2,1)S(1)}, u32[]{:S(2)}, u32[]{:S(2)}) %collective-permute-start.31) | collective-permute-done | bytes 524320 | tf_op jit(solution)/shard_map/ppermute | solution.py:36
  (363 shorter events, 336.9 us)
Async XLA Ops:
  17.5 26.3 %collective-permute-start.4 = (bf16[256,2048]{1,0:T(8,128)(2,1)S(1)}, bf16[256,2048]{1,0:T(8,128)(2,1)S(1)}, u32[]{:S(2)}, u32[]{:S(2)}) collective-permute-start(bf16[256,2048]{1,0:T(8,128)(2,1)S(1)} %get-tuple-element.247.refs_0_), channel_id=1, source_target_pairs={{0,2},{1,3},{2,0},{3,1},{4,6},{5,7},{6,4},{7,5},{8,10},{9,11},{10,... | collective-permute-start | bytes 3145736 | tf_op jit(solution)/shard_map/ppermute | solution.py:36
  78.9 47.8 %collective-permute-start.6 = (bf16[256,2048]{1,0:T(8,128)(2,1)S(1)}, bf16[256,2048]{1,0:T(8,128)(2,1)S(1)}, u32[]{:S(2)}, u32[]{:S(2)}) collective-permute-start(bf16[256,2048]{1,0:T(8,128)(2,1)S(1)} %get-tuple-element.289.refs_0_), channel_id=1, source_target_pairs={{0,2},{1,3},{2,0},{3,1},{4,6},{5,7},{6,4},{7,5},{8,10},{9,11},{10,... | collective-permute-start | bytes 3145736 | tf_op jit(solution)/shard_map/ppermute | solution.py:36
  79.5 41.2 %collective-permute-start.7 = (bf16[256,2048]{1,0:T(8,128)(2,1)S(1)}, bf16[256,2048]{1,0:T(8,128)(2,1)S(1)}, u32[]{:S(2)}, u32[]{:S(2)}) collective-permute-start(bf16[256,2048]{1,0:T(8,128)(2,1)S(1)} %get-tuple-element.289.refs_0_), channel_id=1, source_target_pairs={{0,1},{1,0},{2,3},{3,2},{4,5},{5,4},{6,7},{7,6},{8,9},{9,8},{10,11... | collective-permute-start | bytes 3145736 | tf_op jit(solution)/shard_map/ppermute | solution.py:36
  114.7 25.3 %collective-permute-start.5 = (bf16[256,2048]{1,0:T(8,128)(2,1)S(1)}, bf16[256,2048]{1,0:T(8,128)(2,1)S(1)}, u32[]{:S(2)}, u32[]{:S(2)}) collective-permute-start(bf16[256,2048]{1,0:T(8,128)(2,1)S(1)} %get-tuple-element.287), channel_id=1, source_target_pairs={{0,2},{1,3},{2,0},{3,1},{4,6},{5,7},{6,4},{7,5},{8,10},{9,11},{10,... | collective-permute-start | bytes 3145736 | tf_op jit(solution)/shard_map/ppermute | solution.py:36
  143.2 25.6 %collective-permute-start.8 = (bf16[256,2048]{1,0:T(8,128)(2,1)S(1)}, bf16[256,2048]{1,0:T(8,128)(2,1)S(1)}, u32[]{:S(2)}, u32[]{:S(2)}) collective-permute-start(bf16[256,2048]{1,0:T(8,128)(2,1)S(1)} %get-tuple-element.296.refs_0_), channel_id=1, source_target_pairs={{0,2},{1,3},{2,0},{3,1},{4,6},{5,7},{6,4},{7,5},{8,10},{9,11},{10,... | collective-permute-start | bytes 3145736 | tf_op jit(solution)/shard_map/ppermute | solution.py:36
  214.2 93.5 %collective-permute-start.14 = (bf16[4,256,2048]{2,1,0:T(8,128)(2,1)}, bf16[4,256,2048]{2,1,0:T(8,128)(2,1)}, u32[]{:S(2)}, u32[]{:S(2)}) collective-permute-start(bf16[4,256,2048]{2,1,0:T(8,128)(2,1)} %get-tuple-element.344), channel_id=1, source_target_pairs={{0,4},{4,0},{8,12},{12,8},{16,20},{20,16},{24,28},{28,24},{1,5},{5... | collective-permute-start | bytes 12582920 | tf_op jit(solution)/shard_map/ppermute | solution.py:36
  222.9 158.7 %collective-permute-start.15 = (bf16[4,256,2048]{2,1,0:T(8,128)(2,1)}, bf16[4,256,2048]{2,1,0:T(8,128)(2,1)}, u32[]{:S(2)}, u32[]{:S(2)}) collective-permute-start(bf16[4,256,2048]{2,1,0:T(8,128)(2,1)} %get-tuple-element.369), channel_id=1, source_target_pairs={{0,8},{4,12},{8,0},{12,4},{16,24},{20,28},{24,16},{28,20},{1,9},{5... | collective-permute-start | bytes 12582920 | tf_op jit(solution)/shard_map/ppermute | solution.py:36
  231.9 25.3 %collective-permute-start.10 = (bf16[256,2048]{1,0:T(8,128)(2,1)S(1)}, bf16[256,2048]{1,0:T(8,128)(2,1)S(1)}, u32[]{:S(2)}, u32[]{:S(2)}) collective-permute-start(bf16[256,2048]{1,0:T(8,128)(2,1)S(1)} %get-tuple-element.323), channel_id=1, source_target_pairs={{0,2},{1,3},{2,0},{3,1},{4,6},{5,7},{6,4},{7,5},{8,10},{9,11},{10,... | collective-permute-start | bytes 3145736 | tf_op jit(solution)/shard_map/ppermute | solution.py:36
  261.0 25.6 %collective-permute-start.12 = (bf16[256,2048]{1,0:T(8,128)(2,1)S(1)}, bf16[256,2048]{1,0:T(8,128)(2,1)S(1)}, u32[]{:S(2)}, u32[]{:S(2)}) collective-permute-start(bf16[256,2048]{1,0:T(8,128)(2,1)S(1)} %get-tuple-element.325.refs_0_.refs_5_), channel_id=1, source_target_pairs={{0,2},{1,3},{2,0},{3,1},{4,6},{5,7},{6,4},{7,5},{8,10},{9,11},{10,... | collective-permute-start | bytes 3145736 | tf_op jit(solution)/shard_map/ppermute | solution.py:36
  299.0 77.0 %collective-permute-start.13 = (bf16[256,2048]{1,0:T(8,128)(2,1)S(1)}, bf16[256,2048]{1,0:T(8,128)(2,1)S(1)}, u32[]{:S(2)}, u32[]{:S(2)}) collective-permute-start(bf16[256,2048]{1,0:T(8,128)(2,1)S(1)} %get-tuple-element.338), channel_id=1, source_target_pairs={{0,2},{1,3},{2,0},{3,1},{4,6},{5,7},{6,4},{7,5},{8,10},{9,11},{10,... | collective-permute-start | bytes 3145736 | tf_op jit(solution)/shard_map/ppermute | solution.py:36
  303.4 75.1 %collective-permute-start.16 = (bf16[4,256,512]{2,1,0:T(8,128)(2,1)S(1)}, bf16[4,256,512]{2,1,0:T(8,128)(2,1)S(1)}, u32[]{:S(2)}, u32[]{:S(2)}) collective-permute-start(bf16[4,256,512]{2,1,0:T(8,128)(2,1)S(1)} %get-tuple-element.370), channel_id=1, source_target_pairs={{0,4},{4,0},{8,12},{12,8},{16,20},{20,16},{24,28},{28,24},{1,5},{5... | collective-permute-start | bytes 3145736 | tf_op jit(solution)/shard_map/ppermute | solution.py:36
  315.8 97.9 %collective-permute-start.18 = (bf16[2,256,2048]{2,1,0:T(8,128)(2,1)S(1)}, bf16[2,256,2048]{2,1,0:T(8,128)(2,1)S(1)}, u32[]{:S(2)}, u32[]{:S(2)}) collective-permute-start(bf16[2,256,2048]{2,1,0:T(8,128)(2,1)S(1)} %get-tuple-element.383), channel_id=1, source_target_pairs={{0,8},{4,12},{8,0},{12,4},{16,24},{20,28},{24,16},{28,20},{1,9},{5... | collective-permute-start | bytes 6291464 | tf_op jit(solution)/shard_map/ppermute | solution.py:36
  394.7 75.0 %collective-permute-start.19 = (bf16[4,256,1536]{2,1,0:T(8,128)(2,1)S(1)}, bf16[4,256,1536]{2,1,0:T(8,128)(2,1)S(1)}, u32[]{:S(2)}, u32[]{:S(2)}) collective-permute-start(bf16[4,256,1536]{2,1,0:T(8,128)(2,1)S(1)} %get-tuple-element.398), channel_id=1, source_target_pairs={{0,4},{4,0},{8,12},{12,8},{16,20},{20,16},{24,28},{28,24},{1,5},{5... | collective-permute-start | bytes 9437192 | tf_op jit(solution)/shard_map/ppermute | solution.py:36
  414.8 52.9 %collective-permute-start.20 = (bf16[1,256,2048]{2,1,0:T(8,128)(2,1)S(1)}, bf16[1,256,2048]{2,1,0:T(8,128)(2,1)S(1)}, u32[]{:S(2)}, u32[]{:S(2)}) collective-permute-start(bf16[1,256,2048]{2,1,0:T(8,128)(2,1)S(1)} %get-tuple-element.400), channel_id=1, source_target_pairs={{0,16},{4,20},{8,24},{12,28},{16,0},{20,4},{24,8},{28,12},{1,17},{... | collective-permute-start | bytes 3145736 | tf_op jit(solution)/shard_map/ppermute | solution.py:36
  414.8 34.1 %collective-permute-start.17 = (bf16[2,256,512]{2,1,0:T(8,128)(2,1)S(1)}, bf16[2,256,512]{2,1,0:T(8,128)(2,1)S(1)}, u32[]{:S(2)}, u32[]{:S(2)}) collective-permute-start(bf16[2,256,512]{2,1,0:T(8,128)(2,1)S(1)} %get-tuple-element.381), channel_id=1, source_target_pairs={{0,8},{4,12},{8,0},{12,4},{16,24},{20,28},{24,16},{28,20},{1,9},{5... | collective-permute-start | bytes 1572872 | tf_op jit(solution)/shard_map/ppermute | solution.py:36
  418.0 95.3 %collective-permute-start.22 = (bf16[2,256,2048]{2,1,0:T(8,128)(2,1)}, bf16[2,256,2048]{2,1,0:T(8,128)(2,1)S(1)}, u32[]{:S(2)}, u32[]{:S(2)}) collective-permute-start(bf16[2,256,2048]{2,1,0:T(8,128)(2,1)} %copy-done.80), channel_id=1, source_target_pairs={{0,4},{4,0},{8,12},{12,8},{16,20},{20,16},{24,28},{28,24},{1,5},{5... | collective-permute-start | bytes 6291464 | tf_op jit(solution)/shard_map/ppermute | solution.py:36
  479.9 72.1 %collective-permute-start.26 = (bf16[4,512,512]{2,1,0:T(8,128)(2,1)S(1)}, bf16[4,512,512]{2,1,0:T(8,128)(2,1)S(1)}, u32[]{:S(2)}, u32[]{:S(2)}) collective-permute-start(bf16[4,512,512]{2,1,0:T(8,128)(2,1)S(1)} %get-tuple-element.435), channel_id=1, source_target_pairs={{0,4},{4,0},{8,12},{12,8},{16,20},{20,16},{24,28},{28,24},{1,5},{5... | collective-permute-start | bytes 6291464 | tf_op jit(solution)/shard_map/ppermute | solution.py:36
  480.5 24.9 %collective-permute-start.21 = (bf16[256,2048]{1,0:T(8,128)(2,1)S(1)}, bf16[256,2048]{1,0:T(8,128)(2,1)S(1)}, u32[]{:S(2)}, u32[]{:S(2)}) collective-permute-start(bf16[256,2048]{1,0:T(8,128)(2,1)S(1)} %get-tuple-element.408), channel_id=1, source_target_pairs={{0,2},{1,3},{2,0},{3,1},{4,6},{5,7},{6,4},{7,5},{8,10},{9,11},{10,... | collective-permute-start | bytes 3145736 | tf_op jit(solution)/shard_map/ppermute | solution.py:36
  481.4 80.1 %collective-permute-start.25 = (bf16[2,256,1536]{2,1,0:T(8,128)(2,1)}, bf16[2,256,1536]{2,1,0:T(8,128)(2,1)}, u32[]{:S(2)}, u32[]{:S(2)}) collective-permute-start(bf16[2,256,1536]{2,1,0:T(8,128)(2,1)} %get-tuple-element.434), channel_id=1, source_target_pairs={{0,8},{4,12},{8,0},{12,4},{16,24},{20,28},{24,16},{28,20},{1,9},{5... | collective-permute-start | bytes 4718600 | tf_op jit(solution)/shard_map/ppermute | solution.py:36
  517.9 76.3 %collective-permute-start.29 = (bf16[1,256,2048]{2,1,0:T(8,128)(2,1)}, bf16[1,256,2048]{2,1,0:T(8,128)(2,1)}, u32[]{:S(2)}, u32[]{:S(2)}) collective-permute-start(bf16[1,256,2048]{2,1,0:T(8,128)(2,1)} %get-tuple-element.446), channel_id=1, source_target_pairs={{0,16},{4,20},{8,24},{12,28},{16,0},{20,4},{24,8},{28,12},{1,17},{... | collective-permute-start | bytes 3145736 | tf_op jit(solution)/shard_map/ppermute | solution.py:36
  558.2 39.6 %collective-permute-start.28 = (bf16[2,512,512]{2,1,0:T(8,128)(2,1)}, bf16[2,512,512]{2,1,0:T(8,128)(2,1)}, u32[]{:S(2)}, u32[]{:S(2)}) collective-permute-start(bf16[2,512,512]{2,1,0:T(8,128)(2,1)} %get-tuple-element.444), channel_id=1, source_target_pairs={{0,8},{4,12},{8,0},{12,4},{16,24},{20,28},{24,16},{28,20},{1,9},{5... | collective-permute-start | bytes 3145736 | tf_op jit(solution)/shard_map/ppermute | solution.py:36
  561.4 61.0 %collective-permute-start.32 = (bf16[1,256,512]{2,1,0:T(8,128)(2,1)}, bf16[1,256,512]{2,1,0:T(8,128)(2,1)}, u32[]{:S(2)}, u32[]{:S(2)}) collective-permute-start(bf16[1,256,512]{2,1,0:T(8,128)(2,1)} %get-tuple-element.461), channel_id=1, source_target_pairs={{0,16},{4,20},{8,24},{12,28},{16,0},{20,4},{24,8},{28,12},{1,17},{... | collective-permute-start | bytes 786440 | tf_op jit(solution)/shard_map/ppermute | solution.py:36
  590.6 57.6 %collective-permute-start.30 = (bf16[1,256,1536]{2,1,0:T(8,128)(2,1)}, bf16[1,256,1536]{2,1,0:T(8,128)(2,1)}, u32[]{:S(2)}, u32[]{:S(2)}) collective-permute-start(bf16[1,256,1536]{2,1,0:T(8,128)(2,1)} %copy-done.81), channel_id=1, source_target_pairs={{0,16},{4,20},{8,24},{12,28},{16,0},{20,4},{24,8},{28,12},{1,17},{... | collective-permute-start | bytes 2359304 | tf_op jit(solution)/shard_map/ppermute | solution.py:36
  619.0 26.9 %collective-permute-start.31 = (bf16[1,512,512]{2,1,0:T(8,128)(2,1)}, bf16[1,512,512]{2,1,0:T(8,128)(2,1)S(1)}, u32[]{:S(2)}, u32[]{:S(2)}) collective-permute-start(bf16[1,512,512]{2,1,0:T(8,128)(2,1)} %get-tuple-element.459), channel_id=1, source_target_pairs={{0,16},{4,20},{8,24},{12,28},{16,0},{20,4},{24,8},{28,12},{1,17},{... | collective-permute-start | bytes 1572872 | tf_op jit(solution)/shard_map/ppermute | solution.py:36
  (103 other events, 1631.4 us)
